TPU v7x, 128 devices: a whole 4x4x4 slice. The times are simulated.
128 devices in a mesh: group: 4 (over z), dev: 32 (over x, y, core).
Axes of the slice: x: 4, y: 4, z: 4, core: 2. Of those that a mesh axis runs over, the one named last changes fastest.
Arguments:
- embeddings: bfloat16 [128, 128, 1280], P(('group', 'dev')), may hold values from -8 to 8
- weight_q: bfloat16 [1280, 1280], replicated, may hold values from -0.15625 to 0.15625
- weight_k: bfloat16 [1280, 1280], replicated, may hold values from -0.15625 to 0.15625
- weight_v: bfloat16 [1280, 1280], replicated, may hold values from -0.15625 to 0.15625
- weight_o: bfloat16 [1280, 1280], replicated, may hold values from -0.15625 to 0.15625
- pairs: int32 [256, 2], replicated, may hold values from 0 to 127, as said below
- lengths: int32 [128], replicated, may hold values from 1 to 128, as said below
- holder: int32 [128], replicated, may hold values from 0 to 127, each once
Outputs:
- updated: bfloat16 [128, 128, 1280], P(('group', 'dev'))
Inputs may be any that keep to these rules, and one draw needn't show every extreme that they name: `pairs`: the two proteins of a pair differ. `lengths`: some protein has exactly 128 residues.
All inputs are finite; a program needn't handle non-finite values.
Results may differ from a plain program's by a relative error of at most 0.02.
Values may be sent and summed in bfloat16 or wider, within the bound.
No kernel may reach another device: no remote copies, remote signals or barrier semaphores. Data moves between devices by JAX's collectives and lax.ppermute only.
A program may use at most 128 MiB of HBM per device.

v0:
```python
import jax
import jax.numpy as jnp
from jax import lax
from jax.sharding import PartitionSpec as P

HEADS = 20
HEAD_DIM = 64
PAIR_DEV = 2


def local(embeddings, weight_q, weight_k, weight_v, weight_o, pairs, lengths, holder):
    group_count = lax.axis_size("group")
    dev_count = lax.axis_size("dev")
    my_group = lax.axis_index("group")
    my_dev = lax.axis_index("dev")
    slots = 2 * PAIR_DEV
    residues = embeddings.shape[1]
    model_width = embeddings.shape[2]
    owners = jnp.arange(group_count, dtype=jnp.int32) * dev_count + my_dev
    pair_rows = owners[:, None] * PAIR_DEV + (jnp.arange(slots, dtype=jnp.int32) // 2)[None, :]
    member_side = jnp.arange(slots, dtype=jnp.int32) % 2
    wanted = pairs[pair_rows, member_side[None, :]]
    location = holder[wanted]
    place_group = location // dev_count
    place_dev = location % dev_count
    in_group = place_group == my_group
    whole_group = lax.all_gather(embeddings, "dev", axis=0, tiled=True)
    amount = whole_group.shape[0]
    positions = jnp.arange(amount, dtype=jnp.int32)
    selector = (in_group[:, :, None] & (place_dev[:, :, None] == positions[None, None, :])).astype(
        jnp.bfloat16
    )
    pick_flattened = whole_group.reshape(amount, residues * model_width)
    picked = jnp.einsum("tsj,jf->tsf", selector, pick_flattened, preferred_element_type=jnp.float32)
    selected = picked.astype(jnp.bfloat16)
    arrived = lax.all_to_all(selected, "group", split_axis=0, concat_axis=0, tiled=True)
    fetched = jnp.sum(arrived.astype(jnp.float32), axis=0).astype(jnp.bfloat16)
    flattened = fetched.reshape(slots * residues, model_width)

    def project(weight):
        result = jnp.dot(flattened, weight, preferred_element_type=jnp.float32).astype(jnp.bfloat16)
        return result.reshape(slots, residues, HEADS, HEAD_DIM)

    def partner_of(array):
        return jnp.flip(array.reshape((PAIR_DEV, 2) + array.shape[1:]), axis=1).reshape(array.shape)

    query_rows = project(weight_q)
    key_rows = partner_of(project(weight_k))
    value_rows = partner_of(project(weight_v))
    own_ids = wanted[my_group]
    other_ids = partner_of(own_ids)
    own_len = lengths[own_ids]
    other_len = lengths[other_ids]
    scores = jnp.einsum("sihd,sjhd->shij", query_rows, key_rows, preferred_element_type=jnp.float32)
    scores = scores * HEAD_DIM ** (-0.5)
    positions = jnp.arange(residues, dtype=jnp.int32)
    key_live = positions[None, :] < other_len[:, None]
    scores = jnp.where(key_live[:, None, None, :], scores, -1e30)
    row_max = jnp.max(scores, axis=-1, keepdims=True)
    exponent = jnp.exp(scores - row_max)
    attention = (exponent / jnp.sum(exponent, axis=-1, keepdims=True)).astype(jnp.bfloat16)
    context = jnp.einsum(
        "shij,sjhd->sihd", attention, value_rows, preferred_element_type=jnp.float32
    )
    context = context.astype(jnp.bfloat16).reshape(slots, residues, model_width)
    query_live = positions[None, :] < own_len[:, None]
    my_place_group = place_group[my_group]
    target = jnp.arange(group_count, dtype=jnp.int32)[:, None] == my_place_group[None, :]
    updates = jnp.dot(
        context.reshape(slots * residues, model_width), weight_o, preferred_element_type=jnp.float32
    ).reshape(slots, residues, model_width)
    updates = jnp.where(query_live[:, :, None], updates, 0.0)
    outgoing = jnp.where(
        target[:, :, None], updates.reshape(slots, residues * model_width)[None, :, :], 0.0
    )
    returned = lax.all_to_all(
        outgoing.astype(jnp.bfloat16), "group", split_axis=0, concat_axis=0, tiled=True
    ).astype(outgoing.dtype)
    indices = jnp.arange(dev_count, dtype=jnp.int32)
    selector = (in_group[:, :, None] & (place_dev[:, :, None] == indices[None, None, :])).astype(
        jnp.float32
    )
    summed = jnp.einsum(
        "tsj,tsf->jf",
        selector,
        returned,
        precision=lax.Precision.HIGHEST,
        preferred_element_type=jnp.float32,
    )
    totals = lax.psum_scatter(
        summed.reshape(dev_count, residues, model_width).astype(jnp.bfloat16),
        "dev",
        scatter_dimension=0,
        tiled=True,
    ).astype(jnp.float32)
    return (embeddings.astype(jnp.float32) + totals).astype(jnp.bfloat16)


def solution(mesh):
    in_specs = (P(("group", "dev"), None, None), P(), P(), P(), P(), P(), P(), P())
    out_specs = P(("group", "dev"), None, None)
    return jax.shard_map(local, mesh=mesh, in_specs=in_specs, out_specs=out_specs, check_vma=False)
```

profile of v0, /device:TPU:1, one launch (start us, length us, event | category | flops | bytes accessed | tf_op | source)
XLA Modules:
  0.0 401.1 jit_solution(12334771419042570568)
XLA Ops:
  6.5 0.7 all-gather.2.cloned.1.call-update
  7.3 0.1 fusion.21
  7.4 0.1 reshape.270
  7.5 1.4 gather_fusion
  8.9 0.1 gather.15
  9.0 0.1 reshape.278
  9.1 0.7 gather_fusion.1
  9.8 0.1 reshape.277
  9.9 0.1 copy.29
  10.0 0.1 copy.28
  10.1 0.1 fusion.17
  10.2 60.8 %all-gather.2.cloned.1.call-done = bf16[32,128,1280]{2,1,0:T(8,128)(2,1)} async-done(((bf16[1,128,1280]{2,1,0:T(8,128)(2,1)}), bf16[32,128,1280]{2,1,0:T(8,128)(2,1)}) %all-gather.2.cloned.1.call-update) | async-done | bytes 10485776 | tf_op jit(solution)/shard_map/all_gather | solution.py:27
  71.0 10.5 %reshape.302 = bf16[32,163840,1]{1,0,2:T(8,128)(2,1)} reshape(bf16[32,128,1280]{2,1,0:T(8,128)(2,1)} %all-gather.2.cloned.1.call-done) | data formatting | bytes 20971520 | tf_op jit(solution)/shard_map/reshape | solution.py:33
  81.5 8.9 %convolution_convert_fusion = bf16[4,4,163840]{2,1,0:T(4,128)(2,1)} fusion(bf16[32,163840,1]{1,0,2:T(8,128)(2,1)} %reshape.302, pred[4,4,32]{2,0,1:T(4,128)(4,1)S(1)} %fusion.17), kind=kOutput, calls=%fused_computation.7 | convolution fusion | flops 170393600 | bytes 15729152 | tf_op jit(solution)/shard_map/tsj,jf->tsf/dot_general | solution.py:34
  90.4 5.2 %all-to-all-start = ((bf16[4,4,163840]{2,1,0:T(4,128)(2,1)}), bf16[4,4,163840]{2,1,0:T(4,128)(2,1)}, u32[]{:S(2)}, u32[]{:S(2)}) async-start(bf16[4,4,163840]{2,1,0:T(4,128)(2,1)} %convolution_convert_fusion), calls=%async_computation | async-start | bytes 10485760 | tf_op jit(solution)/shard_map/all_to_all | solution.py:36
  95.6 0.2 reduce-scatter.2.cloned.1.call-start
  95.8 0.1 reshape.273
  95.9 0.1 reshape_squeeze.3
  96.0 0.1 rev.12
  96.1 0.1 reshape.267
  96.2 0.6 gather_fusion.3
  96.9 0.6 gather_fusion.2
  97.7 57.9 %all-to-all-done = bf16[4,4,163840]{2,1,0:T(4,128)(2,1)} async-done(((bf16[4,4,163840]{2,1,0:T(4,128)(2,1)}), bf16[4,4,163840]{2,1,0:T(4,128)(2,1)}, u32[]{:S(2)}, u32[]{:S(2)}) %all-to-all-start) | async-done | bytes 5242912 | tf_op jit(solution)/shard_map/all_to_all | solution.py:36
  155.6 7.0 %reduce_sum.21 = bf16[4,163840]{1,0:T(4,128)(2,1)} reduce(bf16[4,4,163840]{2,1,0:T(4,128)(2,1)} %all-to-all-done, bf16[]{:T(256)} %constant.82.clone.1), dimensions={0}, to_apply=%region_0.1 | reduce | flops 1966080 | bytes 6553602 | tf_op jit(solution)/shard_map/reduce_sum | solution.py:37
  162.6 3.6 reshape.265
  166.1 4.2 %convolution_convert_fusion.1 = bf16[512,1280]{1,0:T(8,128)(2,1)} fusion(bf16[512,1280]{1,0:T(8,128)(2,1)} %reshape.265, bf16[1280,1280]{1,0:T(8,128)(2,1)S(1)} %copy-done), kind=kOutput, calls=%fused_computation.17 | convolution fusion | flops 1678376960 | bytes 5898240 | tf_op jit(solution)/shard_map/dot_general | solution.py:41
  170.4 1.6 copy.33
  172.0 0.3 reshape_reshape.8
  172.4 10.4 %rev.13 = bf16[2,2,128,20,64]{2,1,0,4,3:T(2,128)(2,1)} reverse(bf16[2,2,128,20,64]{2,1,0,4,3:T(2,128)(2,1)S(1)} %reshape_reshape.8), dimensions={1} | reverse | bytes 2621440 | tf_op jit(solution)/shard_map/jit(_flip)/rev | solution.py:45
  182.8 5.4 %convolution_convert_fusion.2 = bf16[512,1280]{1,0:T(8,128)(2,1)} fusion(bf16[512,1280]{1,0:T(8,128)(2,1)} %reshape.265, bf16[1280,1280]{1,0:T(8,128)(2,1)} %param.9), kind=kOutput, calls=%fused_computation.18 | convolution fusion | flops 1678376960 | bytes 5898240 | tf_op jit(solution)/shard_map/dot_general | solution.py:41
  188.2 1.9 convolution_convert_fusion.3
  190.0 0.7 copy.31
  190.7 0.3 reshape_reshape.7
  191.1 10.4 %rev.11 = bf16[2,2,128,20,64]{2,1,0,4,3:T(2,128)(2,1)} reverse(bf16[2,2,128,20,64]{2,1,0,4,3:T(2,128)(2,1)S(1)} %reshape_reshape.7), dimensions={1} | reverse | bytes 2621440 | tf_op jit(solution)/shard_map/jit(_flip)/rev | solution.py:45
  201.4 1.7 copy.32
  203.2 1.2 reshape.268
  204.4 2.2 fusion.14
  206.6 2.4 fusion.30
  209.1 0.9 fusion.12
  210.0 1.0 copy-done.8
  211.0 1.9 fusion.5
  212.9 1.0 copy.42
  213.9 2.0 select_convert_fusion
  215.9 61.6 %all_to_all.10 = bf16[4,4,163840]{2,1,0:T(4,128)(2,1)S(1)} all-to-all(bf16[4,4,163840]{2,1,0:T(4,128)(2,1)S(1)} %select_convert_fusion), channel_id=1, replica_groups=mesh['group'=4,'dev'=32] {'group'}, dimensions={0} | all-to-all | bytes 10485760 | tf_op jit(solution)/shard_map/all_to_all | solution.py:76
  277.5 8.6 %fusion.1 = bf16[32,163840]{1,0:T(8,128)(2,1)} fusion(pred[4,4,32]{2,0,1:T(4,128)(4,1)S(1)} %fusion.17, bf16[4,4,163840]{2,1,0:T(4,128)(2,1)S(1)} %all_to_all.10), kind=kOutput, calls=%fused_computation.6 | convolution fusion | flops 173015040 | bytes 15729152 | tf_op jit(solution)/shard_map/tsj,tsf->jf/dot_general | solution.py:83
  286.1 10.4 %copy.43 = bf16[4,8,128,1280]{3,2,1,0:T(8,128)(2,1)} copy(bf16[4,8,128,1280]{3,1,2,0:T(8,128)(2,1)} %bitcast.47) | data formatting | bytes 20971520
  296.5 95.9 %reduce-scatter.2.cloned.1.call-done = bf16[1,128,1280]{2,1,0:T(8,128)(2,1)} async-done(((bf16[32,128,1280]{2,1,0:T(8,128)(2,1)}), bf16[1,128,1280]{2,1,0:T(8,128)(2,1)}) %reduce-scatter.2.cloned.1.call-update) | async-done | bytes 327696 | tf_op jit(solution)/shard_map/reduce_scatter | solution.py:90
  392.4 1.9 add_convert_fusion
  (34 shorter events, 0.3 us)
Async XLA Ops:
  6.5 159.6 %copy-start = (bf16[1280,1280]{1,0:T(8,128)(2,1)S(1)}, bf16[1280,1280]{1,0:T(8,128)(2,1)}, u32[]{:S(2)}) copy-start(bf16[1280,1280]{1,0:T(8,128)(2,1)} %param.10) | copy-start | bytes 9830404
  6.5 2.6 copy-start.2
  6.5 64.5 %all-gather.2.cloned.1.call-start = ((), (), s32[]{:S(2)}) async-start(), calls=%async_computation.3 | async-start | bytes 10813440 | tf_op jit(solution)/shard_map/all_gather | solution.py:27
  90.4 5.8 %copy-start.3 = (s32[128]{0:T(128)S(1)}, s32[128]{0:T(128)}, u32[]{:S(2)}) copy-start(s32[128]{0:T(128)} %param.14) | copy-start | bytes 1540
  90.4 65.2 %all-to-all-start = ((bf16[4,4,163840]{2,1,0:T(4,128)(2,1)}), bf16[4,4,163840]{2,1,0:T(4,128)(2,1)}, u32[]{:S(2)}, u32[]{:S(2)}) async-start(bf16[4,4,163840]{2,1,0:T(4,128)(2,1)} %convolution_convert_fusion), calls=%async_computation | async-start | bytes 10485760 | tf_op jit(solution)/shard_map/all_to_all | solution.py:36
  95.6 296.8 %reduce-scatter.2.cloned.1.call-start = ((), (), s32[]{:S(2)}) async-start(), calls=%async_computation.4 | async-start | bytes 10813440 | tf_op jit(solution)/shard_map/reduce_scatter | solution.py:90
  182.8 5.4 %copy-start.6 = (bf16[512,1280]{1,0:T(8,128)(2,1)S(1)}, bf16[512,1280]{1,0:T(8,128)(2,1)}, u32[]{:S(2)}) copy-start(bf16[512,1280]{1,0:T(8,128)(2,1)} %reshape.265) | copy-start | bytes 3932164
  182.8 5.4 %copy-start.7 = (bf16[1280,1280]{1,0:T(8,128)(2,1)S(1)}, bf16[1280,1280]{1,0:T(8,128)(2,1)}, u32[]{:S(2)}) copy-start(bf16[1280,1280]{1,0:T(8,128)(2,1)} %param.11) | copy-start | bytes 9830404
  201.4 2.9 copy-start.4
  206.6 2.4 copy-start.5
  209.1 1.9 copy-start.8
  296.5 97.8 %copy-start.1 = (bf16[1280,1280]{1,0:T(8,128)(2,1)S(1)}, bf16[1280,1280]{1,0:T(8,128)(2,1)}, u32[]{:S(2)}) copy-start(bf16[1280,1280]{1,0:T(8,128)(2,1)} %param.10) | copy-start | bytes 9830404
Sparse Core Ops, SparseCore 0:
  9.6 61.3 all-gather.1
  296.6 95.7 reduce-scatter.1
where the time goes:
time: 402 us; the launch traced here: 401 us
  waiting for transfers between devices  215 us (53%)
  blocking collectives  61.6 us (15%)
  local copies, waits for them, and re-layouts  57.5 us (14%)
  matrix products  34 us (8%)
  other arithmetic  13.6 us (3%)
  between operations  13.6 us (3%)
  starting transfers between devices  5.4 us (1%)
    reduce_scatter x1, waiting for transfers between devices, local(): lax.psum_scatter(summed.reshape(dev_count, residues, model_width).astype(...  95.9 us
    all_to_all x1, blocking collectives, local(): lax.all_to_all(outgoing.astype(jnp.bfloat16), 'group', split_axis=0, conc...  61.6 us
    all_gather x1, waiting for transfers between devices, local(): whole_group = lax.all_gather(embeddings, 'dev', axis=0, tiled=True)  60.8 us
    all_to_all x1, waiting for transfers between devices, local(): lax.all_to_all(selected, 'group', split_axis=0, concat_axis=0, tiled=True)  57.9 us
    rev x3, local copies, waits for them, and re-layouts, partner_of(): jnp.flip(array.reshape((PAIR_DEV, 2) + array.shape[1:]), axis=1)  20.9 us
    unnamed x20, local copies, waits for them, and re-layouts  12.4 us
    dot_general x3, matrix products, project(): jnp.dot(flattened, weight, preferred_element_type=jnp.float32)  11.5 us
    reshape x1, local copies, waits for them, and re-layouts, local(): pick_flattened = whole_group.reshape(amount, residues * model_width)  10.5 us
  transfers between devices with their start and end apart: 3, of which 3 were waited for; matrix products, arithmetic and copies ran while one was open for 1% of the time, Pallas kernels for 0%

commit v1 on v0

v1 whole, which is shorter than its diff:
```python
import jax
import jax.numpy as jnp
from jax import lax
from jax.sharding import PartitionSpec as P

HEADS = 20
HEAD_DIM = 64
SLOTS = 4
AXES = ("group", "dev")


def exchange(array):
    return lax.all_to_all(array, AXES, split_axis=0, concat_axis=0, tiled=True)


def attend(query, key, value, other_len):
    rows, width = query.shape
    query = query.reshape(rows, HEADS, HEAD_DIM)
    key = key.reshape(rows, HEADS, HEAD_DIM)
    value = value.reshape(rows, HEADS, HEAD_DIM)
    scores = jnp.einsum("ihd,jhd->hij", query, key, preferred_element_type=jnp.float32)
    scores = scores * HEAD_DIM ** (-0.5)
    live = jnp.arange(rows, dtype=jnp.int32) < other_len
    scores = jnp.where(live[None, None, :], scores, -1e30)
    exponent = jnp.exp(scores - jnp.max(scores, axis=-1, keepdims=True))
    weights = (exponent / jnp.sum(exponent, axis=-1, keepdims=True)).astype(jnp.bfloat16)
    context = jnp.einsum("hij,jhd->ihd", weights, value, preferred_element_type=jnp.float32)
    return context.astype(jnp.bfloat16).reshape(rows, width)


def local(embeddings, weight_q, weight_k, weight_v, weight_o, pairs, lengths, holder):
    residues, width = embeddings.shape[1:]
    count = lax.axis_size("group") * lax.axis_size("dev")
    me = lax.axis_index("group") * lax.axis_size("dev") + lax.axis_index("dev")
    places = holder[pairs.reshape(-1)]
    selector = (places[:, None] == jnp.arange(count, dtype=jnp.int32)[None, :]).astype(jnp.bfloat16)
    mine = exchange(embeddings.reshape(residues, 1, width)).reshape(count, width)
    picked = jnp.dot(selector, mine, preferred_element_type=jnp.float32).astype(jnp.bfloat16)
    arrived = exchange(picked.reshape(count, SLOTS, width))
    features = jnp.swapaxes(arrived, 0, 1).reshape(SLOTS * residues, width)

    def project(weight):
        result = jnp.dot(features, weight, preferred_element_type=jnp.float32)
        return result.astype(jnp.bfloat16).reshape(SLOTS, residues, width)

    query, key, value = project(weight_q), project(weight_k), project(weight_v)
    ids = lax.dynamic_slice_in_dim(pairs.reshape(-1), me * SLOTS, SLOTS)
    lens = lengths[ids]
    contexts = [attend(query[s], key[s ^ 1], value[s ^ 1], lens[s ^ 1]) for s in range(SLOTS)]
    returned = exchange(jnp.stack(contexts, axis=1)).reshape(count * SLOTS, width)
    summed = lax.dot_general(
        selector, returned, (((0,), (0,)), ((), ())), preferred_element_type=jnp.float32
    ).astype(jnp.bfloat16)
    total = exchange(summed.reshape(count, 1, width)).reshape(residues, width)
    update = jnp.dot(total, weight_o, preferred_element_type=jnp.float32)
    own_len = jnp.sum(jnp.where(holder == me, lengths, 0))
    update = jnp.where(jnp.arange(residues, dtype=jnp.int32)[:, None] < own_len, update, 0.0)
    return (embeddings.astype(jnp.float32) + update[None]).astype(jnp.bfloat16)


def solution(mesh):
    in_specs = (P(AXES, None, None), P(), P(), P(), P(), P(), P(), P())
    out_specs = P(AXES, None, None)
    return jax.shard_map(local, mesh=mesh, in_specs=in_specs, out_specs=out_specs, check_vma=False)
```

time: 402 us -> 198 us (0.49)
  waiting for transfers between devices: 215 us -> 35.1 us
  blocking collectives: 61.6 us -> 26.6 us
  starting transfers between devices: 5.4 us -> 23.1 us
  between operations: 13.6 us -> 0.2 us
  matrix products: 34 us -> 38.8 us
    reduce_scatter x1 -> x0, waiting for transfers between devices: 95.9 us -> none  [local(): lax.psum_scatter(summed.reshape(dev_count, residues, model_width).astype(...]
    all_gather x1 -> x0, waiting for transfers between devices: 60.8 us -> none  [local(): whole_group = lax.all_gather(embeddings, 'dev', axis=0, tiled=True)]
    all_to_all x1, blocking collectives: 61.6 us -> 26.6 us  [exchange(): return lax.all_to_all(array, AXES, split_axis=0, concat_axis=0, tiled=True)]
    slice x0 -> x16, local copies, waits for them, and re-layouts: none -> 27.6 us  [the longest x5 9.85 us: local(): query[s]]
    all_to_all x1 -> x3, waiting for transfers between devices: 57.9 us -> 35.1 us  [exchange(): return lax.all_to_all(array, AXES, split_axis=0, concat_axis=0, tiled=True)]
    rev x3 -> x0, local copies, waits for them, and re-layouts: 20.9 us -> none  [partner_of(): jnp.flip(array.reshape((PAIR_DEV, 2) + array.shape[1:]), axis=1)]
    all_to_all x1 -> x3, starting transfers between devices: 5.17 us -> 23.1 us  [exchange(): return lax.all_to_all(array, AXES, split_axis=0, concat_axis=0, tiled=True)]
    sub x0 -> x4, matrix products: none -> 11 us  [attend(): exponent = jnp.exp(scores - jnp.max(scores, axis=-1, keepdims=True))]
  transfers between devices with their start and end apart: 3 -> 3, of which waited for: 3 -> 3; matrix products, arithmetic and copies ran while one was open for 1% -> 5% of each run, Pallas kernels for 0% -> 0%
where the time goes in v1:
time: 198 us; the launch traced here: 196 us
  local copies, waits for them, and re-layouts  59.2 us (30%)
  matrix products  38.8 us (20%)
  waiting for transfers between devices  35.1 us (18%)
  blocking collectives  26.6 us (13%)
  starting transfers between devices  23.1 us (12%)
  other arithmetic  13.4 us (7%)
    all_to_all x3, waiting for transfers between devices, exchange(): return lax.all_to_all(array, AXES, split_axis=0, concat_axis=0, tiled=True)  35.1 us
    all_to_all x1, blocking collectives, exchange(): return lax.all_to_all(array, AXES, split_axis=0, concat_axis=0, tiled=True)  26.6 us
    all_to_all x3, starting transfers between devices, exchange(): return lax.all_to_all(array, AXES, split_axis=0, concat_axis=0, tiled=True)  23.1 us
    sub x4, matrix products, attend(): exponent = jnp.exp(scores - jnp.max(scores, axis=-1, keepdims=True))  11 us
    unnamed x19, local copies, waits for them, and re-layouts  10.1 us
    dot_general x4, matrix products, attend(): jnp.einsum('hij,jhd->ihd', weights, value, preferred_element_type=jnp.flo...  9.89 us
    slice x5, local copies, waits for them, and re-layouts, local(): query[s]  9.85 us
    dot_general x3, matrix products, project(): result = jnp.dot(features, weight, preferred_element_type=jnp.float32)  9.14 us
  transfers between devices with their start and end apart: 3, of which 3 were waited for; matrix products, arithmetic and copies ran while one was open for 5% of the time, Pallas kernels for 0%

profile of v1, /device:TPU:1, one launch (start us, length us, event | category | flops | bytes accessed | tf_op | source)
XLA Modules:
  0.0 196.4 jit_solution(7406708342347402748)
XLA Ops:
  0.6 2.6 %reduce = bf16[128,1280]{1,0:T(8,128)(2,1)} reduce(bf16[128,1,1280]{2,0,1:T(8,128)(2,1)} %bitcast.67, bf16[]{:T(256)} %broadcast.94), dimensions={1}, to_apply=%copy.73.reduce_sub_computation | reduce | bytes 655362 | tf_op jit(solution)/shard_map/reshape | solution.py:37
  3.2 1.8 reshape.138
  5.0 11.9 %all-to-all-start = ((bf16[128,2,640]{2,1,0:T(2,128)(2,1)}), bf16[128,2,640]{2,1,0:T(2,128)(2,1)}, u32[]{:S(2)}, u32[]{:S(2)}) async-start(bf16[128,2,640]{2,1,0:T(2,128)(2,1)} %reshape.138), calls=%async_computation | async-start | bytes 655360 | tf_op jit(solution)/shard_map/all_to_all | solution.py:13
  17.2 3.3 %gather_fusion = s32[512]{0:T(512)S(1)} fusion(s32[128]{0:T(128)S(1)} %copy-done.1, s32[1024]{0:T(1024)S(1)} %pad_clamp_fusion.1), kind=kCustom, calls=%fused_computation | custom fusion | bytes 6144 | tf_op jit(solution)/shard_map/gather | solution.py:35
  20.5 7.6 %all-to-all-done = bf16[128,2,640]{2,1,0:T(2,128)(2,1)} async-done(((bf16[128,2,640]{2,1,0:T(2,128)(2,1)}), bf16[128,2,640]{2,1,0:T(2,128)(2,1)}, u32[]{:S(2)}, u32[]{:S(2)}) %all-to-all-start) | async-done | bytes 327712 | tf_op jit(solution)/shard_map/all_to_all | solution.py:13
  28.1 3.2 %reshape.139 = bf16[128,1,1280]{2,1,0:T(2,128)(2,1)} reshape(bf16[128,2,640]{2,1,0:T(2,128)(2,1)} %all-to-all-done) | data formatting | bytes 655360
  31.4 2.7 %convolution_convert_fusion.3 = bf16[512,1280]{1,0:T(8,128)(2,1)} fusion(bf16[128,1,1280]{2,1,0:T(2,128)(2,1)} %reshape.139, s32[512]{0:T(512)S(1)} %gather_fusion), kind=kOutput, calls=%fused_computation.9 | convolution fusion | flops 168493056 | bytes 1640448 | tf_op jit(solution)/shard_map/dot_general | solution.py:38
  34.1 3.5 %reshape.115 = bf16[128,4,1280]{2,1,0:T(4,128)(2,1)} reshape(bf16[512,1280]{1,0:T(8,128)(2,1)} %convolution_convert_fusion.3) | data formatting | bytes 2621440 | tf_op jit(solution)/shard_map/reshape | solution.py:39
  37.6 5.5 %all-to-all-start.1 = ((bf16[128,4,1280]{2,1,0:T(4,128)(2,1)}), bf16[128,4,1280]{2,1,0:T(4,128)(2,1)}, u32[]{:S(2)}, u32[]{:S(2)}) async-start(bf16[128,4,1280]{2,1,0:T(4,128)(2,1)} %reshape.115), calls=%async_computation.1 | async-start | bytes 2621440 | tf_op jit(solution)/shard_map/all_to_all | solution.py:13
  47.1 17.5 %all-to-all-done.1 = bf16[128,4,1280]{2,1,0:T(4,128)(2,1)} async-done(((bf16[128,4,1280]{2,1,0:T(4,128)(2,1)}), bf16[128,4,1280]{2,1,0:T(4,128)(2,1)}, u32[]{:S(2)}, u32[]{:S(2)}) %all-to-all-start.1) | async-done | bytes 1310752 | tf_op jit(solution)/shard_map/all_to_all | solution.py:13
  66.0 1.9 convolution_convert_fusion
  69.0 1.9 copy.78
  70.9 1.9 copy.90
  72.7 1.9 copy.86
  74.6 1.9 copy.82
  76.5 5.4 %convolution_convert_fusion.1 = bf16[512,1280]{1,0:T(8,128)(2,1)} fusion(bf16[512,1280]{1,0:T(8,128)(2,1)} %bitcast.69, bf16[1280,1280]{1,0:T(8,128)(2,1)} %param.9), kind=kOutput, calls=%fused_computation.7 | convolution fusion | flops 1678376960 | bytes 5898240 | tf_op jit(solution)/shard_map/dot_general | solution.py:43
  81.9 1.9 convolution_convert_fusion.2
  84.8 1.9 copy.75
  86.7 2.4 %fusion.40 = (bf16[128,1280]{1,0:T(8,128)(2,1)}, bf16[128,1280]{1,0:T(8,128)(2,1)}, bf16[128,1280]{1,0:T(8,128)(2,1)}, bf16[128,1280]{1,0:T(8,128)(2,1)}) fusion(bf16[512,1280]{1,0:T(8,128)(2,1)} %convolution_convert_fusion.1), kind=kLoop, calls=%fused_computation.72 | loop fusion | bytes 2621440 | tf_op jit(solution)/shard_map/slice | solution.py:49
  89.1 1.9 copy.77
  90.9 1.9 copy.89
  92.8 1.9 copy.85
  94.7 1.9 copy.81
  96.6 1.9 copy.88
  98.4 1.9 copy.84
  100.3 1.9 copy.80
  102.1 2.8 %fusion.45 = (f32[20,128]{1,0:T(8,128)S(1)}, f32[20,128,128]{1,2,0:T(8,128)}) fusion(bf16[128,20,64]{0,2,1:T(8,128)(2,1)} %bitcast.81, bf16[128,20,64]{0,2,1:T(8,128)(2,1)} %bitcast.78, pred[128]{0:T(512)(128)(4,1)S(1)} %iota_compare_fusion.5), kind=kOutput, calls=%fused_computation.77 | convolution fusion | flops 43253888 | bytes 1976448 | tf_op jit(solution)/shard_map/sub | solution.py:25
  104.9 2.5 %convolution_convert_fusion.7 = bf16[20,64,128]{2,1,0:T(8,128)(2,1)} fusion(bf16[128,20,64]{0,2,1:T(8,128)(2,1)} %bitcast.82, f32[20,128,128]{1,2,0:T(8,128)} %get-tuple-element.26, f32[20,128]{1,0:T(8,128)S(1)} %get-tuple-element.25), kind=kOutput, calls=%fused_computation.39 | convolution fusion | flops 42762240 | bytes 1976320 | tf_op jit(solution)/shard_map/hij,jhd->ihd/dot_general | solution.py:27
  107.4 2.1 %copy.93 = bf16[128,1,1280]{2,1,0:T(2,128)(2,1)} copy(bf16[128,1,1280]{0,2,1:T(8,128)(2,1)} %bitcast.83) | data formatting | bytes 655360 | tf_op jit(solution)/shard_map/stack;reshape | solution.py:50
  109.5 2.8 %fusion.44 = (f32[20,128]{1,0:T(8,128)S(1)}, f32[20,128,128]{1,2,0:T(8,128)}) fusion(bf16[128,20,64]{0,2,1:T(8,128)(2,1)} %bitcast.79, bf16[128,20,64]{0,2,1:T(8,128)(2,1)} %bitcast.75, pred[128]{0:T(512)(128)(4,1)S(1)} %iota_compare_fusion.4), kind=kOutput, calls=%fused_computation.76 | convolution fusion | flops 43253888 | bytes 1976448 | tf_op jit(solution)/shard_map/sub | solution.py:25
  112.2 2.5 %convolution_convert_fusion.6 = bf16[20,64,128]{2,1,0:T(8,128)(2,1)} fusion(bf16[128,20,64]{0,2,1:T(8,128)(2,1)} %bitcast.80, f32[20,128,128]{1,2,0:T(8,128)} %get-tuple-element.24, f32[20,128]{1,0:T(8,128)S(1)} %get-tuple-element.23), kind=kOutput, calls=%fused_computation.38 | convolution fusion | flops 42762240 | bytes 1976320 | tf_op jit(solution)/shard_map/hij,jhd->ihd/dot_general | solution.py:27
  114.7 2.1 %copy.94 = bf16[128,1,1280]{2,1,0:T(2,128)(2,1)} copy(bf16[128,1,1280]{0,2,1:T(8,128)(2,1)} %bitcast.84) | data formatting | bytes 655360 | tf_op jit(solution)/shard_map/stack;reshape | solution.py:50
  116.8 2.8 %fusion.43 = (f32[20,128]{1,0:T(8,128)S(1)}, f32[20,128,128]{1,2,0:T(8,128)}) fusion(bf16[128,20,64]{0,2,1:T(8,128)(2,1)} %bitcast.76, bf16[128,20,64]{0,2,1:T(8,128)(2,1)} %bitcast.73, pred[128]{0:T(512)(128)(4,1)S(1)} %iota_compare_fusion.3), kind=kOutput, calls=%fused_computation.75 | convolution fusion | flops 43253888 | bytes 1976448 | tf_op jit(solution)/shard_map/sub | solution.py:25
  119.5 2.5 %convolution_convert_fusion.5 = bf16[20,64,128]{2,1,0:T(8,128)(2,1)} fusion(bf16[128,20,64]{0,2,1:T(8,128)(2,1)} %bitcast.77, f32[20,128,128]{1,2,0:T(8,128)} %get-tuple-element.22, f32[20,128]{1,0:T(8,128)S(1)} %get-tuple-element.21), kind=kOutput, calls=%fused_computation.37 | convolution fusion | flops 42762240 | bytes 1976320 | tf_op jit(solution)/shard_map/hij,jhd->ihd/dot_general | solution.py:27
  122.0 2.1 %copy.95 = bf16[128,1,1280]{2,1,0:T(2,128)(2,1)} copy(bf16[128,1,1280]{0,2,1:T(8,128)(2,1)} %bitcast.85) | data formatting | bytes 655360 | tf_op jit(solution)/shard_map/stack;reshape | solution.py:50
  124.1 2.8 %fusion.46 = (f32[20,128]{1,0:T(8,128)S(1)}, f32[20,128,128]{1,2,0:T(8,128)}) fusion(bf16[128,20,64]{0,2,1:T(8,128)(2,1)} %bitcast.74, bf16[128,20,64]{0,2,1:T(8,128)(2,1)} %bitcast.71, pred[128]{0:T(512)(128)(4,1)S(1)} %iota_compare_fusion.6), kind=kOutput, calls=%fused_computation.78 | convolution fusion | flops 43253888 | bytes 1976448 | tf_op jit(solution)/shard_map/sub | solution.py:25
  126.9 2.5 %convolution_convert_fusion.8 = bf16[20,64,128]{2,1,0:T(8,128)(2,1)} fusion(bf16[128,20,64]{0,2,1:T(8,128)(2,1)} %bitcast.72, f32[20,128,128]{1,2,0:T(8,128)} %get-tuple-element.28, f32[20,128]{1,0:T(8,128)S(1)} %get-tuple-element.27), kind=kOutput, calls=%fused_computation.40 | convolution fusion | flops 42762240 | bytes 1976320 | tf_op jit(solution)/shard_map/hij,jhd->ihd/dot_general | solution.py:27
  129.3 2.1 %copy.92 = bf16[128,1,1280]{2,1,0:T(2,128)(2,1)} copy(bf16[128,1,1280]{0,2,1:T(8,128)(2,1)} %bitcast.86) | data formatting | bytes 655360 | tf_op jit(solution)/shard_map/stack;reshape | solution.py:50
  131.4 4.4 %pad_maximum_fusion = bf16[128,4,1280]{2,1,0:T(4,128)(2,1)S(1)} fusion(bf16[128,1,1280]{2,1,0:T(2,128)(2,1)} %copy.95, bf16[128,1,1280]{2,1,0:T(2,128)(2,1)} %copy.94, bf16[128,1,1280]{2,1,0:T(2,128)(2,1)} %copy.93, bf16[128,1,1280]{2,1,0:T(2,128)(2,1)} %copy.92), kind=kLoop, calls=%fused_computation.32 | loop fusion | flops 5242880 | bytes 2621440 | tf_op jit(solution)/shard_map/stack | solution.py:50
  135.8 26.6 %all_to_all.20 = bf16[128,4,1280]{2,1,0:T(4,128)(2,1)} all-to-all(bf16[128,4,1280]{2,1,0:T(4,128)(2,1)S(1)} %pad_maximum_fusion), channel_id=1, replica_groups=mesh['group'=4,'dev'=32] {'group','dev'}, dimensions={0} | all-to-all | bytes 2621440 | tf_op jit(solution)/shard_map/all_to_all | solution.py:13
  162.4 3.4 %reshape.118 = bf16[512,1280]{1,0:T(8,128)(2,1)} reshape(bf16[128,4,1280]{2,1,0:T(4,128)(2,1)} %all_to_all.20) | data formatting | bytes 2621440 | tf_op jit(solution)/shard_map/reshape | solution.py:50
  165.7 2.5 %fusion.7 = bf16[128,1,1280]{2,0,1:T(8,128)(2,1)} fusion(bf16[512,1280]{1,0:T(8,128)(2,1)} %reshape.118, s32[512]{0:T(512)S(1)} %gather_fusion), kind=kOutput, calls=%fused_computation.15 | convolution fusion | flops 168001536 | bytes 1640448 | tf_op jit(solution)/shard_map/dot_general | solution.py:51
  168.3 2.5 %reduce.1 = bf16[128,1280]{1,0:T(8,128)(2,1)} reduce(bf16[128,1,1280]{2,0,1:T(8,128)(2,1)} %fusion.7, bf16[]{:T(256)} %broadcast.94), dimensions={1}, to_apply=%copy.96.reduce_sub_computation | reduce | bytes 655362 | tf_op jit(solution)/shard_map/reshape | solution.py:54
  170.8 1.8 reshape.140
  172.6 5.7 %all-to-all-start.3 = ((bf16[128,2,640]{2,1,0:T(2,128)(2,1)}), bf16[128,2,640]{2,1,0:T(2,128)(2,1)}, u32[]{:S(2)}, u32[]{:S(2)}) async-start(bf16[128,2,640]{2,1,0:T(2,128)(2,1)} %reshape.140), calls=%async_computation.3 | async-start | bytes 655360 | tf_op jit(solution)/shard_map/all_to_all | solution.py:13
  179.7 10.0 %all-to-all-done.3 = bf16[128,2,640]{2,1,0:T(2,128)(2,1)} async-done(((bf16[128,2,640]{2,1,0:T(2,128)(2,1)}), bf16[128,2,640]{2,1,0:T(2,128)(2,1)}, u32[]{:S(2)}, u32[]{:S(2)}) %all-to-all-start.3) | async-done | bytes 327712 | tf_op jit(solution)/shard_map/all_to_all | solution.py:13
  189.7 3.2 %reshape.141 = bf16[128,1,1280]{2,1,0:T(2,128)(2,1)} reshape(bf16[128,2,640]{2,1,0:T(2,128)(2,1)} %all-to-all-done.3) | data formatting | bytes 655360
  192.9 3.5 %fusion.6 = bf16[1,128,1280]{2,1,0:T(8,128)(2,1)} fusion(bf16[1280,1280]{1,0:T(8,128)(2,1)} %param.12, bf16[1,128,1280]{2,1,0:T(8,128)(2,1)} %param.8, bf16[128,1,1280]{2,1,0:T(2,128)(2,1)} %reshape.141, pred[128]{0:T(512)(128)(4,1)S(1)} %iota_compare_fusion.7), kind=kOutput, calls=%fused_computation.13 | convolution fusion | flops 420085760 | bytes 4259968 | tf_op jit(solution)/shard_map/dot_general | solution.py:55
  (33 shorter events, 9.9 us)
Async XLA Ops:
  0.0 66.0 %copy-start = (bf16[1280,1280]{1,0:T(8,128)(2,1)S(1)}, bf16[1280,1280]{1,0:T(8,128)(2,1)}, u32[]{:S(2)}) copy-start(bf16[1280,1280]{1,0:T(8,128)(2,1)} %param.10) | copy-start | bytes 9830404
  0.0 16.9 %copy-start.5 = (s32[256,2]{0,1:T(2,128)S(1)}, s32[256,2]{0,1:T(2,128)}, u32[]{:S(2)}) copy-start(s32[256,2]{0,1:T(2,128)} %param.13) | copy-start | bytes 6148
  0.0 17.2 %copy-start.1 = (s32[128]{0:T(128)S(1)}, s32[128]{0:T(128)}, u32[]{:S(2)}) copy-start(s32[128]{0:T(128)} %param.15) | copy-start | bytes 1540
  5.0 23.2 %all-to-all-start = ((bf16[128,2,640]{2,1,0:T(2,128)(2,1)}), bf16[128,2,640]{2,1,0:T(2,128)(2,1)}, u32[]{:S(2)}, u32[]{:S(2)}) async-start(bf16[128,2,640]{2,1,0:T(2,128)(2,1)} %reshape.138), calls=%async_computation | async-start | bytes 655360 | tf_op jit(solution)/shard_map/all_to_all | solution.py:13
  37.6 5.7 %copy-start.2 = (s32[128]{0:T(128)S(1)}, s32[128]{0:T(128)}, u32[]{:S(2)}) copy-start(s32[128]{0:T(128)} %param.14) | copy-start | bytes 1540
  37.6 27.0 %all-to-all-start.1 = ((bf16[128,4,1280]{2,1,0:T(4,128)(2,1)}), bf16[128,4,1280]{2,1,0:T(4,128)(2,1)}, u32[]{:S(2)}, u32[]{:S(2)}) async-start(bf16[128,4,1280]{2,1,0:T(4,128)(2,1)} %reshape.115), calls=%async_computation.1 | async-start | bytes 2621440 | tf_op jit(solution)/shard_map/all_to_all | solution.py:13
  66.0 1.9 copy-start.3
  76.5 5.4 %copy-start.4 = (bf16[128,4,1280]{2,0,1:T(8,128)(2,1)S(1)}, bf16[128,4,1280]{2,0,1:T(8,128)(2,1)}, u32[]{:S(2)}) copy-start(bf16[128,4,1280]{2,0,1:T(8,128)(2,1)} %copy-done.3) | copy-start | bytes 3932164
  76.5 5.4 %copy-start.6 = (bf16[1280,1280]{1,0:T(8,128)(2,1)S(1)}, bf16[1280,1280]{1,0:T(8,128)(2,1)}, u32[]{:S(2)}) copy-start(bf16[1280,1280]{1,0:T(8,128)(2,1)} %param.11) | copy-start | bytes 9830404
  172.6 17.1 %all-to-all-start.3 = ((bf16[128,2,640]{2,1,0:T(2,128)(2,1)}), bf16[128,2,640]{2,1,0:T(2,128)(2,1)}, u32[]{:S(2)}, u32[]{:S(2)}) async-start(bf16[128,2,640]{2,1,0:T(2,128)(2,1)} %reshape.140), calls=%async_computation.3 | async-start | bytes 655360 | tf_op jit(solution)/shard_map/all_to_all | solution.py:13

commit v2 on v1

v2 whole, which is shorter than its diff:
```python
import functools

import jax
import jax.numpy as jnp
from jax import lax
from jax.experimental import pallas as pl
from jax.experimental.pallas import tpu as pltpu
from jax.sharding import PartitionSpec as P

HEAD_DIM = 64
AXES = ("group", "dev")
BLOCK = 64
UNITS = 16
BF = jnp.bfloat16
F32 = jnp.float32


def exchange(array):
    return lax.all_to_all(array, AXES, split_axis=0, concat_axis=0, tiled=True)


def swap(array):
    count = lax.axis_size("dev")
    return lax.ppermute(array, "dev", [(i, i ^ 1) for i in range(count)])


def mm(a, b):
    return jnp.dot(a, b, preferred_element_type=F32)


def plan(pairs, lengths, holder):
    own, other = pairs.reshape(-1), pairs[:, ::-1].reshape(-1)
    place, source, length = holder[own], holder[other], lengths[other]
    amount = 1 + (length > BLOCK).astype(jnp.int32)
    order = jnp.arange(own.shape[0], dtype=jnp.int32)
    earlier = order[:, None] < order[None, :]
    chip = place // 2
    same = chip[:, None] == chip[None, :]
    column = amount[:, None]
    before = jnp.sum(jnp.where(same & earlier, column, 0), axis=0)
    whole = jnp.sum(jnp.where(same, column, 0), axis=0)
    dest = 2 * chip + (2 * before + amount > whole).astype(jnp.int32)
    alike = (dest[:, None] == dest[None, :]) & earlier
    base = jnp.sum(jnp.where(alike, column, 0), axis=0)
    rank = jnp.sum(alike.astype(jnp.int32), axis=0)
    fits = jnp.max(base + amount) <= UNITS
    half = UNITS // 2
    turn = jnp.where(fits, 0, rank // half)
    slot = jnp.where(fits, rank, rank % half)
    base = jnp.where(fits, base, 2 * slot)
    return dest, source, length, amount, base, slot, turn, place % 2, jnp.max(turn) + 1


def attend_kernel(meta, got, query, weight_k, weight_v, out, rows, keys, values):
    width = weight_k.shape[0]
    half = width // 2
    lead = lax.broadcasted_iota(jnp.int32, (256, 256), 0)
    lane = lax.broadcasted_iota(jnp.int32, (256, 256), 1)
    turned = ((lead // 16 == lane % 16) & (lead % 16 == lane // 16)).astype(BF)
    for side in range(2):
        for part in range(BLOCK // 16):
            at = side * BLOCK + part * 16
            piece = mm(turned, got[at : at + 16].reshape(256, half)).astype(BF)
            for u in range(UNITS):
                to = u * BLOCK + part * 16
                rows[to : to + 16, side * half : (side + 1) * half] = piece[u * 16 : (u + 1) * 16]

    def project(chunk, carry):
        at = pl.ds(pl.multiple_of(chunk * 256, 256), 256)
        block = rows[at, :]
        keys[at, :] = mm(block, weight_k[...]).astype(BF)
        values[at, :] = mm(block, weight_v[...]).astype(BF)
        return carry

    lax.fori_loop(0, UNITS * BLOCK // 256, project, 0)
    tail = pl.ds(UNITS * BLOCK, BLOCK)
    keys[tail, :] = jnp.zeros((BLOCK, width), BF)
    values[tail, :] = jnp.zeros((BLOCK, width), BF)
    out[...] = jnp.zeros_like(out)
    first = lax.broadcasted_iota(jnp.int32, (128, 128), 1) < HEAD_DIM
    ones = jnp.ones((128, 128), BF)
    none = jnp.zeros((128, 128), BF)
    sums = jnp.concatenate([jnp.where(first, ones, none), jnp.where(first, none, ones)], axis=0)
    position = lax.broadcasted_iota(jnp.int32, (128, 128), 1)

    def item(index, carry):
        start = pl.multiple_of(meta[1 + index] * BLOCK, BLOCK)
        length = meta[1 + UNITS + index]
        whose = pl.multiple_of(meta[1 + 2 * UNITS + index] * 128, 128)
        live = position < length
        for pair in range(width // 128):
            at = slice(pair * 128, (pair + 1) * 128)
            q = query[pl.ds(whose, 128), at]
            k = keys[pl.ds(start, 128), at]
            v = values[pl.ds(start, 128), at]
            k2 = jnp.concatenate([jnp.where(first, k, none), jnp.where(first, none, k)], axis=0)
            v2 = jnp.concatenate([jnp.where(first, v, none), jnp.where(first, none, v)], axis=0)
            scores = lax.dot_general(q, k2, (((1,), (1,)), ((), ())), preferred_element_type=F32)
            parts = []
            for head in range(2):
                s = jnp.where(live, scores[:, head * 128 : (head + 1) * 128], -1e30)
                parts.append(jnp.exp(s - jnp.max(s, axis=1, keepdims=True)).astype(BF))
            weights = jnp.concatenate(parts, axis=1)
            result = mm(weights, jnp.concatenate([v2, sums], axis=1))
            out[pl.ds(whose, 128), at] += result[:, :128] / result[:, 128:]
        return carry

    lax.fori_loop(0, meta[0], item, 0)


def attend(meta, got, query, weight_k, weight_v):
    width = weight_k.shape[0]
    vmem = pl.BlockSpec(memory_space=pltpu.VMEM)
    return pl.pallas_call(
        attend_kernel,
        out_shape=jax.ShapeDtypeStruct((256, width), F32),
        in_specs=[pl.BlockSpec(memory_space=pltpu.SMEM)] + [vmem] * 4,
        out_specs=vmem,
        scratch_shapes=[
            pltpu.VMEM((UNITS * BLOCK, width), BF),
            pltpu.VMEM(((UNITS + 1) * BLOCK, width), BF),
            pltpu.VMEM(((UNITS + 1) * BLOCK, width), BF),
        ],
        compiler_params=pltpu.CompilerParams(vmem_limit_bytes=40 * 1024 * 1024),
        cost_estimate=pl.CostEstimate(flops=10**10, bytes_accessed=10**7, transcendentals=10**6),
    )(meta, got, query, weight_k, weight_v)


def local(embeddings, weight_q, weight_k, weight_v, weight_o, pairs, lengths, holder):
    residues, width = embeddings.shape[1:]
    half = width // 2
    count = lax.axis_size("group") * lax.axis_size("dev")
    me = lax.axis_index("group") * lax.axis_size("dev") + lax.axis_index("dev")
    own = embeddings[0]
    pieces = own.reshape(2, BLOCK, 2, half).transpose(2, 1, 0, 3).reshape(count, 2, half)
    mine = exchange(pieces).reshape(2 * count, half)
    query = mm(jnp.concatenate([own, swap(own)], axis=0), weight_q).astype(BF) * BF(HEAD_DIM**-0.5)
    dest, source, length, amount, base, slot, turn, core, rounds = plan(pairs, lengths, holder)
    spots = jnp.arange(UNITS, dtype=jnp.int32)
    devices = jnp.arange(count, dtype=jnp.int32)

    def one_round(number):
        active = turn == number
        target = ((dest[None, :] == devices[:, None]) & active[None, :]).astype(BF)
        entry = jnp.where(base[:, None] == spots[None, :], 2 * source[:, None] + 1, 0)
        second = (base[:, None] + 1 == spots[None, :]) & (amount[:, None] == 2)
        entry = jnp.where(second, 2 * source[:, None] + 2, entry)
        table = mm(target, entry.astype(BF)).astype(jnp.int32)
        units = 1 + jnp.arange(2 * count, dtype=jnp.int32)
        selector = (table.reshape(-1)[:, None] == units[None, :]).astype(BF)
        picked = mm(selector, mine).astype(BF)
        got = exchange(picked.reshape(count, UNITS, half))
        held = active & (dest == me)
        chosen = held[None, :] & (slot[None, :] == spots[:, None])

        def listed(values):
            return jnp.sum(jnp.where(chosen, values[None, :], 0), axis=1)

        number_held = jnp.sum(held.astype(jnp.int32)).reshape(1)
        whose = listed(core ^ (me % 2))
        meta = jnp.concatenate([number_held, listed(base), listed(length), whose])
        return attend(meta, got, query, weight_k, weight_v)

    total = one_round(0)
    _, total = lax.while_loop(
        lambda c: c[0] < rounds, lambda c: (c[0] + 1, c[1] + one_round(c[0])), (jnp.int32(1), total)
    )
    context = total[:residues] + swap(total[residues:].astype(BF)).astype(F32)
    update = mm(context.astype(BF), weight_o)
    own_len = jnp.sum(jnp.where(holder == me, lengths, 0))
    update = jnp.where(jnp.arange(residues, dtype=jnp.int32)[:, None] < own_len, update, 0.0)
    return (embeddings.astype(F32) + update[None]).astype(BF)


def solution(mesh):
    in_specs = (P(AXES, None, None), P(), P(), P(), P(), P(), P(), P())
    out_specs = P(AXES, None, None)
    return jax.shard_map(local, mesh=mesh, in_specs=in_specs, out_specs=out_specs, check_vma=False)
```

time: 198 us -> 113 us (0.57)
  local copies, waits for them, and re-layouts: 59.2 us -> 19.4 us
  matrix products: 38.8 us -> 10.3 us
  blocking collectives: 26.6 us -> 0 us
  Pallas kernels: 0 us -> 15 us
  other arithmetic: 13.4 us -> 4.73 us
  waiting for transfers between devices: 35.1 us -> 40.6 us
  starting transfers between devices: 23.1 us -> 20.4 us
    all_to_all x1 -> x0, blocking collectives: 26.6 us -> none  [exchange(): return lax.all_to_all(array, AXES, split_axis=0, concat_axis=0, tiled=True)]
    slice x16 -> x1, local copies, waits for them, and re-layouts: 27.6 us -> 1.13 us  [local(): context = total[:residues] + swap(total[residues:].astype(BF)).astype(F32)]
    dot_general x10 -> x4, matrix products: 27.8 us -> 10.3 us  [mm(): return jnp.dot(a, b, preferred_element_type=F32)]
    pallas_call x0 -> x1, Pallas kernels: none -> 15 us  [attend(): pl.pallas_call(attend_kernel, out_shape=jax.ShapeDtypeStruct((256, width)...]
    sub x4 -> x0, matrix products: 11 us -> none  [attend(): exponent = jnp.exp(scores - jnp.max(scores, axis=-1, keepdims=True))]
    unnamed x19 -> x7, local copies, waits for them, and re-layouts: 10.1 us -> 0.96 us
    another operation x4 -> x1, local copies, waits for them, and re-layouts: 8.34 us -> 1.77 us  [local(): own.reshape(2, BLOCK, 2, half).transpose(2, 1, 0, 3).reshape(count, 2, half)]
    gather x2 -> x3, local copies, waits for them, and re-layouts: 3.99 us -> 10.1 us  [plan(): place, source, length = (holder[own], holder[other], lengths[other])]
  transfers between devices with their start and end apart: 3 -> 4, of which waited for: 3 -> 3; matrix products, arithmetic and copies ran while one was open for 5% -> 5% of each run, Pallas kernels for 0% -> 0%
where the time goes in v2:
time: 113 us; the launch traced here: 112 us
  waiting for transfers between devices  40.6 us (36%)
  starting transfers between devices  20.4 us (18%)
  local copies, waits for them, and re-layouts  19.4 us (17%)
  Pallas kernels  15 us (13%)
  matrix products  10.3 us (9%)
  other arithmetic  4.73 us (4%)
  between operations  1.56 us (1%)
    all_to_all x2, waiting for transfers between devices, exchange(): return lax.all_to_all(array, AXES, split_axis=0, concat_axis=0, tiled=True)  40.5 us
    all_to_all x2, starting transfers between devices, exchange(): return lax.all_to_all(array, AXES, split_axis=0, concat_axis=0, tiled=True)  17.3 us
    pallas_call x1, Pallas kernels, attend(): pl.pallas_call(attend_kernel, out_shape=jax.ShapeDtypeStruct((256, width)...  15 us
    dot_general x4, matrix products, mm(): return jnp.dot(a, b, preferred_element_type=F32)  10.3 us
    gather x3, local copies, waits for them, and re-layouts, plan(): place, source, length = (holder[own], holder[other], lengths[other])  10.1 us
    ppermute x2, starting transfers between devices, swap(): return lax.ppermute(array, 'dev', [(i, i ^ 1) for i in range(count)])  3.14 us
  transfers between devices with their start and end apart: 4, of which 3 were waited for; matrix products, arithmetic and copies ran while one was open for 5% of the time, Pallas kernels for 0%

profile of v2, /device:TPU:1, one launch (start us, length us, event | category | flops | bytes accessed | tf_op | source)
XLA Modules:
  0.0 112.0 jit_solution(17804862617674621257)
XLA Ops:
  0.0 0.0 copy-start
  0.0 0.0 copy-start.1
  0.0 0.9 rev.3
  0.9 0.9 copy.16
  1.8 0.1 copy.17
  2.0 0.1 reshape.321
  2.2 3.4 %gather_fusion.1 = s32[512]{0:T(512)S(1)} fusion(s32[128]{0:T(128)} %param.16, s32[1024]{0:T(1024)S(1)} %pad_clamp_fusion), kind=kCustom, calls=%fused_computation.1 | custom fusion | bytes 6144 | tf_op jit(solution)/shard_map/gather | solution.py:33
  5.6 0.1 reshape.320
  5.8 0.0 copy-done.1
  5.8 3.3 %gather_fusion.2 = s32[512]{0:T(512)S(1)} fusion(s32[128]{0:T(128)S(1)} %copy-done.1, s32[1024]{0:T(1024)S(1)} %pad_clamp_fusion), kind=kCustom, calls=%fused_computation.2 | custom fusion | bytes 6144 | tf_op jit(solution)/shard_map/gather | solution.py:33
  9.2 3.3 %gather_fusion = s32[512]{0:T(512)S(1)} fusion(s32[128]{0:T(128)S(1)} %copy-done.1, s32[1024]{0:T(1024)S(1)} %pad_clamp_fusion.1), kind=kCustom, calls=%fused_computation | custom fusion | bytes 6144 | tf_op jit(solution)/shard_map/gather | solution.py:33
  12.5 0.3 select_reduce_fusion.4
  12.9 0.2 select_reduce_fusion.3
  13.1 0.7 add_reduce_fusion
  13.8 1.8 %reshape_squeeze.3 = bf16[2,64,2,640]{3,2,1,0:T(2,128)(2,1)} reshape(bf16[1,128,1280]{2,1,0:T(8,128)(2,1)} %param.10) | data formatting | bytes 655360 | tf_op jit(solution)/shard_map/reshape;squeeze | solution.py:135
  15.6 2.0 %copy.19 = bf16[2,64,2,640]{3,2,1,0:T(2,128)(2,1)} copy(bf16[2,64,2,640]{3,0,1,2:T(2,128)(2,1)} %bitcast.30) | data formatting | bytes 655360 | tf_op jit(solution)/shard_map/transpose | solution.py:135
  18.3 0.7 fusion.52
  19.0 0.6 convert_reduce_fusion.2
  19.7 11.9 %all-to-all-start.1 = ((bf16[128,2,640]{2,1,0:T(2,128)(2,1)}), bf16[128,2,640]{2,1,0:T(2,128)(2,1)}, u32[]{:S(2)}, u32[]{:S(2)}) async-start(bf16[128,2,640]{2,1,0:T(2,128)(2,1)} %bitcast.29), calls=%async_computation.1 | async-start | bytes 655360 | tf_op jit(solution)/shard_map/all_to_all | solution.py:19
  31.6 0.6 convolution_convert_fusion.4
  32.1 0.1 copy.18
  32.3 0.1 eq.306
  32.4 10.5 %all-to-all-done.1 = bf16[128,2,640]{2,1,0:T(2,128)(2,1)} async-done(((bf16[128,2,640]{2,1,0:T(2,128)(2,1)}), bf16[128,2,640]{2,1,0:T(2,128)(2,1)}, u32[]{:S(2)}, u32[]{:S(2)}) %all-to-all-start.1) | async-done | bytes 327712 | tf_op jit(solution)/shard_map/all_to_all | solution.py:19
  42.8 1.8 %reshape.324 = bf16[256,640]{1,0:T(8,128)(2,1)} reshape(bf16[128,2,640]{2,1,0:T(2,128)(2,1)} %all-to-all-done.1) | data formatting | bytes 655360 | tf_op jit(solution)/shard_map/reshape | solution.py:136
  44.7 3.3 %convolution_convert_fusion.2 = bf16[2048,640]{1,0:T(8,128)(2,1)} fusion(bf16[256,640]{1,0:T(8,128)(2,1)} %reshape.324, s32[256]{0:T(256)S(1)} %iota_add_fusion.1, s32[2048]{0:T(1024)S(1)} %eq.306), kind=kOutput, calls=%fused_computation.40 | convolution fusion | flops 672923648 | bytes 2958336 | tf_op jit(solution)/shard_map/dot_general | solution.py:28
  48.0 5.4 %all-to-all-start.2 = ((bf16[128,16,640]{2,1,0:T(8,128)(2,1)}), bf16[128,16,640]{2,1,0:T(8,128)(2,1)}, u32[]{:S(2)}, u32[]{:S(2)}) async-start(bf16[128,16,640]{2,1,0:T(8,128)(2,1)} %bitcast.26), calls=%async_computation.2 | async-start | bytes 5242880 | tf_op jit(solution)/shard_map/all_to_all | solution.py:19
  53.3 1.4 %collective-permute-start = (bf16[128,1280]{1,0:T(8,128)(2,1)}, bf16[128,1280]{1,0:T(8,128)(2,1)}, u32[]{:S(2)}, u32[]{:S(2)}) collective-permute-start(bf16[128,1280]{1,0:T(8,128)(2,1)} %bitcast.27), channel_id=1, source_target_pairs={{0,1},{1,0},{2,3},{3,2},{4,5},{5,4},{6,7},{7,6},{8,9},{9,8},{10,11... | collective-permute-start | bytes 983048 | tf_op jit(solution)/shard_map/ppermute | solution.py:24
  55.4 0.2 select_reduce_fusion.7
  55.5 0.6 pad_add_fusion.1.meta
  56.2 0.1 collective-permute-done
  56.3 0.0 copy-done
  56.3 2.9 %fusion.20.query = bf16[256,1280]{1,0:T(8,128)(2,1)} fusion(bf16[1280,1280]{1,0:T(8,128)(2,1)S(1)} %copy-done, bf16[128,1280]{1,0:T(8,128)(2,1)} %collective-permute-done, bf16[128,1280]{1,0:T(8,128)(2,1)} %bitcast.28), kind=kOutput, calls=%fused_computation.43 | convolution fusion | flops 840826880 | bytes 4587520 | tf_op jit(solution)/shard_map/dot_general | solution.py:28
  59.2 30.1 %all-to-all-done.2.got = bf16[128,16,640]{2,1,0:T(8,128)(2,1)} async-done(((bf16[128,16,640]{2,1,0:T(8,128)(2,1)}), bf16[128,16,640]{2,1,0:T(8,128)(2,1)}, u32[]{:S(2)}, u32[]{:S(2)}) %all-to-all-start.2) | async-done | bytes 2621472 | tf_op jit(solution)/shard_map/all_to_all | solution.py:19
  89.3 15.0 %shard_map.82 = f32[256,1280]{1,0:T(8,128)} custom-call(s32[49]{0:T(128)S(1)} %pad_add_fusion.1.meta, bf16[128,16,640]{2,1,0:T(8,128)(2,1)} %all-to-all-done.2.got, bf16[256,1280]{1,0:T(8,128)(2,1)} %fusion.20.query, bf16[1280,1280]{1,0:T(8,128)(2,1)} %weight_k.1, bf16[1280,1280]{1,0:T(8,128)(2,1)} %weight_v.1), custom_call_target="tpu_custom_call" | custom-call | flops 10000000000 | bytes 10000000 | tf_op jit(solution)/shard_map/pallas_call | solution.py:114
  104.3 0.0 copy-start.2
  104.3 1.1 %slice.19 = bf16[128,1280]{1,0:T(8,128)(2,1)S(1)} slice(f32[256,1280]{1,0:T(8,128)} %get-tuple-element.226), slice={[128:256], [0:1280]} | slice | bytes 655360 | tf_op jit(solution)/shard_map/slice | solution.py:168
  105.5 1.8 %collective-permute-start.1 = (bf16[128,1280]{1,0:T(8,128)(2,1)S(1)}, bf16[128,1280]{1,0:T(8,128)(2,1)S(1)}, u32[]{:S(2)}, u32[]{:S(2)}) collective-permute-start(bf16[128,1280]{1,0:T(8,128)(2,1)S(1)} %slice.19), channel_id=1, source_target_pairs={{0,1},{1,0},{2,3},{3,2},{4,5},{5,4},{6,7},{7,6},{8,9},{9,8},{10,11... | collective-permute-start | bytes 983048 | tf_op jit(solution)/shard_map/ppermute | solution.py:24
  107.2 0.0 copy-done.2
  107.2 0.6 fusion.49
  107.9 0.6 iota_compare_fusion.9
  108.5 0.0 collective-permute-done.1
  108.5 3.5 %fusion.23 = bf16[1,128,1280]{2,1,0:T(8,128)(2,1)} fusion(bf16[1280,1280]{1,0:T(8,128)(2,1)} %param.14, bf16[1,128,1280]{2,1,0:T(8,128)(2,1)} %param.10, bf16[128,1280]{1,0:T(8,128)(2,1)S(1)} %collective-permute-done.1, f32[256,1280]{1,0:T(8,128)} %get-tuple-element.226, pred[128]{0:T(512)(128)(4,1)S(1)} %iota_compare_fusion.9), kind=kOutput, calls=%fused_computation.46 | convolution fusion | flops 420577280 | bytes 4915328 | tf_op jit(solution)/shard_map/dot_general | solution.py:28
  (10 shorter events, 0.1 us)
Async XLA Ops:
  0.0 56.3 %copy-start = (bf16[1280,1280]{1,0:T(8,128)(2,1)S(1)}, bf16[1280,1280]{1,0:T(8,128)(2,1)}, u32[]{:S(2)}) copy-start(bf16[1280,1280]{1,0:T(8,128)(2,1)} %param.11) | copy-start | bytes 9830404
  0.0 5.8 %copy-start.1 = (s32[128]{0:T(128)S(1)}, s32[128]{0:T(128)}, u32[]{:S(2)}) copy-start(s32[128]{0:T(128)} %param.17) | copy-start | bytes 1540
  19.7 23.2 %all-to-all-start.1 = ((bf16[128,2,640]{2,1,0:T(2,128)(2,1)}), bf16[128,2,640]{2,1,0:T(2,128)(2,1)}, u32[]{:S(2)}, u32[]{:S(2)}) async-start(bf16[128,2,640]{2,1,0:T(2,128)(2,1)} %bitcast.29), calls=%async_computation.1 | async-start | bytes 655360 | tf_op jit(solution)/shard_map/all_to_all | solution.py:19
  48.0 41.3 %all-to-all-start.2 = ((bf16[128,16,640]{2,1,0:T(8,128)(2,1)}), bf16[128,16,640]{2,1,0:T(8,128)(2,1)}, u32[]{:S(2)}, u32[]{:S(2)}) async-start(bf16[128,16,640]{2,1,0:T(8,128)(2,1)} %bitcast.26), calls=%async_computation.2 | async-start | bytes 5242880 | tf_op jit(solution)/shard_map/all_to_all | solution.py:19
  53.3 2.9 %collective-permute-start = (bf16[128,1280]{1,0:T(8,128)(2,1)}, bf16[128,1280]{1,0:T(8,128)(2,1)}, u32[]{:S(2)}, u32[]{:S(2)}) collective-permute-start(bf16[128,1280]{1,0:T(8,128)(2,1)} %bitcast.27), channel_id=1, source_target_pairs={{0,1},{1,0},{2,3},{3,2},{4,5},{5,4},{6,7},{7,6},{8,9},{9,8},{10,11... | collective-permute-start | bytes 983048 | tf_op jit(solution)/shard_map/ppermute | solution.py:24
  104.3 2.9 %copy-start.2 = (s32[128]{0:T(128)S(1)}, s32[128]{0:T(128)}, u32[]{:S(2)}) copy-start(s32[128]{0:T(128)} %param.16) | copy-start | bytes 1540
  105.5 3.1 %collective-permute-start.1 = (bf16[128,1280]{1,0:T(8,128)(2,1)S(1)}, bf16[128,1280]{1,0:T(8,128)(2,1)S(1)}, u32[]{:S(2)}, u32[]{:S(2)}) collective-permute-start(bf16[128,1280]{1,0:T(8,128)(2,1)S(1)} %slice.19), channel_id=1, source_target_pairs={{0,1},{1,0},{2,3},{3,2},{4,5},{5,4},{6,7},{7,6},{8,9},{9,8},{10,11... | collective-permute-start | bytes 983048 | tf_op jit(solution)/shard_map/ppermute | solution.py:24

commit v3 on v2

v3 whole, which is shorter than its diff:
```python
import jax
import jax.numpy as jnp
from jax import lax
from jax.experimental import pallas as pl
from jax.experimental.pallas import tpu as pltpu
from jax.sharding import PartitionSpec as P

HEAD_DIM = 64
AXES = ("group", "dev")
BLOCK = 64
UNITS = 16
BF = jnp.bfloat16
F32 = jnp.float32


def exchange(array):
    return lax.all_to_all(array, AXES, split_axis=0, concat_axis=0, tiled=True)


def swap(array):
    count = lax.axis_size("dev")
    return lax.ppermute(array, "dev", [(i, i ^ 1) for i in range(count)])


def mm(a, b):
    return jnp.dot(a, b, preferred_element_type=F32)


def plan_kernel(place, pairs, lengths, holder, selector, meta, sides):
    me = place[0]
    count = pairs.shape[0]
    total = 2 * count
    devices = holder.shape[1]
    lane = lax.broadcasted_iota(jnp.int32, (count, devices), 1)
    marks = [pairs[:, i : i + 1] == lane for i in range(2)]
    held_at = holder[...].astype(F32)
    long = lengths[...].astype(F32)
    places = [jnp.sum(jnp.where(m, held_at, 0.0), axis=1, keepdims=True) for m in marks]
    sizes = [jnp.sum(jnp.where(m, long, 0.0), axis=1, keepdims=True) for m in marks]
    place_col = jnp.concatenate(places, axis=0)
    source_col = jnp.concatenate(places[::-1], axis=0)
    length_col = jnp.concatenate(sizes[::-1], axis=0)
    lane = lax.broadcasted_iota(jnp.int32, (total, devices), 1)
    listed = jnp.where(lane == 0, place_col, jnp.where(lane == 1, source_col, length_col))
    turned = jnp.transpose(listed).astype(jnp.int32)
    place_row, source, length = turned[0:1], turned[1:2], turned[2:3]
    amount = 1 + (length > BLOCK).astype(jnp.int32)
    amount_col = 1.0 + (length_col > BLOCK).astype(F32)
    chip = place_row // 2
    lead = lax.broadcasted_iota(jnp.int32, (total, total), 0)
    follow = lax.broadcasted_iota(jnp.int32, (total, total), 1)
    earlier = lead < follow
    same = place_col.astype(jnp.int32) // 2 == chip
    before = jnp.sum(jnp.where(same & earlier, amount_col, 0.0), axis=0, keepdims=True)
    whole = jnp.sum(jnp.where(same, amount_col, 0.0), axis=0, keepdims=True)
    later = 2.0 * before + amount.astype(F32) > whole
    dest = 2 * chip + later.astype(jnp.int32)
    dest_col = jnp.transpose(jnp.broadcast_to(dest.astype(F32), (devices, total)))[:, 0:1]
    alike = (dest_col.astype(jnp.int32) == dest) & earlier
    base = jnp.sum(jnp.where(alike, amount_col, 0.0), axis=0, keepdims=True).astype(jnp.int32)
    rank = jnp.sum(jnp.where(alike, 1.0, 0.0), axis=0, keepdims=True).astype(jnp.int32)
    half = UNITS // 2
    fits = jnp.max(base + amount, axis=1, keepdims=True) <= UNITS
    turn = jnp.where(fits, 0, rank // half)
    slot = jnp.where(fits, rank, rank % half)
    base = jnp.where(fits, base, 2 * slot)
    sides[...] = jnp.concatenate([dest, source, length, amount, base, slot, turn, place_row], axis=0)
    active = turn == 0
    spot = lax.broadcasted_iota(jnp.int32, (devices, total), 0)
    target = jnp.where((dest == spot) & active, 1.0, 0.0).astype(BF)
    entry = jnp.where(base == spot, 2 * source + 1, 0)
    entry = jnp.where((base + 1 == spot) & (amount == 2), 2 * source + 2, entry)
    across = (((1,), (1,)), ((), ()))
    table = lax.dot_general(target, entry.astype(F32).astype(BF), across, preferred_element_type=F32)
    row = lax.broadcasted_iota(jnp.int32, (devices * UNITS, devices), 0)
    lane = lax.broadcasted_iota(jnp.int32, (devices * UNITS, devices), 1)
    spread = mm(jnp.where(row // UNITS == lane, 1.0, 0.0).astype(BF), table.astype(BF))
    unit = jnp.sum(jnp.where(row % UNITS == lane, spread, 0.0), axis=1, keepdims=True)
    units = lax.broadcasted_iota(jnp.int32, selector.shape, 1)
    selector[...] = jnp.where(unit.astype(jnp.int32) == units + 1, 1.0, 0.0).astype(BF)
    held = active & (dest == me)
    spot = lax.broadcasted_iota(jnp.int32, (UNITS, total), 0)
    chosen = held & (slot == spot)

    def column(values):
        return jnp.sum(jnp.where(chosen, values.astype(F32), 0.0), axis=1, keepdims=True)

    whose = (place_row + me) % 2
    amount_held = jnp.sum(jnp.where(held, 1.0, 0.0), axis=1, keepdims=True)
    lane = lax.broadcasted_iota(jnp.int32, meta.shape, 1)
    listed = jnp.where(lane == 1, column(length), column(base))
    listed = jnp.where(lane == 2, column(whose), listed)
    meta[...] = jnp.where(lane == 3, amount_held, listed).astype(jnp.int32)


def plan(me, pairs, lengths, holder):
    devices = holder.shape[0]
    vmem = pl.BlockSpec(memory_space=pltpu.VMEM)
    return pl.pallas_call(
        plan_kernel,
        out_shape=(
            jax.ShapeDtypeStruct((devices * UNITS, 2 * devices), BF),
            jax.ShapeDtypeStruct((UNITS, 128), jnp.int32),
            jax.ShapeDtypeStruct((8, 2 * pairs.shape[0]), jnp.int32),
        ),
        in_specs=[pl.BlockSpec(memory_space=pltpu.SMEM)] + [vmem] * 3,
        out_specs=(vmem,) * 3,
        compiler_params=pltpu.CompilerParams(vmem_limit_bytes=24 * 1024 * 1024),
        cost_estimate=pl.CostEstimate(flops=10**9, bytes_accessed=10**6, transcendentals=0),
    )(me.reshape(1), pairs, lengths.reshape(1, -1), holder.reshape(1, -1))


def front_kernel(own, pieces):
    half = own.shape[1] // 2
    for side in range(2):
        for j in range(2):
            pieces[side * BLOCK : (side + 1) * BLOCK, j, :] = own[
                j * BLOCK : (j + 1) * BLOCK, side * half : (side + 1) * half
            ]


def front(own):
    rows, width = own.shape
    vmem = pl.BlockSpec(memory_space=pltpu.VMEM)
    return pl.pallas_call(
        front_kernel,
        out_shape=jax.ShapeDtypeStruct((rows, 2, width // 2), BF),
        in_specs=[vmem],
        out_specs=vmem,
    )(own)


def pick_kernel(selector, mine, picked):
    rows, _, half = mine.shape
    units = mine[...].reshape(2 * rows, half)

    def some(chunk, carry):
        at = pl.ds(pl.multiple_of(chunk * 512, 512), 512)
        picked[at, :] = mm(selector[at, :], units).astype(BF)
        return carry

    lax.fori_loop(0, selector.shape[0] // 512, some, 0)


def pick(selector, mine):
    vmem = pl.BlockSpec(memory_space=pltpu.VMEM)
    return pl.pallas_call(
        pick_kernel,
        out_shape=jax.ShapeDtypeStruct((selector.shape[0], mine.shape[2]), BF),
        in_specs=[vmem] * 2,
        out_specs=vmem,
        compiler_params=pltpu.CompilerParams(vmem_limit_bytes=24 * 1024 * 1024),
        cost_estimate=pl.CostEstimate(flops=10**9, bytes_accessed=10**7, transcendentals=0),
    )(selector, mine)


def attend_kernel(
    meta, got, query, weight_k, weight_v, weight_o, out, sibling, rows, keys, values, context
):
    width = weight_k.shape[0]
    half = width // 2
    lead = lax.broadcasted_iota(jnp.int32, (256, 256), 0)
    lane = lax.broadcasted_iota(jnp.int32, (256, 256), 1)
    turned = ((lead // 16 == lane % 16) & (lead % 16 == lane // 16)).astype(BF)
    for side in range(2):
        for part in range(BLOCK // 16):
            at = side * BLOCK + part * 16
            piece = mm(turned, got[at : at + 16].reshape(256, half)).astype(BF)
            for u in range(UNITS):
                to = u * BLOCK + part * 16
                rows[to : to + 16, side * half : (side + 1) * half] = piece[u * 16 : (u + 1) * 16]

    def project(chunk, carry):
        at = pl.ds(pl.multiple_of(chunk * 256, 256), 256)
        block = rows[at, :]
        keys[at, :] = mm(block, weight_k[...]).astype(BF)
        values[at, :] = mm(block, weight_v[...]).astype(BF)
        return carry

    lax.fori_loop(0, UNITS * BLOCK // 256, project, 0)
    tail = pl.ds(UNITS * BLOCK, BLOCK)
    keys[tail, :] = jnp.zeros((BLOCK, width), BF)
    values[tail, :] = jnp.zeros((BLOCK, width), BF)
    context[...] = jnp.zeros_like(context)
    first = lax.broadcasted_iota(jnp.int32, (128, 128), 1) < HEAD_DIM
    ones = jnp.ones((128, 128), BF)
    none = jnp.zeros((128, 128), BF)
    sums = jnp.concatenate([jnp.where(first, ones, none), jnp.where(first, none, ones)], axis=0)
    position = lax.broadcasted_iota(jnp.int32, (128, 128), 1)

    def item(index, carry):
        start = pl.multiple_of(meta[index, 0] * BLOCK, BLOCK)
        length = meta[index, 1]
        whose = pl.multiple_of(meta[index, 2] * 128, 128)
        live = position < length
        for pair in range(width // 128):
            at = slice(pair * 128, (pair + 1) * 128)
            q = query[pl.ds(whose, 128), at]
            k = keys[pl.ds(start, 128), at]
            v = values[pl.ds(start, 128), at]
            k2 = jnp.concatenate([jnp.where(first, k, none), jnp.where(first, none, k)], axis=0)
            v2 = jnp.concatenate([jnp.where(first, v, none), jnp.where(first, none, v)], axis=0)
            scores = lax.dot_general(q, k2, (((1,), (1,)), ((), ())), preferred_element_type=F32)
            parts = []
            for head in range(2):
                s = jnp.where(live, scores[:, head * 128 : (head + 1) * 128], -1e30)
                parts.append(jnp.exp(s - jnp.max(s, axis=1, keepdims=True)).astype(BF))
            weights = jnp.concatenate(parts, axis=1)
            result = mm(weights, jnp.concatenate([v2, sums], axis=1))
            context[pl.ds(whose, 128), at] += result[:, :128] / result[:, 128:]
        return carry

    lax.fori_loop(0, meta[0, 3], item, 0)
    update = mm(context[...].astype(BF), weight_o[...])
    out[...] = update[:128]
    sibling[...] = update[128:].astype(BF)


def attend(meta, got, query, weight_k, weight_v, weight_o):
    width = weight_k.shape[0]
    vmem = pl.BlockSpec(memory_space=pltpu.VMEM)
    return pl.pallas_call(
        attend_kernel,
        out_shape=(
            jax.ShapeDtypeStruct((128, width), F32),
            jax.ShapeDtypeStruct((128, width), BF),
        ),
        in_specs=[pl.BlockSpec(memory_space=pltpu.SMEM)] + [vmem] * 5,
        out_specs=(vmem, vmem),
        scratch_shapes=[
            pltpu.VMEM((UNITS * BLOCK, width), BF),
            pltpu.VMEM(((UNITS + 1) * BLOCK, width), BF),
            pltpu.VMEM(((UNITS + 1) * BLOCK, width), BF),
            pltpu.VMEM((256, width), F32),
        ],
        compiler_params=pltpu.CompilerParams(vmem_limit_bytes=40 * 1024 * 1024),
        cost_estimate=pl.CostEstimate(flops=10**10, bytes_accessed=10**7, transcendentals=10**6),
    )(meta, got, query, weight_k, weight_v, weight_o)


def later_round(number, sides, me, count):
    dest, source, length, amount, base, slot, turn, place = sides
    spots = jnp.arange(UNITS, dtype=jnp.int32)
    active = turn == number
    target = (dest[None, :] == jnp.arange(count, dtype=jnp.int32)[:, None]) & active[None, :]
    entry = jnp.where(base[:, None] == spots[None, :], 2 * source[:, None] + 1, 0)
    second = (base[:, None] + 1 == spots[None, :]) & (amount[:, None] == 2)
    entry = jnp.where(second, 2 * source[:, None] + 2, entry)
    table = mm(target.astype(BF), entry.astype(BF)).astype(jnp.int32)
    units = 1 + jnp.arange(2 * count, dtype=jnp.int32)
    selector = (table.reshape(-1)[:, None] == units[None, :]).astype(BF)
    held = active & (dest == me)
    chosen = held[None, :] & (slot[None, :] == spots[:, None])

    def listed(values):
        return jnp.sum(jnp.where(chosen, values[None, :], 0), axis=1)

    amount_held = jnp.broadcast_to(jnp.sum(held.astype(jnp.int32)), (UNITS,))
    columns = [listed(base), listed(length), listed((place + me) % 2), amount_held]
    meta = jnp.stack(columns, axis=1)
    return selector, jnp.pad(meta, ((0, 0), (0, 124)))


def local(embeddings, weight_q, weight_k, weight_v, weight_o, pairs, lengths, holder):
    residues, width = embeddings.shape[1:]
    count = lax.axis_size("group") * lax.axis_size("dev")
    me = lax.axis_index("group") * lax.axis_size("dev") + lax.axis_index("dev")
    own = embeddings[0]
    mine = exchange(front(own))
    selector, meta, sides = plan(me, pairs, lengths, holder)
    rounds = jnp.max(sides[6]) + 1
    both = jnp.concatenate([own, swap(own)], axis=0)
    query = (mm(both, weight_q) * HEAD_DIM**-0.5).astype(BF)

    def one_round(selector, meta):
        got = exchange(pick(selector, mine).reshape(count, UNITS, width // 2))
        return attend(meta, got, query, weight_k, weight_v, weight_o)

    def another(carry):
        number, kept, given = carry
        more, also = one_round(*later_round(number, sides, me, count))
        given = (given.astype(F32) + also.astype(F32)).astype(BF)
        return number + 1, kept + more, given

    kept, given = one_round(selector, meta)
    _, kept, given = lax.while_loop(lambda c: c[0] < rounds, another, (jnp.int32(1), kept, given))
    update = kept + swap(given).astype(F32)
    own_len = jnp.sum(jnp.where(holder == me, lengths, 0))
    update = jnp.where(jnp.arange(residues, dtype=jnp.int32)[:, None] < own_len, update, 0.0)
    return (embeddings.astype(F32) + update[None]).astype(BF)


def solution(mesh):
    in_specs = (P(AXES, None, None), P(), P(), P(), P(), P(), P(), P())
    out_specs = P(AXES, None, None)
    return jax.shard_map(local, mesh=mesh, in_specs=in_specs, out_specs=out_specs, check_vma=False)
```

time: 113 us -> 95.4 us (0.84)
  local copies, waits for them, and re-layouts: 19.4 us -> 5.83 us
  Pallas kernels: 15 us -> 24.2 us
  matrix products: 10.3 us -> 2.95 us
  waiting for transfers between devices: 40.6 us -> 36.6 us
    gather x3 -> x0, local copies, waits for them, and re-layouts: 10.1 us -> none  [plan(): place, source, length = (holder[own], holder[other], lengths[other])]
    pallas_call x1 -> x4, Pallas kernels: 15 us -> 24.2 us  [the longest x1 17.4 us: attend(): pl.pallas_call(attend_kernel, out_shape=(jax.ShapeDtypeStruct((128, width...]
    dot_general x4 -> x1, matrix products: 10.3 us -> 2.95 us  [mm(): return jnp.dot(a, b, preferred_element_type=F32)]
    unnamed x7 -> x17, local copies, waits for them, and re-layouts: 0.96 us -> 5.83 us
    all_to_all x2, waiting for transfers between devices: 40.5 us -> 36.1 us  [exchange(): return lax.all_to_all(array, AXES, split_axis=0, concat_axis=0, tiled=True)]
    reshape x3 -> x0, local copies, waits for them, and re-layouts: 2.1 us -> none  [the longest x1 1.82 us: local(): mine = exchange(pieces).reshape(2 * count, half)]
    convert_element_type x0 -> x1, other arithmetic: none -> 2.04 us  [local(): return (embeddings.astype(F32) + update[None]).astype(BF)]
    transpose x1 -> x0, local copies, waits for them, and re-layouts: 2.02 us -> none  [local(): own.reshape(2, BLOCK, 2, half).transpose(2, 1, 0, 3).reshape(count, 2, half)]
  transfers between devices with their start and end apart: 4 -> 4, of which waited for: 3 -> 4; matrix products, arithmetic and copies ran while one was open for 5% -> 6% of each run, Pallas kernels for 0% -> 2%
where the time goes in v3:
time: 95.4 us; the launch traced here: 94.8 us
  waiting for transfers between devices  36.6 us (38%)
  Pallas kernels  24.2 us (25%)
  starting transfers between devices  20.4 us (21%)
  local copies, waits for them, and re-layouts  5.83 us (6%)
  other arithmetic  3.89 us (4%)
  matrix products  2.95 us (3%)
    all_to_all x2, waiting for transfers between devices, exchange(): return lax.all_to_all(array, AXES, split_axis=0, concat_axis=0, tiled=True)  36.1 us
    pallas_call x1, Pallas kernels, attend(): pl.pallas_call(attend_kernel, out_shape=(jax.ShapeDtypeStruct((128, width...  17.4 us
    all_to_all x2, starting transfers between devices, exchange(): return lax.all_to_all(array, AXES, split_axis=0, concat_axis=0, tiled=True)  17.3 us
    unnamed x17, local copies, waits for them, and re-layouts  5.83 us
    ppermute x2, starting transfers between devices, swap(): return lax.ppermute(array, 'dev', [(i, i ^ 1) for i in range(count)])  3.14 us
    dot_general x1, matrix products, mm(): return jnp.dot(a, b, preferred_element_type=F32)  2.95 us
    pallas_call x1, Pallas kernels, pick(): pl.pallas_call(pick_kernel, out_shape=jax.ShapeDtypeStruct((selector.shap...  2.57 us
    pallas_call x1, Pallas kernels, plan(): pl.pallas_call(plan_kernel, out_shape=(jax.ShapeDtypeStruct((devices * UN...  2.13 us
  transfers between devices with their start and end apart: 4, of which 4 were waited for; matrix products, arithmetic and copies ran while one was open for 6% of the time, Pallas kernels for 2%

profile of v3, /device:TPU:1, one launch (start us, length us, event | category | flops | bytes accessed | tf_op | source)
XLA Modules:
  0.0 94.8 jit_solution(3241192642477278588)
XLA Ops:
  0.0 0.0 copy-start
  0.0 2.0 %shard_map.83 = bf16[128,2,640]{2,1,0:T(2,128)(2,1)} custom-call(bf16[128,1280]{1,0:T(8,128)(2,1)} %bitcast.50), custom_call_target="tpu_custom_call" | custom-call | tf_op jit(solution)/shard_map/pallas_call | solution.py:125
  2.0 11.9 %all-to-all-start.1 = ((bf16[128,2,640]{2,1,0:T(2,128)(2,1)}), bf16[128,2,640]{2,1,0:T(2,128)(2,1)}, u32[]{:S(2)}, u32[]{:S(2)}) async-start(bf16[128,2,640]{2,1,0:T(2,128)(2,1)} %shard_map.83), calls=%async_computation.1 | async-start | bytes 655360 | tf_op jit(solution)/shard_map/all_to_all | solution.py:17
  13.9 0.8 copy.23.pairs
  14.8 0.0 copy-start.5
  14.8 0.6 copy-done.5
  15.4 0.0 copy-start.7
  15.4 0.7 copy-done.7
  16.1 2.1 %shard_map.82 = (bf16[2048,256]{1,0:T(8,128)(2,1)S(1)}, s32[16,128]{1,0:T(8,128)S(1)}, s32[8,512]{1,0:T(8,128)S(1)}) custom-call(s32[1]{0:T(128)} %bitcast.11.place, s32[256,2]{1,0:T(8,128)S(1)} %copy.23.pairs, s32[1,128]{1,0:T(1,128)S(1)} %bitcast.48, s32[1,128]{1,0:T(1,128)S(1)} %bitcast.49), custom_call_target="tpu_custom_call" | custom-call | flops 1000000000 | bytes 1000000 | tf_op jit(solution)/shard_map/pallas_call | solution.py:99
  18.2 0.0 copy-start.3
  18.2 1.0 %copy-done.3 = bf16[2048,256]{1,0:T(8,128)(2,1)} copy-done((bf16[2048,256]{1,0:T(8,128)(2,1)}, bf16[2048,256]{1,0:T(8,128)(2,1)S(1)}, u32[]{:S(2)}) %copy-start.3) | copy-done | bytes 1048600
  19.2 6.0 %all-to-all-done.1.mine = bf16[128,2,640]{2,1,0:T(2,128)(2,1)} async-done(((bf16[128,2,640]{2,1,0:T(2,128)(2,1)}), bf16[128,2,640]{2,1,0:T(2,128)(2,1)}, u32[]{:S(2)}, u32[]{:S(2)}) %all-to-all-start.1) | async-done | bytes 327712 | tf_op jit(solution)/shard_map/all_to_all | solution.py:17
  25.2 0.0 copy-start.4
  25.2 1.2 %copy-done.4 = bf16[2048,256]{1,0:T(8,128)(2,1)S(1)} copy-done((bf16[2048,256]{1,0:T(8,128)(2,1)S(1)}, bf16[2048,256]{1,0:T(8,128)(2,1)}, u32[]{:S(2)}) %copy-start.4) | copy-done | bytes 1048600
  26.4 2.6 %shard_map.84 = bf16[2048,640]{1,0:T(8,128)(2,1)S(1)} custom-call(bf16[2048,256]{1,0:T(8,128)(2,1)S(1)} %copy-done.4, bf16[128,2,640]{2,1,0:T(2,128)(2,1)} %all-to-all-done.1.mine), custom_call_target="tpu_custom_call" | custom-call | flops 1000000000 | bytes 10000000 | tf_op jit(solution)/shard_map/pallas_call | solution.py:147
  29.0 0.0 copy-start.2
  29.0 1.5 %copy-done.2 = bf16[2048,640]{1,0:T(8,128)(2,1)} copy-done((bf16[2048,640]{1,0:T(8,128)(2,1)}, bf16[2048,640]{1,0:T(8,128)(2,1)S(1)}, u32[]{:S(2)}) %copy-start.2) | copy-done | bytes 2621464
  30.5 5.4 %all-to-all-start.2 = ((bf16[128,16,640]{2,1,0:T(8,128)(2,1)}), bf16[128,16,640]{2,1,0:T(8,128)(2,1)}, u32[]{:S(2)}, u32[]{:S(2)}) async-start(bf16[128,16,640]{2,1,0:T(8,128)(2,1)} %bitcast.47), calls=%async_computation.2 | async-start | bytes 5242880 | tf_op jit(solution)/shard_map/all_to_all | solution.py:17
  35.9 1.4 %collective-permute-start = (bf16[128,1280]{1,0:T(8,128)(2,1)}, bf16[128,1280]{1,0:T(8,128)(2,1)}, u32[]{:S(2)}, u32[]{:S(2)}) collective-permute-start(bf16[128,1280]{1,0:T(8,128)(2,1)} %bitcast.51), channel_id=1, source_target_pairs={{0,1},{1,0},{2,3},{3,2},{4,5},{5,4},{6,7},{7,6},{8,9},{9,8},{10,11... | collective-permute-start | bytes 983048 | tf_op jit(solution)/shard_map/ppermute | solution.py:22
  37.3 0.6 slice_reduce_fusion
  38.6 0.3 collective-permute-done
  38.9 0.0 copy-done
  38.9 3.0 %fusion.14.query = bf16[256,1280]{1,0:T(8,128)(2,1)} fusion(bf16[1280,1280]{1,0:T(8,128)(2,1)S(1)} %copy-done, bf16[128,1280]{1,0:T(8,128)(2,1)} %collective-permute-done, bf16[128,1280]{1,0:T(8,128)(2,1)} %bitcast.52), kind=kOutput, calls=%fused_computation.38 | convolution fusion | flops 840826880 | bytes 4587520 | tf_op jit(solution)/shard_map/dot_general | solution.py:26
  41.8 30.1 %all-to-all-done.2.got = bf16[128,16,640]{2,1,0:T(8,128)(2,1)} async-done(((bf16[128,16,640]{2,1,0:T(8,128)(2,1)}), bf16[128,16,640]{2,1,0:T(8,128)(2,1)}, u32[]{:S(2)}, u32[]{:S(2)}) %all-to-all-start.2) | async-done | bytes 2621472 | tf_op jit(solution)/shard_map/all_to_all | solution.py:17
  71.9 17.4 %shard_map.85 = (f32[128,1280]{1,0:T(8,128)}, bf16[128,1280]{1,0:T(8,128)(2,1)}) custom-call(s32[16,128]{1,0:T(8,128)S(1)} %get-tuple-element.149.meta, bf16[128,16,640]{2,1,0:T(8,128)(2,1)} %all-to-all-done.2.got, bf16[256,1280]{1,0:T(8,128)(2,1)} %fusion.14.query, bf16[1280,1280]{1,0:T(8,128)(2,1)} %weight_k.1, bf16[1280,1280]{1,0:T(8,128)(2,1)} %weight_v.1, ...), custom_call_target="tpu_custom_call" | custom-call | flops 10000000000 | bytes 10000000 | tf_op jit(solution)/shard_map/pallas_call | solution.py:222
  89.3 0.0 copy-start.6
  89.3 0.0 copy-start.8
  89.3 0.1 while.14
  89.5 1.8 %collective-permute-start.1 = (bf16[128,1280]{1,0:T(8,128)(2,1)}, bf16[128,1280]{1,0:T(8,128)(2,1)S(1)}, u32[]{:S(2)}, u32[]{:S(2)}) collective-permute-start(bf16[128,1280]{1,0:T(8,128)(2,1)} %get-tuple-element.155), channel_id=1, source_target_pairs={{0,1},{1,0},{2,3},{3,2},{4,5},{5,4},{6,7},{7,6},{8,9},{9,8},{10,11... | collective-permute-start | bytes 983048 | tf_op jit(solution)/shard_map/ppermute | solution.py:22
  91.3 0.0 copy-done.6
  91.3 0.0 copy-done.8
  91.3 0.6 fusion.19
  91.9 0.6 iota_compare_fusion.4
  92.5 0.2 collective-permute-done.1
  92.7 2.0 %fusion.18 = bf16[1,128,1280]{2,1,0:T(8,128)(2,1)} fusion(f32[128,1280]{1,0:T(8,128)} %get-tuple-element.154, bf16[128,1280]{1,0:T(8,128)(2,1)S(1)} %collective-permute-done.1, bf16[1,128,1280]{2,1,0:T(8,128)(2,1)} %param.10, pred[128]{0:T(512)(128)(4,1)S(1)} %iota_compare_fusion.4), kind=kLoop, calls=%fused_computation.43 | loop fusion | flops 983040 | bytes 1638528 | tf_op jit(solution)/shard_map/convert_element_type | solution.py:290
Async XLA Ops:
  0.0 38.9 %copy-start = (bf16[1280,1280]{1,0:T(8,128)(2,1)S(1)}, bf16[1280,1280]{1,0:T(8,128)(2,1)}, u32[]{:S(2)}) copy-start(bf16[1280,1280]{1,0:T(8,128)(2,1)} %param.11) | copy-start | bytes 9830404
  2.0 23.2 %all-to-all-start.1 = ((bf16[128,2,640]{2,1,0:T(2,128)(2,1)}), bf16[128,2,640]{2,1,0:T(2,128)(2,1)}, u32[]{:S(2)}, u32[]{:S(2)}) async-start(bf16[128,2,640]{2,1,0:T(2,128)(2,1)} %shard_map.83), calls=%async_computation.1 | async-start | bytes 655360 | tf_op jit(solution)/shard_map/all_to_all | solution.py:17
  14.8 0.7 copy-start.5
  15.4 0.7 copy-start.7
  18.2 1.0 %copy-start.3 = (bf16[2048,256]{1,0:T(8,128)(2,1)}, bf16[2048,256]{1,0:T(8,128)(2,1)S(1)}, u32[]{:S(2)}) copy-start(bf16[2048,256]{1,0:T(8,128)(2,1)S(1)} %get-tuple-element.150.selector) | copy-start | bytes 3145732
  25.2 1.2 %copy-start.4 = (bf16[2048,256]{1,0:T(8,128)(2,1)S(1)}, bf16[2048,256]{1,0:T(8,128)(2,1)}, u32[]{:S(2)}) copy-start(bf16[2048,256]{1,0:T(8,128)(2,1)} %copy-done.3) | copy-start | bytes 3145732
  29.0 1.5 %copy-start.2 = (bf16[2048,640]{1,0:T(8,128)(2,1)}, bf16[2048,640]{1,0:T(8,128)(2,1)S(1)}, u32[]{:S(2)}) copy-start(bf16[2048,640]{1,0:T(8,128)(2,1)S(1)} %shard_map.84) | copy-start | bytes 7864324
  30.5 41.3 %all-to-all-start.2 = ((bf16[128,16,640]{2,1,0:T(8,128)(2,1)}), bf16[128,16,640]{2,1,0:T(8,128)(2,1)}, u32[]{:S(2)}, u32[]{:S(2)}) async-start(bf16[128,16,640]{2,1,0:T(8,128)(2,1)} %bitcast.47), calls=%async_computation.2 | async-start | bytes 5242880 | tf_op jit(solution)/shard_map/all_to_all | solution.py:17
  35.9 2.9 %collective-permute-start = (bf16[128,1280]{1,0:T(8,128)(2,1)}, bf16[128,1280]{1,0:T(8,128)(2,1)}, u32[]{:S(2)}, u32[]{:S(2)}) collective-permute-start(bf16[128,1280]{1,0:T(8,128)(2,1)} %bitcast.51), channel_id=1, source_target_pairs={{0,1},{1,0},{2,3},{3,2},{4,5},{5,4},{6,7},{7,6},{8,9},{9,8},{10,11... | collective-permute-start | bytes 983048 | tf_op jit(solution)/shard_map/ppermute | solution.py:22
  89.3 1.9 %copy-start.6 = (s32[128]{0:T(128)S(1)}, s32[128]{0:T(128)}, u32[]{:S(2)}) copy-start(s32[128]{0:T(128)} %param.16) | copy-start | bytes 1540
  89.3 1.9 %copy-start.8 = (s32[128]{0:T(128)S(1)}, s32[128]{0:T(128)}, u32[]{:S(2)}) copy-start(s32[128]{0:T(128)} %param.17) | copy-start | bytes 1540
  89.5 3.3 %collective-permute-start.1 = (bf16[128,1280]{1,0:T(8,128)(2,1)}, bf16[128,1280]{1,0:T(8,128)(2,1)S(1)}, u32[]{:S(2)}, u32[]{:S(2)}) collective-permute-start(bf16[128,1280]{1,0:T(8,128)(2,1)} %get-tuple-element.155), channel_id=1, source_target_pairs={{0,1},{1,0},{2,3},{3,2},{4,5},{5,4},{6,7},{7,6},{8,9},{9,8},{10,11... | collective-permute-start | bytes 983048 | tf_op jit(solution)/shard_map/ppermute | solution.py:22

commit v4 on v1

v4 whole, which is shorter than its diff:
```python
import jax
import jax.numpy as jnp
from jax import lax
from jax.experimental import pallas as pl
from jax.experimental.pallas import tpu as pltpu
from jax.sharding import PartitionSpec as P

HEAD_DIM = 64
AXES = ("group", "dev")
BLOCK = 32
PARTS = 4
FIRST = 24
LATER = 16
STEP = LATER - PARTS + 1
MIB = 1024 * 1024
BF = jnp.bfloat16
F32 = jnp.float32
VMEM = pl.BlockSpec(memory_space=pltpu.VMEM)
SMEM = pl.BlockSpec(memory_space=pltpu.SMEM)
ANY = pl.BlockSpec(memory_space=pl.ANY)
ACROSS = (((1,), (1,)), ((), ()))
DOWN = (((0,), (0,)), ((), ()))


def exchange(array):
    return lax.all_to_all(array, AXES, split_axis=0, concat_axis=0, tiled=True)


def swap(array):
    count = lax.axis_size("dev")
    return lax.ppermute(array, "dev", [(i, i ^ 1) for i in range(count)])


def mm(a, b):
    return jnp.dot(a, b, preferred_element_type=F32)


def iota(shape, dim):
    return lax.broadcasted_iota(jnp.int32, shape, dim)


def half_turn(array):
    return pltpu.roll(array.astype(F32), 64, 1)


def front_kernel(own, pieces):
    low = iota((BLOCK, 128), 1) < 64
    for quarter in range(4):
        main = slice(256 * quarter, 256 * quarter + 256)
        tile = slice(1024 + 128 * (quarter // 2), 1152 + 128 * (quarter // 2))
        for h in range(2):
            even = slice(2 * h * BLOCK, (2 * h + 1) * BLOCK)
            odd = slice((2 * h + 1) * BLOCK, (2 * h + 2) * BLOCK)
            if quarter % 2 == 0:
                rest = jnp.where(low, own[even, tile].astype(F32), half_turn(own[odd, tile]))
            else:
                rest = jnp.where(low, half_turn(own[even, tile]), own[odd, tile].astype(F32))
            to = slice(quarter * BLOCK, (quarter + 1) * BLOCK)
            pieces[to, h, 0:256] = own[even, main]
            pieces[to, h, 256:512] = own[odd, main]
            pieces[to, h, 512:640] = rest.astype(BF)


def front(own):
    rows, width = own.shape
    return pl.pallas_call(
        front_kernel,
        out_shape=jax.ShapeDtypeStruct((rows, 2, width // 2), BF),
        in_specs=[VMEM],
        out_specs=VMEM,
        compiler_params=pltpu.CompilerParams(vmem_limit_bytes=4 * MIB),
    )(own)


def plan_kernel(place, pairs, lengths, holder, selector, meta, sides):
    me = place[0]
    count = pairs.shape[0]
    total = 2 * count
    devices = holder.shape[1]
    lane = iota((count, devices), 1)
    marks = [pairs[:, i : i + 1] == lane for i in range(2)]
    held_at = holder[...].astype(F32)
    long = lengths[...].astype(F32)
    places = [jnp.sum(jnp.where(m, held_at, 0.0), axis=1, keepdims=True) for m in marks]
    sizes = [jnp.sum(jnp.where(m, long, 0.0), axis=1, keepdims=True) for m in marks]
    place_col = jnp.concatenate(places, axis=0)
    source_col = jnp.concatenate(places[::-1], axis=0)
    length_col = jnp.concatenate(sizes[::-1], axis=0)
    lane = iota((total, devices), 1)
    listed = jnp.where(lane == 0, place_col, jnp.where(lane == 1, source_col, length_col))
    turned = jnp.transpose(listed).astype(jnp.int32)
    place_row, source, length = turned[0:1], turned[1:2], turned[2:3]
    amount = (length + (BLOCK - 1)) // BLOCK
    amount_col = ((length_col.astype(jnp.int32) + (BLOCK - 1)) // BLOCK).astype(F32)
    chip = place_row // 2
    earlier = iota((total, total), 0) < iota((total, total), 1)
    same = place_col.astype(jnp.int32) // 2 == chip
    before = jnp.sum(jnp.where(same & earlier, amount_col, 0.0), axis=0, keepdims=True)
    whole = jnp.sum(jnp.where(same, amount_col, 0.0), axis=0, keepdims=True)
    second = 2.0 * before + amount.astype(F32) > whole
    dest = 2 * chip + second.astype(jnp.int32)
    dest_col = jnp.transpose(jnp.broadcast_to(dest.astype(F32), (devices, total)))[:, 0:1]
    alike = (dest_col.astype(jnp.int32) == dest) & earlier
    base = jnp.sum(jnp.where(alike, amount_col, 0.0), axis=0, keepdims=True).astype(jnp.int32)
    slot = jnp.sum(jnp.where(alike, 1.0, 0.0), axis=0, keepdims=True).astype(jnp.int32)
    sides[...] = jnp.concatenate(
        [dest, source, length, amount, base, slot, place_row, place_row], axis=0
    )
    active = base + amount <= FIRST
    spot = iota((devices, total), 0)
    target = jnp.where((dest == spot) & active, 1.0, 0.0).astype(BF)
    there = (base <= spot) & (spot < base + amount)
    entry = jnp.where(there, source + 1, 0)
    shifted = spot - 64
    entry = entry + jnp.where((base <= shifted) & (shifted < base + amount), shifted - base, 0)
    table = lax.dot_general(target, entry.astype(F32).astype(BF), ACROSS, preferred_element_type=F32)
    rows = devices * FIRST // 2
    row, lane = iota((rows, devices), 0), iota((rows, devices), 1)
    which, v = lax.div(row, jnp.int32(FIRST // 2)), lax.rem(row, jnp.int32(FIRST // 2))
    spread = mm(jnp.where(which == lane, 1.0, 0.0).astype(BF), table.astype(BF))
    columns = iota((rows, 4 * devices), 1)
    unit_at = 2 * (columns % (2 * devices)) + columns // (2 * devices)
    for side in range(2):
        u = 2 * v + side
        value = jnp.where(lane == u, 4.0 * spread, jnp.where(lane == u + 64, spread, 0.0))
        unit = jnp.sum(value, axis=1, keepdims=True).astype(jnp.int32) - 4
        at = slice(side * 4 * devices, (side + 1) * 4 * devices)
        selector[:, at] = jnp.where(unit == unit_at, 1.0, 0.0).astype(BF)
    held = active & (dest == me)
    chosen = held & (slot == iota((FIRST, total), 0))

    def column(values):
        return jnp.sum(jnp.where(chosen, values.astype(F32), 0.0), axis=1, keepdims=True)

    amount_held = jnp.sum(jnp.where(held, 1.0, 0.0), axis=1, keepdims=True)
    rounds = jnp.max(jnp.where(active, 0, 1 + (base - (FIRST - PARTS + 1)) // STEP), axis=1, keepdims=True)
    ends = [
        jnp.sum(jnp.where(holder[...] == which, long, 0.0), axis=1, keepdims=True)
        for which in (me, me + 1 - 2 * (me % 2))
    ]
    lane = iota(meta.shape, 1)
    listed = jnp.where(lane == 1, column(length), column(base))
    listed = jnp.where(lane == 2, column((place_row + me) % 2), listed)
    listed = jnp.where(lane == 3, amount_held, listed)
    listed = jnp.where(lane == 4, ends[0], jnp.where(lane == 5, ends[1], listed))
    meta[...] = jnp.where(lane == 6, rounds.astype(F32), listed).astype(jnp.int32)


def plan(me, pairs, lengths, holder):
    devices = holder.shape[0]
    return pl.pallas_call(
        plan_kernel,
        out_shape=(
            jax.ShapeDtypeStruct((devices * FIRST // 2, 8 * devices), BF),
            jax.ShapeDtypeStruct((FIRST, 128), jnp.int32),
            jax.ShapeDtypeStruct((8, 2 * pairs.shape[0]), jnp.int32),
        ),
        in_specs=[SMEM] + [VMEM] * 3,
        out_specs=(VMEM,) * 3,
        compiler_params=pltpu.CompilerParams(vmem_limit_bytes=16 * MIB),
        cost_estimate=pl.CostEstimate(flops=10**9, bytes_accessed=10**6, transcendentals=0),
    )(me.reshape(1), pairs, lengths.reshape(1, -1), holder.reshape(1, -1))


def pick_kernel(selector, mine, picked):
    rows, _, half = mine.shape
    units = mine[...].reshape(2 * rows, half)
    ends = units[:, 512:640].astype(F32)
    turned = half_turn(ends)
    low = iota(ends.shape, 1) < 64
    nil = jnp.zeros_like(ends)
    main = jnp.concatenate([units[:, 0:256], units[:, 256:512]], axis=0)
    ends_low = jnp.concatenate([jnp.where(low, ends, nil), jnp.where(low, turned, nil)], axis=0)
    ends_high = jnp.concatenate([jnp.where(low, nil, turned), jnp.where(low, nil, ends)], axis=0)
    even = jnp.concatenate([main, ends_low.astype(BF)], axis=1)
    odd = jnp.concatenate([main, ends_high.astype(BF)], axis=1)
    outer = picked.shape[1:-1]
    each = 1
    for n in outer:
        each *= n

    def some(chunk, carry):
        at = pl.ds(pl.multiple_of(chunk * (32 * each), 32 * each), 32 * each)
        first = mm(selector[at, : 4 * rows], even)
        second = mm(selector[at, 4 * rows :], odd)
        rest = first[:, 256:] + second[:, 256:]
        message = jnp.concatenate([first[:, :256], second[:, :256], rest], axis=1).astype(BF)
        picked[pl.ds(chunk * 32, 32)] = message.reshape((32,) + outer + (half,))
        return carry

    lax.fori_loop(0, rows // 32, some, 0)


def pick(selector, mine, outer):
    devices, _, half = mine.shape
    return pl.pallas_call(
        pick_kernel,
        out_shape=jax.ShapeDtypeStruct((devices,) + outer + (half,), BF),
        in_specs=[VMEM] * 2,
        out_specs=VMEM,
        compiler_params=pltpu.CompilerParams(vmem_limit_bytes=16 * MIB),
        cost_estimate=pl.CostEstimate(flops=10**9, bytes_accessed=10**7, transcendentals=0),
    )(selector, mine)


def query_kernel(own, other, weight, query):
    first = iota((128, 128), 1) < HEAD_DIM
    none = jnp.zeros((128, 128), BF)
    for who, rows in enumerate((own, other)):
        result = (mm(rows[...], weight[...]).astype(BF)) * BF(HEAD_DIM**-0.5)
        for pair in range(result.shape[1] // 128):
            at = (who * (result.shape[1] // 128) + pair) * 256
            tile = result[:, pair * 128 : (pair + 1) * 128]
            query[at : at + 128, :] = jnp.where(first, tile, none)
            query[at + 128 : at + 256, :] = jnp.where(first, none, tile)


def queries(own, other, weight):
    return pl.pallas_call(
        query_kernel,
        out_shape=jax.ShapeDtypeStruct((4 * own.shape[1], 128), BF),
        in_specs=[VMEM] * 3,
        out_specs=VMEM,
        compiler_params=pltpu.CompilerParams(vmem_limit_bytes=12 * MIB),
        cost_estimate=pl.CostEstimate(flops=10**9, bytes_accessed=10**7, transcendentals=0),
    )(own, other, weight)


def attend_kernel(
    meta, got_at, query_at, k_at, v_at, o_at, out, sibling,
    got, query, weight_k, weight_v, weight_o, rows, keys, values, context, sems,
):
    copies = [
        pltpu.make_async_copy(a, b, sems.at[i])
        for i, (a, b) in enumerate(
            [(got_at, got), (k_at, weight_k), (v_at, weight_v), (query_at, query), (o_at, weight_o)]
        )
    ]
    for copy in copies:
        copy.start()
    width = weight_k.shape[0]
    each = 1
    for n in got.shape[1:-1]:
        each *= n
    tall = 16 * each
    context[...] = jnp.zeros_like(context)
    tail = pl.ds(2 * each * BLOCK, (PARTS - 1) * BLOCK)
    keys[tail, :] = jnp.zeros(((PARTS - 1) * BLOCK, width), BF)
    values[tail, :] = jnp.zeros(((PARTS - 1) * BLOCK, width), BF)
    lead, lane = iota((tall, tall), 0), iota((tall, tall), 1)
    n = jnp.int32(each)
    turned = (lead == lax.rem(lane, n) * 16 + lax.div(lane, n)).astype(BF)
    low = iota((tall, 128), 1) < 64
    copies[0].wait()
    for part in range(2):
        rests = []
        for quarter in range(4):
            at = quarter * BLOCK + part * 16
            piece = mm(turned, got[at : at + 16].reshape(tall, width // 2))
            rests.append(piece[:, 512:640])
            piece = piece.astype(BF)
            for u in range(2 * each):
                to = u * BLOCK + part * 16
                side = (u % 2) * 256
                rows[to : to + 16, quarter * 256 : quarter * 256 + 256] = piece[
                    (u // 2) * 16 : (u // 2) * 16 + 16, side : side + 256
                ]
            if quarter % 2 == 1:
                left, right = rests[-2:]
                even = jnp.where(low, left, half_turn(right)).astype(BF)
                odd = jnp.where(low, half_turn(left), right).astype(BF)
                tile = 1024 + 128 * (quarter // 2)
                for u in range(2 * each):
                    to = u * BLOCK + part * 16
                    rows[to : to + 16, tile : tile + 128] = (odd if u % 2 else even)[
                        (u // 2) * 16 : (u // 2) * 16 + 16
                    ]
    copies[1].wait()
    copies[2].wait()

    def project(chunk, carry):
        at = pl.ds(pl.multiple_of(chunk * 256, 256), 256)
        block = rows[at, :]
        keys[at, :] = mm(block, weight_k[...]).astype(BF)
        values[at, :] = mm(block, weight_v[...]).astype(BF)
        return carry

    lax.fori_loop(0, 2 * each * BLOCK // 256, project, 0)
    copies[3].wait()

    def item(index, carry):
        start = pl.multiple_of(meta[index, 0] * BLOCK, BLOCK)
        length = meta[index, 1]
        whose = meta[index, 2]

        def with_keys(size):
            live = iota((size, 256), 0) < length
            span = pl.ds(start, size)
            for pair in range(width // 128):
                at = slice(pair * 128, (pair + 1) * 128)
                q = query[pl.ds(pl.multiple_of(whose * (2 * width) + pair * 256, 256), 256), :]
                scores = lax.dot_general(keys[span, at], q, ACROSS, preferred_element_type=F32)
                scores = jnp.where(live, scores, -1e30)
                weights = jnp.exp(scores - jnp.max(scores, axis=0, keepdims=True))
                scale = 1.0 / jnp.sum(weights, axis=0, keepdims=True)
                result = lax.dot_general(
                    values[span, at], weights.astype(BF), DOWN, preferred_element_type=F32
                )
                to = pl.multiple_of(whose * width + pair * 128, 128)
                context[pl.ds(to, 64), :] += result[:64, :128] * scale[:, :128]
                context[pl.ds(to + 64, 64), :] += result[64:, 128:] * scale[:, 128:]

        @pl.when(length <= 64)
        def _():
            with_keys(64)

        @pl.when(length > 64)
        def _():
            with_keys(128)

        return carry

    lax.fori_loop(0, meta[0, 3], item, 0)
    copies[4].wait()
    for who, to in enumerate((out, sibling)):
        part = context[who * width : (who + 1) * width, :].astype(BF)
        update = lax.dot_general(part, weight_o[...], DOWN, preferred_element_type=F32)
        update = jnp.where(iota(update.shape, 0) < meta[0, 4 + who], update, 0.0)
        to[...] = update.astype(to.dtype)


def attend(meta, got, query, weight_k, weight_v, weight_o):
    width = weight_k.shape[0]
    each = 1
    for n in got.shape[1:-1]:
        each *= n
    tall = 2 * each * BLOCK
    return pl.pallas_call(
        attend_kernel,
        out_shape=(
            jax.ShapeDtypeStruct((128, width), F32),
            jax.ShapeDtypeStruct((128, width), BF),
        ),
        in_specs=[SMEM] + [ANY] * 5,
        out_specs=(VMEM, VMEM),
        scratch_shapes=[
            pltpu.VMEM(got.shape, BF),
            pltpu.VMEM(query.shape, BF),
            pltpu.VMEM((width, width), BF),
            pltpu.VMEM((width, width), BF),
            pltpu.VMEM((width, width), BF),
            pltpu.VMEM((tall, width), BF),
            pltpu.VMEM((tall + (PARTS - 1) * BLOCK, width), BF),
            pltpu.VMEM((tall + (PARTS - 1) * BLOCK, width), BF),
            pltpu.VMEM((2 * width, 128), F32),
            pltpu.SemaphoreType.DMA((5,)),
        ],
        compiler_params=pltpu.CompilerParams(vmem_limit_bytes=36 * MIB),
        cost_estimate=pl.CostEstimate(flops=10**10, bytes_accessed=10**7, transcendentals=10**6),
    )(meta, got, query, weight_k, weight_v, weight_o)


def later_round(number, sides, me, count, meta):
    dest, source, length, amount, base, _, place, _ = sides
    origin = FIRST - PARTS + 1
    turn = jnp.where(base + amount <= FIRST, 0, 1 + (base - origin) // STEP)
    active = turn == number
    base = base - origin - (number - 1) * STEP
    spots = jnp.arange(LATER, dtype=jnp.int32)
    target = (dest[None, :] == jnp.arange(count, dtype=jnp.int32)[:, None]) & active[None, :]
    there = (base[:, None] <= spots) & (spots < (base + amount)[:, None])
    entries = [jnp.where(there, source[:, None] + 1, 0), jnp.where(there, spots - base[:, None], 0)]
    high, low = (mm(target.astype(BF), entry.astype(BF)).astype(jnp.int32) for entry in entries)
    unit = (4 * (high - 1) + low).reshape(-1, 2)
    columns = jnp.arange(4 * count, dtype=jnp.int32)
    unit_at = 2 * (columns % (2 * count)) + columns // (2 * count)
    selector = (unit[:, :, None] == unit_at).reshape(unit.shape[0], -1).astype(BF)
    held = active & (dest == me)
    order = jnp.cumsum(held.astype(jnp.int32)) - 1
    chosen = held[None, :] & (order[None, :] == spots[:, None])

    def listed(values):
        return jnp.sum(jnp.where(chosen, values[None, :], 0), axis=1)

    held_count = jnp.broadcast_to(jnp.sum(held.astype(jnp.int32)), (LATER,))
    columns = [listed(base), listed(length), listed((place + me) % 2), held_count]
    return selector, meta[:LATER].at[:, :4].set(jnp.stack(columns, axis=1))


def local(embeddings, weight_q, weight_k, weight_v, weight_o, pairs, lengths, holder):
    count = lax.axis_size("group") * lax.axis_size("dev")
    me = lax.axis_index("group") * lax.axis_size("dev") + lax.axis_index("dev")
    own = embeddings[0]
    mine = exchange(front(own))
    selector, meta, sides = plan(me, pairs, lengths, holder)
    query = queries(own, swap(own), weight_q)

    def one_round(selector, meta, outer):
        got = exchange(pick(selector, mine, outer))
        return attend(meta, got, query, weight_k, weight_v, weight_o)

    def another(carry):
        number, total = carry
        kept, given = one_round(*later_round(number, sides, me, count, meta), (LATER // 2,))
        return number + 1, total + kept + swap(given).astype(F32)

    kept, given = one_round(selector, meta, (FIRST // 8, 4))
    received = swap(given)
    _, kept = lax.while_loop(lambda c: c[0] <= meta[0, 6], another, (jnp.int32(1), kept))
    return (own.astype(F32) + (kept + received.astype(F32))).astype(BF)[None]


def solution(mesh):
    in_specs = (P(AXES, None, None), P(), P(), P(), P(), P(), P(), P())
    out_specs = P(AXES, None, None)
    return jax.shard_map(local, mesh=mesh, in_specs=in_specs, out_specs=out_specs, check_vma=False)
```

time: 198 us -> 85.2 us (0.43)
  local copies, waits for them, and re-layouts: 59.2 us -> 6.15 us
  matrix products: 38.8 us -> 0 us
  Pallas kernels: 0 us -> 26.6 us
  blocking collectives: 26.6 us -> 0 us
  other arithmetic: 13.4 us -> 2.01 us
  waiting for transfers between devices: 35.1 us -> 28.5 us
  starting transfers between devices: 23.1 us -> 20 us
    dot_general x10 -> x0, matrix products: 27.8 us -> none  [the longest x4 9.89 us: attend(): jnp.einsum('hij,jhd->ihd', weights, value, preferred_element_type=jnp.flo...]
    pallas_call x0 -> x5, Pallas kernels: none -> 26.6 us  [the longest x1 14.1 us: attend(): pl.pallas_call(attend_kernel, out_shape=(jax.ShapeDtypeStruct((128, width...]
    all_to_all x1 -> x0, blocking collectives: 26.6 us -> none  [exchange(): return lax.all_to_all(array, AXES, split_axis=0, concat_axis=0, tiled=True)]
    slice x16 -> x1, local copies, waits for them, and re-layouts: 27.6 us -> 1.38 us  [local(): meta[0, 6]]
    sub x4 -> x0, matrix products: 11 us -> none  [attend(): exponent = jnp.exp(scores - jnp.max(scores, axis=-1, keepdims=True))]
    reshape x5 -> x0, local copies, waits for them, and re-layouts: 7.75 us -> none  [the longest x1 3.5 us: local(): arrived = exchange(picked.reshape(count, SLOTS, width))]
    another operation x4 -> x1, local copies, waits for them, and re-layouts: 8.34 us -> 0.7 us  [local(): jnp.stack(contexts, axis=1)]
    all_to_all x3 -> x2, waiting for transfers between devices: 35.1 us -> 27.6 us  [exchange(): return lax.all_to_all(array, AXES, split_axis=0, concat_axis=0, tiled=True)]
  transfers between devices with their start and end apart: 3 -> 4, of which waited for: 3 -> 3; matrix products, arithmetic and copies ran while one was open for 5% -> 3% of each run, Pallas kernels for 0% -> 8%
where the time goes in v4:
time: 85.2 us; the launch traced here: 84.2 us
  waiting for transfers between devices  28.5 us (33%)
  Pallas kernels  26.6 us (31%)
  starting transfers between devices  20 us (23%)
  local copies, waits for them, and re-layouts  6.15 us (7%)
  other arithmetic  2.01 us (2%)
  loops' own time  0.88 us (1%)
    all_to_all x2, waiting for transfers between devices, exchange(): return lax.all_to_all(array, AXES, split_axis=0, concat_axis=0, tiled=True)  27.6 us
    all_to_all x2, starting transfers between devices, exchange(): return lax.all_to_all(array, AXES, split_axis=0, concat_axis=0, tiled=True)  17.6 us
    pallas_call x1, Pallas kernels, attend(): pl.pallas_call(attend_kernel, out_shape=(jax.ShapeDtypeStruct((128, width...  14.1 us
    pallas_call x1, Pallas kernels, pick(): pl.pallas_call(pick_kernel, out_shape=jax.ShapeDtypeStruct((devices,) + o...  4.74 us
    unnamed x13, local copies, waits for them, and re-layouts  4.07 us
    pallas_call x1, Pallas kernels, plan(): pl.pallas_call(plan_kernel, out_shape=(jax.ShapeDtypeStruct((devices * FI...  3.34 us
    pallas_call x1, Pallas kernels, queries(): pl.pallas_call(query_kernel, out_shape=jax.ShapeDtypeStruct((4 * own.shap...  3.21 us
    ppermute x2, starting transfers between devices, swap(): return lax.ppermute(array, 'dev', [(i, i ^ 1) for i in range(count)])  2.37 us
  transfers between devices with their start and end apart: 4, of which 3 were waited for; matrix products, arithmetic and copies ran while one was open for 3% of the time, Pallas kernels for 8%

profile of v4, /device:TPU:1, one launch (start us, length us, event | category | flops | bytes accessed | tf_op | source)
XLA Modules:
  0.0 84.2 jit_solution(9858280165036300125)
XLA Ops:
  0.0 0.0 copy-start.1
  0.0 1.0 %copy-done.1 = bf16[1,128,1280]{2,1,0:T(8,128)(2,1)S(1)} copy-done((bf16[1,128,1280]{2,1,0:T(8,128)(2,1)S(1)}, bf16[1,128,1280]{2,1,0:T(8,128)(2,1)}, u32[]{:S(2)}) %copy-start.1) | copy-done | bytes 327704
  1.0 1.2 %shard_map.83 = bf16[128,2,640]{2,1,0:T(2,128)(2,1)} custom-call(bf16[128,1280]{1,0:T(8,128)(2,1)S(1)} %bitcast.77), custom_call_target="tpu_custom_call" | custom-call | tf_op jit(solution)/shard_map/pallas_call | solution.py:66
  2.2 11.9 %all-to-all-start.1 = ((bf16[128,2,640]{2,1,0:T(2,128)(2,1)}), bf16[128,2,640]{2,1,0:T(2,128)(2,1)}, u32[]{:S(2)}, u32[]{:S(2)}) async-start(bf16[128,2,640]{2,1,0:T(2,128)(2,1)} %shard_map.83), calls=%async_computation.1 | async-start | bytes 655360 | tf_op jit(solution)/shard_map/all_to_all | solution.py:26
  14.1 0.8 copy.23.pairs
  14.9 0.0 copy-start.4
  14.9 0.6 copy-done.4
  15.6 0.0 copy-start.5
  15.6 0.7 copy-done.5
  16.2 3.3 %shard_map.82 = (bf16[1536,1024]{1,0:T(8,128)(2,1)S(1)}, s32[24,128]{1,0:T(8,128)}, s32[8,512]{1,0:T(8,128)S(1)}) custom-call(s32[1]{0:T(128)} %bitcast.14.place, s32[256,2]{1,0:T(8,128)S(1)} %copy.23.pairs, s32[1,128]{1,0:T(1,128)S(1)} %bitcast.79, s32[1,128]{1,0:T(1,128)S(1)} %bitcast.80), custom_call_target="tpu_custom_call" | custom-call | flops 1000000000 | bytes 1000000 | tf_op jit(solution)/shard_map/pallas_call | solution.py:151
  19.5 5.8 %all-to-all-done.1.mine = bf16[128,2,640]{2,1,0:T(2,128)(2,1)} async-done(((bf16[128,2,640]{2,1,0:T(2,128)(2,1)}), bf16[128,2,640]{2,1,0:T(2,128)(2,1)}, u32[]{:S(2)}, u32[]{:S(2)}) %all-to-all-start.1) | async-done | bytes 327712 | tf_op jit(solution)/shard_map/all_to_all | solution.py:26
  25.3 4.7 %shard_map.84 = bf16[128,3,4,640]{3,2,1,0:T(4,128)(2,1)} custom-call(bf16[1536,1024]{1,0:T(8,128)(2,1)S(1)} %get-tuple-element.235.selector, bf16[128,2,640]{2,1,0:T(2,128)(2,1)} %all-to-all-done.1.mine), custom_call_target="tpu_custom_call" | custom-call | flops 1000000000 | bytes 10000000 | tf_op jit(solution)/shard_map/pallas_call | solution.py:196
  30.1 0.0 copy-start
  30.1 5.7 %all-to-all-start.2 = ((bf16[128,3,4,640]{3,2,1,0:T(4,128)(2,1)}), bf16[128,3,4,640]{3,2,1,0:T(4,128)(2,1)}, u32[]{:S(2)}, u32[]{:S(2)}) async-start(bf16[128,3,4,640]{3,2,1,0:T(4,128)(2,1)} %shard_map.84), calls=%async_computation.2 | async-start | bytes 3932160 | tf_op jit(solution)/shard_map/all_to_all | solution.py:26
  35.8 1.4 %collective-permute-start.1 = (bf16[128,1280]{1,0:T(8,128)(2,1)}, bf16[128,1280]{1,0:T(8,128)(2,1)}, u32[]{:S(2)}, u32[]{:S(2)}) collective-permute-start(bf16[128,1280]{1,0:T(8,128)(2,1)} %bitcast.76), channel_id=1, source_target_pairs={{0,1},{1,0},{2,3},{3,2},{4,5},{5,4},{6,7},{7,6},{8,9},{9,8},{10,11... | collective-permute-start | bytes 983048 | tf_op jit(solution)/shard_map/ppermute | solution.py:31
  37.2 0.7 slice.49
  37.9 0.9 %collective-permute-done.1.other = bf16[128,1280]{1,0:T(8,128)(2,1)} collective-permute-done((bf16[128,1280]{1,0:T(8,128)(2,1)}, bf16[128,1280]{1,0:T(8,128)(2,1)}, u32[]{:S(2)}, u32[]{:S(2)}) %collective-permute-start.1) | collective-permute-done | bytes 327712 | tf_op jit(solution)/shard_map/ppermute | solution.py:31
  38.8 0.0 copy-done
  38.8 0.0 copy-start.2
  38.8 1.0 %copy-done.2 = bf16[1,128,1280]{2,1,0:T(8,128)(2,1)S(1)} copy-done((bf16[1,128,1280]{2,1,0:T(8,128)(2,1)S(1)}, bf16[1,128,1280]{2,1,0:T(8,128)(2,1)}, u32[]{:S(2)}) %copy-start.2) | copy-done | bytes 327704
  39.7 3.2 %shard_map.85.query_at = bf16[5120,128]{1,0:T(8,128)(2,1)} custom-call(bf16[128,1280]{1,0:T(8,128)(2,1)S(1)} %bitcast.78, bf16[128,1280]{1,0:T(8,128)(2,1)} %collective-permute-done.1.other, bf16[1280,1280]{1,0:T(8,128)(2,1)S(1)} %copy-done), custom_call_target="tpu_custom_call" | custom-call | flops 1000000000 | bytes 10000000 | tf_op jit(solution)/shard_map/pallas_call | solution.py:219
  42.9 21.8 %all-to-all-done.2.got_at = bf16[128,3,4,640]{3,2,1,0:T(4,128)(2,1)} async-done(((bf16[128,3,4,640]{3,2,1,0:T(4,128)(2,1)}), bf16[128,3,4,640]{3,2,1,0:T(4,128)(2,1)}, u32[]{:S(2)}, u32[]{:S(2)}) %all-to-all-start.2) | async-done | bytes 1966112 | tf_op jit(solution)/shard_map/all_to_all | solution.py:26
  64.8 14.1 %shard_map.86 = (f32[128,1280]{1,0:T(8,128)}, bf16[128,1280]{1,0:T(8,128)(2,1)S(1)}) custom-call(s32[24,128]{1,0:T(8,128)} %get-tuple-element.408.meta, bf16[128,3,4,640]{3,2,1,0:T(4,128)(2,1)} %all-to-all-done.2.got_at, bf16[5120,128]{1,0:T(8,128)(2,1)} %shard_map.85.query_at, bf16[1280,1280]{1,0:T(8,128)(2,1)} %k_at.1, bf16[1280,1280]{1,0:T(8,128)(2,1)} %v_at.1, ...), custom_call_target="tpu_custom_call" | custom-call | flops 10000000000 | bytes 10000000 | tf_op jit(solution)/shard_map/pallas_call | solution.py:338
  78.9 1.0 %collective-permute-start.2 = (bf16[128,1280]{1,0:T(8,128)(2,1)S(1)}, bf16[128,1280]{1,0:T(8,128)(2,1)}, u32[]{:S(2)}, u32[]{:S(2)}) collective-permute-start(bf16[128,1280]{1,0:T(8,128)(2,1)S(1)} %get-tuple-element.239), channel_id=1, source_target_pairs={{0,1},{1,0},{2,3},{3,2},{4,5},{5,4},{6,7},{7,6},{8,9},{9,8},{10,11... | collective-permute-start | bytes 983048 | tf_op jit(solution)/shard_map/ppermute | solution.py:31
  79.9 0.0 copy-start.3
  79.9 2.3 %while.14 = (s32[]{:T(128)}, f32[128,1280]{1,0:T(8,128)}, s32[24,128]{1,0:T(8,128)}, s32[1,512]{1,0:T(1,128)S(1)}, s32[8,512]{1,0:T(8,128)S(1)}, /*index=5*/s32[...) while((s32[]{:T(128)}, f32[128,1280]{1,0:T(8,128)}, ...), condition=%wide.region_8.9_spmd, body=%wide.region_0.8_spmd.sunk | while | flops 11007309824 | bytes 46608472 | solution.py:409
  79.9 1.4 %slice.51 = s32[1,1]{1,0:T(1,128)} slice(s32[24,128]{1,0:T(8,128)} %get-tuple-element.299), slice={[0:1], [6:7]} | slice | bytes 8 | tf_op jit(solution)/shard_map/while/cond/slice | solution.py:409
  82.2 0.0 collective-permute-done.2
  82.2 0.0 copy-done.3
  82.2 2.0 %fusion.39 = bf16[1,128,1280]{2,1,0:T(8,128)(2,1)} fusion(f32[128,1280]{1,0:T(8,128)} %get-tuple-element.238, bf16[128,1280]{1,0:T(8,128)(2,1)} %collective-permute-done.2, bf16[1,128,1280]{2,1,0:T(8,128)(2,1)S(1)} %copy-done.3), kind=kLoop, calls=%fused_computation.78 | loop fusion | flops 819200 | bytes 1638400 | tf_op jit(solution)/shard_map/broadcast_in_dim | solution.py:410
  (1 shorter events, 0.0 us)
Async XLA Ops:
  0.0 1.0 %copy-start.1 = (bf16[1,128,1280]{2,1,0:T(8,128)(2,1)S(1)}, bf16[1,128,1280]{2,1,0:T(8,128)(2,1)}, u32[]{:S(2)}) copy-start(bf16[1,128,1280]{2,1,0:T(8,128)(2,1)} %param.12) | copy-start | bytes 983044
  2.2 23.2 %all-to-all-start.1 = ((bf16[128,2,640]{2,1,0:T(2,128)(2,1)}), bf16[128,2,640]{2,1,0:T(2,128)(2,1)}, u32[]{:S(2)}, u32[]{:S(2)}) async-start(bf16[128,2,640]{2,1,0:T(2,128)(2,1)} %shard_map.83), calls=%async_computation.1 | async-start | bytes 655360 | tf_op jit(solution)/shard_map/all_to_all | solution.py:26
  14.9 0.7 copy-start.4
  15.6 0.7 copy-start.5
  30.1 8.7 %copy-start = (bf16[1280,1280]{1,0:T(8,128)(2,1)S(1)}, bf16[1280,1280]{1,0:T(8,128)(2,1)}, u32[]{:S(2)}) copy-start(bf16[1280,1280]{1,0:T(8,128)(2,1)} %weight.1) | copy-start | bytes 9830404
  30.1 34.7 %all-to-all-start.2 = ((bf16[128,3,4,640]{3,2,1,0:T(4,128)(2,1)}), bf16[128,3,4,640]{3,2,1,0:T(4,128)(2,1)}, u32[]{:S(2)}, u32[]{:S(2)}) async-start(bf16[128,3,4,640]{3,2,1,0:T(4,128)(2,1)} %shard_map.84), calls=%async_computation.2 | async-start | bytes 3932160 | tf_op jit(solution)/shard_map/all_to_all | solution.py:26
  35.8 2.9 %collective-permute-start.1 = (bf16[128,1280]{1,0:T(8,128)(2,1)}, bf16[128,1280]{1,0:T(8,128)(2,1)}, u32[]{:S(2)}, u32[]{:S(2)}) collective-permute-start(bf16[128,1280]{1,0:T(8,128)(2,1)} %bitcast.76), channel_id=1, source_target_pairs={{0,1},{1,0},{2,3},{3,2},{4,5},{5,4},{6,7},{7,6},{8,9},{9,8},{10,11... | collective-permute-start | bytes 983048 | tf_op jit(solution)/shard_map/ppermute | solution.py:31
  38.8 1.0 %copy-start.2 = (bf16[1,128,1280]{2,1,0:T(8,128)(2,1)S(1)}, bf16[1,128,1280]{2,1,0:T(8,128)(2,1)}, u32[]{:S(2)}) copy-start(bf16[1,128,1280]{2,1,0:T(8,128)(2,1)} %param.12) | copy-start | bytes 983044
  78.9 3.3 %collective-permute-start.2 = (bf16[128,1280]{1,0:T(8,128)(2,1)S(1)}, bf16[128,1280]{1,0:T(8,128)(2,1)}, u32[]{:S(2)}, u32[]{:S(2)}) collective-permute-start(bf16[128,1280]{1,0:T(8,128)(2,1)S(1)} %get-tuple-element.239), channel_id=1, source_target_pairs={{0,1},{1,0},{2,3},{3,2},{4,5},{5,4},{6,7},{7,6},{8,9},{9,8},{10,11... | collective-permute-start | bytes 983048 | tf_op jit(solution)/shard_map/ppermute | solution.py:31
  79.9 2.3 %copy-start.3 = (bf16[1,128,1280]{2,1,0:T(8,128)(2,1)S(1)}, bf16[1,128,1280]{2,1,0:T(8,128)(2,1)}, u32[]{:S(2)}) copy-start(bf16[1,128,1280]{2,1,0:T(8,128)(2,1)} %param.12) | copy-start | bytes 983044

commit v5 on v4

--- a/solution.py
+++ b/solution.py
@@ -142,6 +142,8 @@
     listed = jnp.where(lane == 1, column(length), column(base))
     listed = jnp.where(lane == 2, column((place_row + me) % 2), listed)
     listed = jnp.where(lane == 3, amount_held, listed)
+    blocks = jnp.max(jnp.where(held, base + amount, 0), axis=1, keepdims=True).astype(F32)
+    listed = jnp.where(lane == 7, blocks, listed)
     listed = jnp.where(lane == 4, ends[0], jnp.where(lane == 5, ends[1], listed))
     meta[...] = jnp.where(lane == 6, rounds.astype(F32), listed).astype(jnp.int32)
 
@@ -162,63 +164,65 @@
     )(me.reshape(1), pairs, lengths.reshape(1, -1), holder.reshape(1, -1))
 
 
-def pick_kernel(selector, mine, picked):
+def pick_kernel(selector, mine, picked, even, odd):
     rows, _, half = mine.shape
-    units = mine[...].reshape(2 * rows, half)
-    ends = units[:, 512:640].astype(F32)
-    turned = half_turn(ends)
-    low = iota(ends.shape, 1) < 64
-    nil = jnp.zeros_like(ends)
-    main = jnp.concatenate([units[:, 0:256], units[:, 256:512]], axis=0)
-    ends_low = jnp.concatenate([jnp.where(low, ends, nil), jnp.where(low, turned, nil)], axis=0)
-    ends_high = jnp.concatenate([jnp.where(low, nil, turned), jnp.where(low, nil, ends)], axis=0)
-    even = jnp.concatenate([main, ends_low.astype(BF)], axis=1)
-    odd = jnp.concatenate([main, ends_high.astype(BF)], axis=1)
-    outer = picked.shape[1:-1]
-    each = 1
-    for n in outer:
-        each *= n
-
-    def some(chunk, carry):
-        at = pl.ds(pl.multiple_of(chunk * (32 * each), 32 * each), 32 * each)
-        first = mm(selector[at, : 4 * rows], even)
-        second = mm(selector[at, 4 * rows :], odd)
-        rest = first[:, 256:] + second[:, 256:]
-        message = jnp.concatenate([first[:, :256], second[:, :256], rest], axis=1).astype(BF)
-        picked[pl.ds(chunk * 32, 32)] = message.reshape((32,) + outer + (half,))
-        return carry
-
-    lax.fori_loop(0, rows // 32, some, 0)
+
+    @pl.when(pl.program_id(0) == 0)
+    def _():
+        units = mine[...].reshape(2 * rows, half)
+        ends = units[:, 512:640].astype(F32)
+        turned = half_turn(ends)
+        low = iota(ends.shape, 1) < 64
+        nil = jnp.zeros_like(ends)
+        main = jnp.concatenate([units[:, 0:256], units[:, 256:512]], axis=0)
+        first = jnp.concatenate([jnp.where(low, ends, nil), jnp.where(low, turned, nil)], axis=0)
+        second = jnp.concatenate([jnp.where(low, nil, turned), jnp.where(low, nil, ends)], axis=0)
+        even[...] = jnp.concatenate([main, first.astype(BF)], axis=1)
+        odd[...] = jnp.concatenate([main, second.astype(BF)], axis=1)
+
+    first = mm(selector[:, : 4 * rows], even[...])
+    second = mm(selector[:, 4 * rows :], odd[...])
+    rest = first[:, 256:] + second[:, 256:]
+    message = jnp.concatenate([first[:, :256], second[:, :256], rest], axis=1).astype(BF)
+    picked[...] = message.reshape(picked.shape)
 
 
 def pick(selector, mine, outer):
     devices, _, half = mine.shape
+    rows, units = selector.shape
+    steps = 4
+    nought = (0,) * (len(outer) + 1)
     return pl.pallas_call(
         pick_kernel,
         out_shape=jax.ShapeDtypeStruct((devices,) + outer + (half,), BF),
-        in_specs=[VMEM] * 2,
-        out_specs=VMEM,
+        grid=(steps,),
+        in_specs=[
+            pl.BlockSpec((rows // steps, units), lambda i: (i, 0)),
+            pl.BlockSpec(mine.shape, lambda i: (0, 0, 0)),
+        ],
+        out_specs=pl.BlockSpec((devices // steps,) + outer + (half,), lambda i: (i,) + nought),
+        scratch_shapes=[pltpu.VMEM((4 * devices, 384), BF)] * 2,
         compiler_params=pltpu.CompilerParams(vmem_limit_bytes=16 * MIB),
         cost_estimate=pl.CostEstimate(flops=10**9, bytes_accessed=10**7, transcendentals=0),
     )(selector, mine)
 
 
 def query_kernel(own, other, weight, query):
-    first = iota((128, 128), 1) < HEAD_DIM
-    none = jnp.zeros((128, 128), BF)
+    first = iota((128, 128), 0) < HEAD_DIM
     for who, rows in enumerate((own, other)):
-        result = (mm(rows[...], weight[...]).astype(BF)) * BF(HEAD_DIM**-0.5)
-        for pair in range(result.shape[1] // 128):
-            at = (who * (result.shape[1] // 128) + pair) * 256
-            tile = result[:, pair * 128 : (pair + 1) * 128]
-            query[at : at + 128, :] = jnp.where(first, tile, none)
-            query[at + 128 : at + 256, :] = jnp.where(first, none, tile)
+        result = mm(rows[...], weight[...]).astype(BF).astype(F32) * HEAD_DIM**-0.5
+        width = result.shape[1]
+        for pair in range(width // 128):
+            at = slice(who * width + pair * 128, who * width + (pair + 1) * 128)
+            tile = jnp.transpose(result[:, pair * 128 : (pair + 1) * 128])
+            query[at, :128] = jnp.where(first, tile, 0.0).astype(BF)
+            query[at, 128:] = jnp.where(first, 0.0, tile).astype(BF)
 
 
 def queries(own, other, weight):
     return pl.pallas_call(
         query_kernel,
-        out_shape=jax.ShapeDtypeStruct((4 * own.shape[1], 128), BF),
+        out_shape=jax.ShapeDtypeStruct((2 * own.shape[1], 256), BF),
         in_specs=[VMEM] * 3,
         out_specs=VMEM,
         compiler_params=pltpu.CompilerParams(vmem_limit_bytes=12 * MIB),
@@ -228,7 +232,8 @@
 
 def attend_kernel(
     meta, got_at, query_at, k_at, v_at, o_at, out, sibling,
-    got, query, weight_k, weight_v, weight_o, rows, keys, values, context, sems,
+    got, query, weight_k, weight_v, weight_o, rows, keys, values,
+    context, scores, weights, scales, sems,
 ):
     copies = [
         pltpu.make_async_copy(a, b, sems.at[i])
@@ -236,7 +241,7 @@
             [(got_at, got), (k_at, weight_k), (v_at, weight_v), (query_at, query), (o_at, weight_o)]
         )
     ]
-    for copy in copies:
+    for copy in copies[:3]:
         copy.start()
     width = weight_k.shape[0]
     each = 1
@@ -244,14 +249,14 @@
         each *= n
     tall = 16 * each
     context[...] = jnp.zeros_like(context)
-    tail = pl.ds(2 * each * BLOCK, (PARTS - 1) * BLOCK)
-    keys[tail, :] = jnp.zeros(((PARTS - 1) * BLOCK, width), BF)
-    values[tail, :] = jnp.zeros(((PARTS - 1) * BLOCK, width), BF)
+    values[...] = jnp.zeros_like(values)
     lead, lane = iota((tall, tall), 0), iota((tall, tall), 1)
     n = jnp.int32(each)
     turned = (lead == lax.rem(lane, n) * 16 + lax.div(lane, n)).astype(BF)
     low = iota((tall, 128), 1) < 64
     copies[0].wait()
+    copies[3].start()
+    copies[4].start()
     for part in range(2):
         rests = []
         for quarter in range(4):
@@ -275,17 +280,20 @@
                     rows[to : to + 16, tile : tile + 128] = (odd if u % 2 else even)[
                         (u // 2) * 16 : (u // 2) * 16 + 16
                     ]
+    chunks = (meta[0, 7] + 7) // 8
+
+    def project(weight, to):
+        def some(chunk, carry):
+            at = pl.ds(pl.multiple_of(chunk * 256, 256), 256)
+            to[at, :] = mm(rows[at, :], weight[...]).astype(BF)
+            return carry
+
+        lax.fori_loop(0, chunks, some, 0)
+
     copies[1].wait()
+    project(weight_k, keys)
     copies[2].wait()
-
-    def project(chunk, carry):
-        at = pl.ds(pl.multiple_of(chunk * 256, 256), 256)
-        block = rows[at, :]
-        keys[at, :] = mm(block, weight_k[...]).astype(BF)
-        values[at, :] = mm(block, weight_v[...]).astype(BF)
-        return carry
-
-    lax.fori_loop(0, 2 * each * BLOCK // 256, project, 0)
+    project(weight_v, values)
     copies[3].wait()
 
     def item(index, carry):
@@ -296,16 +304,22 @@
         def with_keys(size):
             live = iota((size, 256), 0) < length
             span = pl.ds(start, size)
-            for pair in range(width // 128):
+            pairs = range(width // 128)
+            for pair in pairs:
                 at = slice(pair * 128, (pair + 1) * 128)
-                q = query[pl.ds(pl.multiple_of(whose * (2 * width) + pair * 256, 256), 256), :]
-                scores = lax.dot_general(keys[span, at], q, ACROSS, preferred_element_type=F32)
-                scores = jnp.where(live, scores, -1e30)
-                weights = jnp.exp(scores - jnp.max(scores, axis=0, keepdims=True))
-                scale = 1.0 / jnp.sum(weights, axis=0, keepdims=True)
-                result = lax.dot_general(
-                    values[span, at], weights.astype(BF), DOWN, preferred_element_type=F32
-                )
+                q = query[pl.ds(pl.multiple_of(whose * width + pair * 128, 128), 128), :]
+                scores[:size, pair * 256 : (pair + 1) * 256] = mm(keys[span, at], q)
+            for pair in pairs:
+                at = slice(pair * 256, (pair + 1) * 256)
+                score = jnp.where(live, scores[:size, at], -1e30)
+                power = jnp.exp(score - jnp.max(score, axis=0, keepdims=True))
+                weights[:size, at] = power.astype(BF)
+                scales[0:1, at] = 1.0 / jnp.sum(power, axis=0, keepdims=True)
+            for pair in pairs:
+                at = slice(pair * 256, (pair + 1) * 256)
+                v = values[span, pair * 128 : (pair + 1) * 128]
+                result = lax.dot_general(v, weights[:size, at], DOWN, preferred_element_type=F32)
+                scale = scales[0:1, at]
                 to = pl.multiple_of(whose * width + pair * 128, 128)
                 context[pl.ds(to, 64), :] += result[:64, :128] * scale[:, :128]
                 context[pl.ds(to + 64, 64), :] += result[64:, 128:] * scale[:, 128:]
@@ -353,6 +367,9 @@
             pltpu.VMEM((tall + (PARTS - 1) * BLOCK, width), BF),
             pltpu.VMEM((tall + (PARTS - 1) * BLOCK, width), BF),
             pltpu.VMEM((2 * width, 128), F32),
+            pltpu.VMEM((128, 2 * width), F32),
+            pltpu.VMEM((128, 2 * width), BF),
+            pltpu.VMEM((8, 2 * width), F32),
             pltpu.SemaphoreType.DMA((5,)),
         ],
         compiler_params=pltpu.CompilerParams(vmem_limit_bytes=36 * MIB),
@@ -384,7 +401,8 @@
 
     held_count = jnp.broadcast_to(jnp.sum(held.astype(jnp.int32)), (LATER,))
     columns = [listed(base), listed(length), listed((place + me) % 2), held_count]
-    return selector, meta[:LATER].at[:, :4].set(jnp.stack(columns, axis=1))
+    meta = meta[:LATER].at[:, :4].set(jnp.stack(columns, axis=1))
+    return selector, meta.at[:, 7].set(jnp.max(jnp.where(held, base + amount, 0)))
 
 
 def local(embeddings, weight_q, weight_k, weight_v, weight_o, pairs, lengths, holder):
@@ -393,6 +411,7 @@
     own = embeddings[0]
     mine = exchange(front(own))
     selector, meta, sides = plan(me, pairs, lengths, holder)
+    rounds = meta[0, 6]
     query = queries(own, swap(own), weight_q)
 
     def one_round(selector, meta, outer):
@@ -406,7 +425,7 @@
 
     kept, given = one_round(selector, meta, (FIRST // 8, 4))
     received = swap(given)
-    _, kept = lax.while_loop(lambda c: c[0] <= meta[0, 6], another, (jnp.int32(1), kept))
+    _, kept = lax.while_loop(lambda c: c[0] <= rounds, another, (jnp.int32(1), kept))
     return (own.astype(F32) + (kept + received.astype(F32))).astype(BF)[None]
 
 

time: 85.2 us -> 83.6 us (0.981); the launches traced: 84.2 us -> 84 us
  local copies, waits for them, and re-layouts: 6.15 us -> 4.66 us
  starting transfers between devices: 20 us -> 19 us
  waiting for transfers between devices: 28.5 us -> 29.5 us
    pallas_call x1, Pallas kernels: 14.1 us -> 15.6 us  [attend(): pl.pallas_call(attend_kernel, out_shape=(jax.ShapeDtypeStruct((128, width...]
    ppermute x2, starting transfers between devices: 2.37 us -> 1.44 us  [swap(): return lax.ppermute(array, 'dev', [(i, i ^ 1) for i in range(count)])]
  transfers between devices with their start and end apart: 4 -> 4, of which waited for: 3 -> 4; matrix products, arithmetic and copies ran while one was open for 3% -> 2% of each run, Pallas kernels for 8% -> 7%
where the time goes in v5:
time: 83.6 us; the launch traced here: 84 us
  waiting for transfers between devices  29.5 us (35%)
  Pallas kernels  27.3 us (33%)
  starting transfers between devices  19 us (23%)
  local copies, waits for them, and re-layouts  4.66 us (6%)
  other arithmetic  2.66 us (3%)
    all_to_all x2, waiting for transfers between devices, exchange(): return lax.all_to_all(array, AXES, split_axis=0, concat_axis=0, tiled=True)  28.2 us
    all_to_all x2, starting transfers between devices, exchange(): return lax.all_to_all(array, AXES, split_axis=0, concat_axis=0, tiled=True)  17.6 us
    pallas_call x1, Pallas kernels, attend(): pl.pallas_call(attend_kernel, out_shape=(jax.ShapeDtypeStruct((128, width...  15.6 us
    pallas_call x1, Pallas kernels, pick(): pl.pallas_call(pick_kernel, out_shape=jax.ShapeDtypeStruct((devices,) + o...  4.5 us
    unnamed x13, local copies, waits for them, and re-layouts  4.07 us
    pallas_call x1, Pallas kernels, queries(): pl.pallas_call(query_kernel, out_shape=jax.ShapeDtypeStruct((2 * own.shap...  3.22 us
    pallas_call x1, Pallas kernels, plan(): pl.pallas_call(plan_kernel, out_shape=(jax.ShapeDtypeStruct((devices * FI...  2.76 us
    broadcast_in_dim x1, other arithmetic, local(): return (own.astype(F32) + (kept + received.astype(F32))).astype(BF)[None]  2.01 us
  transfers between devices with their start and end apart: 4, of which 4 were waited for; matrix products, arithmetic and copies ran while one was open for 2% of the time, Pallas kernels for 7%

profile of v5, /device:TPU:1, one launch (start us, length us, event | category | flops | bytes accessed | tf_op | source)
XLA Modules:
  0.0 84.0 jit_solution(12861792728776599831)
XLA Ops:
  0.0 0.0 copy-start.1
  0.0 1.0 %copy-done.1 = bf16[1,128,1280]{2,1,0:T(8,128)(2,1)S(1)} copy-done((bf16[1,128,1280]{2,1,0:T(8,128)(2,1)S(1)}, bf16[1,128,1280]{2,1,0:T(8,128)(2,1)}, u32[]{:S(2)}) %copy-start.1) | copy-done | bytes 327704
  1.0 1.2 %shard_map.83 = bf16[128,2,640]{2,1,0:T(2,128)(2,1)} custom-call(bf16[128,1280]{1,0:T(8,128)(2,1)S(1)} %bitcast.76), custom_call_target="tpu_custom_call" | custom-call | tf_op jit(solution)/shard_map/pallas_call | solution.py:66
  2.2 11.9 %all-to-all-start.1 = ((bf16[128,2,640]{2,1,0:T(2,128)(2,1)}), bf16[128,2,640]{2,1,0:T(2,128)(2,1)}, u32[]{:S(2)}, u32[]{:S(2)}) async-start(bf16[128,2,640]{2,1,0:T(2,128)(2,1)} %shard_map.83), calls=%async_computation.1 | async-start | bytes 655360 | tf_op jit(solution)/shard_map/all_to_all | solution.py:26
  14.1 0.8 copy.23.pairs
  14.9 0.0 copy-start.4
  14.9 0.6 copy-done.4
  15.6 0.0 copy-start.5
  15.6 0.7 copy-done.5
  16.2 2.8 %shard_map.82 = (bf16[1536,1024]{1,0:T(8,128)(2,1)S(1)}, s32[24,128]{1,0:T(8,128)S(1)}, s32[8,512]{1,0:T(8,128)S(1)}) custom-call(s32[1]{0:T(128)} %bitcast.13.place, s32[256,2]{1,0:T(8,128)S(1)} %copy.23.pairs, s32[1,128]{1,0:T(1,128)S(1)} %bitcast.78, s32[1,128]{1,0:T(1,128)S(1)} %bitcast.79), custom_call_target="tpu_custom_call" | custom-call | flops 1000000000 | bytes 1000000 | tf_op jit(solution)/shard_map/pallas_call | solution.py:153
  19.0 6.4 %all-to-all-done.1.mine = bf16[128,2,640]{2,1,0:T(2,128)(2,1)} async-done(((bf16[128,2,640]{2,1,0:T(2,128)(2,1)}), bf16[128,2,640]{2,1,0:T(2,128)(2,1)}, u32[]{:S(2)}, u32[]{:S(2)}) %all-to-all-start.1) | async-done | bytes 327712 | tf_op jit(solution)/shard_map/all_to_all | solution.py:26
  25.3 4.5 %shard_map.84 = bf16[128,3,4,640]{3,2,1,0:T(4,128)(2,1)} custom-call(bf16[1536,1024]{1,0:T(8,128)(2,1)S(1)} %get-tuple-element.365.selector, bf16[128,2,640]{2,1,0:T(2,128)(2,1)} %all-to-all-done.1.mine), custom_call_target="tpu_custom_call" | custom-call | flops 1000000000 | bytes 10000000 | tf_op jit(solution)/shard_map/pallas_call | solution.py:195
  29.9 0.0 copy-start
  29.9 5.7 %all-to-all-start.2 = ((bf16[128,3,4,640]{3,2,1,0:T(4,128)(2,1)}), bf16[128,3,4,640]{3,2,1,0:T(4,128)(2,1)}, u32[]{:S(2)}, u32[]{:S(2)}) async-start(bf16[128,3,4,640]{3,2,1,0:T(4,128)(2,1)} %shard_map.84), calls=%async_computation.2 | async-start | bytes 3932160 | tf_op jit(solution)/shard_map/all_to_all | solution.py:26
  35.6 1.4 %collective-permute-start.1 = (bf16[128,1280]{1,0:T(8,128)(2,1)}, bf16[128,1280]{1,0:T(8,128)(2,1)}, u32[]{:S(2)}, u32[]{:S(2)}) collective-permute-start(bf16[128,1280]{1,0:T(8,128)(2,1)} %bitcast.75), channel_id=1, source_target_pairs={{0,1},{1,0},{2,3},{3,2},{4,5},{5,4},{6,7},{7,6},{8,9},{9,8},{10,11... | collective-permute-start | bytes 983048 | tf_op jit(solution)/shard_map/ppermute | solution.py:31
  36.9 0.6 slice.70
  37.5 0.6 and_reduce_fusion.1
  38.2 0.4 collective-permute-done.1.other
  38.5 0.0 copy-done
  38.5 0.0 copy-start.2
  38.5 1.0 %copy-done.2 = bf16[1,128,1280]{2,1,0:T(8,128)(2,1)S(1)} copy-done((bf16[1,128,1280]{2,1,0:T(8,128)(2,1)S(1)}, bf16[1,128,1280]{2,1,0:T(8,128)(2,1)}, u32[]{:S(2)}) %copy-start.2) | copy-done | bytes 327704
  39.5 3.2 %shard_map.85.query_at = bf16[2560,256]{1,0:T(8,128)(2,1)} custom-call(bf16[128,1280]{1,0:T(8,128)(2,1)S(1)} %bitcast.77, bf16[128,1280]{1,0:T(8,128)(2,1)} %collective-permute-done.1.other, bf16[1280,1280]{1,0:T(8,128)(2,1)S(1)} %copy-done), custom_call_target="tpu_custom_call" | custom-call | flops 1000000000 | bytes 10000000 | tf_op jit(solution)/shard_map/pallas_call | solution.py:223
  42.7 21.8 %all-to-all-done.2.got_at = bf16[128,3,4,640]{3,2,1,0:T(4,128)(2,1)} async-done(((bf16[128,3,4,640]{3,2,1,0:T(4,128)(2,1)}), bf16[128,3,4,640]{3,2,1,0:T(4,128)(2,1)}, u32[]{:S(2)}, u32[]{:S(2)}) %all-to-all-start.2) | async-done | bytes 1966112 | tf_op jit(solution)/shard_map/all_to_all | solution.py:26
  64.5 15.6 %shard_map.86 = (f32[128,1280]{1,0:T(8,128)}, bf16[128,1280]{1,0:T(8,128)(2,1)S(1)}) custom-call(s32[24,128]{1,0:T(8,128)S(1)} %get-tuple-element.564.meta, bf16[128,3,4,640]{3,2,1,0:T(4,128)(2,1)} %all-to-all-done.2.got_at, bf16[2560,256]{1,0:T(8,128)(2,1)} %shard_map.85.query_at, bf16[1280,1280]{1,0:T(8,128)(2,1)} %k_at.1, bf16[1280,1280]{1,0:T(8,128)(2,1)} %v_at.1, ...), custom_call_target="tpu_custom_call" | custom-call | flops 10000000000 | bytes 10000000 | tf_op jit(solution)/shard_map/pallas_call | solution.py:352
  80.2 0.1 collective-permute-start.2
  80.3 0.0 copy-start.3
  80.3 0.8 while.16
  81.1 0.9 %collective-permute-done.2 = bf16[128,1280]{1,0:T(8,128)(2,1)} collective-permute-done((bf16[128,1280]{1,0:T(8,128)(2,1)S(1)}, bf16[128,1280]{1,0:T(8,128)(2,1)}, u32[]{:S(2)}, u32[]{:S(2)}) %collective-permute-start.2) | collective-permute-done | bytes 327712 | tf_op jit(solution)/shard_map/ppermute | solution.py:31
  82.0 0.0 copy-done.3
  82.0 2.0 %fusion.39 = bf16[1,128,1280]{2,1,0:T(8,128)(2,1)} fusion(f32[128,1280]{1,0:T(8,128)} %get-tuple-element.368, bf16[128,1280]{1,0:T(8,128)(2,1)} %collective-permute-done.2, bf16[1,128,1280]{2,1,0:T(8,128)(2,1)S(1)} %copy-done.3), kind=kLoop, calls=%fused_computation.81 | loop fusion | flops 819200 | bytes 1638400 | tf_op jit(solution)/shard_map/broadcast_in_dim | solution.py:429
  (2 shorter events, 0.0 us)
Async XLA Ops:
  0.0 1.0 %copy-start.1 = (bf16[1,128,1280]{2,1,0:T(8,128)(2,1)S(1)}, bf16[1,128,1280]{2,1,0:T(8,128)(2,1)}, u32[]{:S(2)}) copy-start(bf16[1,128,1280]{2,1,0:T(8,128)(2,1)} %param.14) | copy-start | bytes 983044
  2.2 23.2 %all-to-all-start.1 = ((bf16[128,2,640]{2,1,0:T(2,128)(2,1)}), bf16[128,2,640]{2,1,0:T(2,128)(2,1)}, u32[]{:S(2)}, u32[]{:S(2)}) async-start(bf16[128,2,640]{2,1,0:T(2,128)(2,1)} %shard_map.83), calls=%async_computation.1 | async-start | bytes 655360 | tf_op jit(solution)/shard_map/all_to_all | solution.py:26
  14.9 0.7 copy-start.4
  15.6 0.7 copy-start.5
  29.9 8.7 %copy-start = (bf16[1280,1280]{1,0:T(8,128)(2,1)S(1)}, bf16[1280,1280]{1,0:T(8,128)(2,1)}, u32[]{:S(2)}) copy-start(bf16[1280,1280]{1,0:T(8,128)(2,1)} %weight.1) | copy-start | bytes 9830404
  29.9 34.7 %all-to-all-start.2 = ((bf16[128,3,4,640]{3,2,1,0:T(4,128)(2,1)}), bf16[128,3,4,640]{3,2,1,0:T(4,128)(2,1)}, u32[]{:S(2)}, u32[]{:S(2)}) async-start(bf16[128,3,4,640]{3,2,1,0:T(4,128)(2,1)} %shard_map.84), calls=%async_computation.2 | async-start | bytes 3932160 | tf_op jit(solution)/shard_map/all_to_all | solution.py:26
  35.6 2.9 %collective-permute-start.1 = (bf16[128,1280]{1,0:T(8,128)(2,1)}, bf16[128,1280]{1,0:T(8,128)(2,1)}, u32[]{:S(2)}, u32[]{:S(2)}) collective-permute-start(bf16[128,1280]{1,0:T(8,128)(2,1)} %bitcast.75), channel_id=1, source_target_pairs={{0,1},{1,0},{2,3},{3,2},{4,5},{5,4},{6,7},{7,6},{8,9},{9,8},{10,11... | collective-permute-start | bytes 983048 | tf_op jit(solution)/shard_map/ppermute | solution.py:31
  38.5 1.0 %copy-start.2 = (bf16[1,128,1280]{2,1,0:T(8,128)(2,1)S(1)}, bf16[1,128,1280]{2,1,0:T(8,128)(2,1)}, u32[]{:S(2)}) copy-start(bf16[1,128,1280]{2,1,0:T(8,128)(2,1)} %param.14) | copy-start | bytes 983044
  80.2 1.8 %collective-permute-start.2 = (bf16[128,1280]{1,0:T(8,128)(2,1)S(1)}, bf16[128,1280]{1,0:T(8,128)(2,1)}, u32[]{:S(2)}, u32[]{:S(2)}) collective-permute-start(bf16[128,1280]{1,0:T(8,128)(2,1)S(1)} %get-tuple-element.369), channel_id=1, source_target_pairs={{0,1},{1,0},{2,3},{3,2},{4,5},{5,4},{6,7},{7,6},{8,9},{9,8},{10,11... | collective-permute-start | bytes 983048 | tf_op jit(solution)/shard_map/ppermute | solution.py:31
  80.3 1.7 %copy-start.3 = (bf16[1,128,1280]{2,1,0:T(8,128)(2,1)S(1)}, bf16[1,128,1280]{2,1,0:T(8,128)(2,1)}, u32[]{:S(2)}) copy-start(bf16[1,128,1280]{2,1,0:T(8,128)(2,1)} %param.14) | copy-start | bytes 983044

commit v6 on v5

--- a/solution.py
+++ b/solution.py
@@ -93,12 +93,11 @@
     amount = (length + (BLOCK - 1)) // BLOCK
     amount_col = ((length_col.astype(jnp.int32) + (BLOCK - 1)) // BLOCK).astype(F32)
     chip = place_row // 2
-    earlier = iota((total, total), 0) < iota((total, total), 1)
+    tied = (amount_col == amount.astype(F32)) & (iota((total, total), 0) < iota((total, total), 1))
+    earlier = (amount_col > amount.astype(F32)) | tied
     same = place_col.astype(jnp.int32) // 2 == chip
-    before = jnp.sum(jnp.where(same & earlier, amount_col, 0.0), axis=0, keepdims=True)
-    whole = jnp.sum(jnp.where(same, amount_col, 0.0), axis=0, keepdims=True)
-    second = 2.0 * before + amount.astype(F32) > whole
-    dest = 2 * chip + second.astype(jnp.int32)
+    before = jnp.sum(jnp.where(same & earlier, 1.0, 0.0), axis=0, keepdims=True).astype(jnp.int32)
+    dest = 2 * chip + ((before + 1) // 2) % 2
     dest_col = jnp.transpose(jnp.broadcast_to(dest.astype(F32), (devices, total)))[:, 0:1]
     alike = (dest_col.astype(jnp.int32) == dest) & earlier
     base = jnp.sum(jnp.where(alike, amount_col, 0.0), axis=0, keepdims=True).astype(jnp.int32)
@@ -190,7 +189,7 @@
 def pick(selector, mine, outer):
     devices, _, half = mine.shape
     rows, units = selector.shape
-    steps = 4
+    steps = 2
     nought = (0,) * (len(outer) + 1)
     return pl.pallas_call(
         pick_kernel,
@@ -296,47 +295,74 @@
     project(weight_v, values)
     copies[3].wait()
 
-    def item(index, carry):
-        start = pl.multiple_of(meta[index, 0] * BLOCK, BLOCK)
-        length = meta[index, 1]
-        whose = meta[index, 2]
-
-        def with_keys(size):
-            live = iota((size, 256), 0) < length
-            span = pl.ds(start, size)
-            pairs = range(width // 128)
-            for pair in pairs:
+    def two_sides(index, carry):
+        sides = [2 * index, 2 * index + 1]
+        starts = [pl.multiple_of(meta[i, 0] * BLOCK, BLOCK) for i in sides]
+        lengths = [meta[i, 1] for i in sides]
+        whose = [meta[i, 2] for i in sides]
+        pairs = range(width // 128)
+
+        def with_keys(*sizes):
+            positions = [iota((size, 256), 0) for size in sizes]
+
+            def score(side, pair):
                 at = slice(pair * 128, (pair + 1) * 128)
-                q = query[pl.ds(pl.multiple_of(whose * width + pair * 128, 128), 128), :]
-                scores[:size, pair * 256 : (pair + 1) * 256] = mm(keys[span, at], q)
-            for pair in pairs:
+                first = pl.multiple_of(whose[side] * width + pair * 128, 128)
+                size = sizes[side]
+                result = mm(keys[pl.ds(starts[side], size), at], query[pl.ds(first, 128), :])
+                scores[side, :size, pair * 256 : (pair + 1) * 256] = result
+
+            def soften(side, pair):
                 at = slice(pair * 256, (pair + 1) * 256)
-                score = jnp.where(live, scores[:size, at], -1e30)
+                size = sizes[side]
+                live = positions[side] < lengths[side]
+                score = jnp.where(live, scores[side, :size, at], -1e30)
                 power = jnp.exp(score - jnp.max(score, axis=0, keepdims=True))
-                weights[:size, at] = power.astype(BF)
-                scales[0:1, at] = 1.0 / jnp.sum(power, axis=0, keepdims=True)
-            for pair in pairs:
+                weights[side, :size, at] = power.astype(BF)
+                scale = 1.0 / jnp.sum(power, axis=0, keepdims=True)
+                scales[side, 0:1, at] = jnp.where(lengths[side] > 0, scale, 0.0)
+
+            def gather(side, pair):
                 at = slice(pair * 256, (pair + 1) * 256)
-                v = values[span, pair * 128 : (pair + 1) * 128]
-                result = lax.dot_general(v, weights[:size, at], DOWN, preferred_element_type=F32)
-                scale = scales[0:1, at]
-                to = pl.multiple_of(whose * width + pair * 128, 128)
+                size = sizes[side]
+                v = values[pl.ds(starts[side], size), pair * 128 : (pair + 1) * 128]
+                w = weights[side, :size, at]
+                result = lax.dot_general(v, w, DOWN, preferred_element_type=F32)
+                scale = scales[side, 0:1, at]
+                to = pl.multiple_of(whose[side] * width + pair * 128, 128)
                 context[pl.ds(to, 64), :] += result[:64, :128] * scale[:, :128]
                 context[pl.ds(to + 64, 64), :] += result[64:, 128:] * scale[:, 128:]
 
-        @pl.when(length <= 64)
+            for pair in pairs:
+                score(0, pair)
+            for pair in pairs:
+                score(1, pair)
+                soften(0, pair)
+            for pair in pairs:
+                soften(1, pair)
+                gather(0, pair)
+            for pair in pairs:
+                gather(1, pair)
+
+        longer = [length > 64 for length in lengths]
+
+        @pl.when(longer[1])
         def _():
-            with_keys(64)
-
-        @pl.when(length > 64)
+            with_keys(128, 128)
+
+        @pl.when(jnp.logical_and(longer[0], jnp.logical_not(longer[1])))
         def _():
-            with_keys(128)
+            with_keys(128, 64)
+
+        @pl.when(jnp.logical_not(jnp.logical_or(longer[0], longer[1])))
+        def _():
+            with_keys(64, 64)
 
         return carry
 
-    lax.fori_loop(0, meta[0, 3], item, 0)
+    lax.fori_loop(0, (meta[0, 3] + 1) // 2, two_sides, 0)
     copies[4].wait()
-    for who, to in enumerate((out, sibling)):
+    for who, to in ((1, sibling), (0, out)):
         part = context[who * width : (who + 1) * width, :].astype(BF)
         update = lax.dot_general(part, weight_o[...], DOWN, preferred_element_type=F32)
         update = jnp.where(iota(update.shape, 0) < meta[0, 4 + who], update, 0.0)
@@ -367,9 +393,9 @@
             pltpu.VMEM((tall + (PARTS - 1) * BLOCK, width), BF),
             pltpu.VMEM((tall + (PARTS - 1) * BLOCK, width), BF),
             pltpu.VMEM((2 * width, 128), F32),
-            pltpu.VMEM((128, 2 * width), F32),
-            pltpu.VMEM((128, 2 * width), BF),
-            pltpu.VMEM((8, 2 * width), F32),
+            pltpu.VMEM((2, 128, 2 * width), F32),
+            pltpu.VMEM((2, 128, 2 * width), BF),
+            pltpu.VMEM((2, 8, 2 * width), F32),
             pltpu.SemaphoreType.DMA((5,)),
         ],
         compiler_params=pltpu.CompilerParams(vmem_limit_bytes=36 * MIB),
@@ -393,7 +419,7 @@
     unit_at = 2 * (columns % (2 * count)) + columns // (2 * count)
     selector = (unit[:, :, None] == unit_at).reshape(unit.shape[0], -1).astype(BF)
     held = active & (dest == me)
-    order = jnp.cumsum(held.astype(jnp.int32)) - 1
+    order = jnp.sum(held[:, None] & (base[:, None] < base[None, :]), axis=0)
     chosen = held[None, :] & (order[None, :] == spots[:, None])
 
     def listed(values):

time: 83.6 us -> 83.7 us (level)
  starting transfers between devices: 19 us -> 19.9 us
    ppermute x2, starting transfers between devices: 1.44 us -> 2.33 us  [swap(): return lax.ppermute(array, 'dev', [(i, i ^ 1) for i in range(count)])]
where the time goes in v6:
time: 83.7 us; the launch traced here: 84.7 us
  waiting for transfers between devices  29 us (35%)
  Pallas kernels  27.7 us (33%)
  starting transfers between devices  19.9 us (24%)
  local copies, waits for them, and re-layouts  4.66 us (6%)
  other arithmetic  2.66 us (3%)
    all_to_all x2, waiting for transfers between devices, exchange(): return lax.all_to_all(array, AXES, split_axis=0, concat_axis=0, tiled=True)  27.9 us
    all_to_all x2, starting transfers between devices, exchange(): return lax.all_to_all(array, AXES, split_axis=0, concat_axis=0, tiled=True)  17.6 us
    pallas_call x1, Pallas kernels, attend(): pl.pallas_call(attend_kernel, out_shape=(jax.ShapeDtypeStruct((128, width...  16.2 us
    pallas_call x1, Pallas kernels, pick(): pl.pallas_call(pick_kernel, out_shape=jax.ShapeDtypeStruct((devices,) + o...  4.08 us
    unnamed x13, local copies, waits for them, and re-layouts  4.07 us
    pallas_call x1, Pallas kernels, queries(): pl.pallas_call(query_kernel, out_shape=jax.ShapeDtypeStruct((2 * own.shap...  3.21 us
    pallas_call x1, Pallas kernels, plan(): pl.pallas_call(plan_kernel, out_shape=(jax.ShapeDtypeStruct((devices * FI...  3.08 us
    ppermute x2, starting transfers between devices, swap(): return lax.ppermute(array, 'dev', [(i, i ^ 1) for i in range(count)])  2.33 us
  transfers between devices with their start and end apart: 4, of which 4 were waited for; matrix products, arithmetic and copies ran while one was open for 2% of the time, Pallas kernels for 7%

profile of v6, /device:TPU:1, one launch (start us, length us, event | category | flops | bytes accessed | tf_op | source)
XLA Modules:
  0.0 84.7 jit_solution(9862730172177781553)
XLA Ops:
  0.0 0.0 copy-start.1
  0.0 1.0 %copy-done.1 = bf16[1,128,1280]{2,1,0:T(8,128)(2,1)S(1)} copy-done((bf16[1,128,1280]{2,1,0:T(8,128)(2,1)S(1)}, bf16[1,128,1280]{2,1,0:T(8,128)(2,1)}, u32[]{:S(2)}) %copy-start.1) | copy-done | bytes 327704
  1.0 1.2 %shard_map.83 = bf16[128,2,640]{2,1,0:T(2,128)(2,1)} custom-call(bf16[128,1280]{1,0:T(8,128)(2,1)S(1)} %bitcast.58), custom_call_target="tpu_custom_call" | custom-call | tf_op jit(solution)/shard_map/pallas_call | solution.py:66
  2.2 11.9 %all-to-all-start.1 = ((bf16[128,2,640]{2,1,0:T(2,128)(2,1)}), bf16[128,2,640]{2,1,0:T(2,128)(2,1)}, u32[]{:S(2)}, u32[]{:S(2)}) async-start(bf16[128,2,640]{2,1,0:T(2,128)(2,1)} %shard_map.83), calls=%async_computation.1 | async-start | bytes 655360 | tf_op jit(solution)/shard_map/all_to_all | solution.py:26
  14.1 0.8 copy.23.pairs
  14.9 0.0 copy-start.4
  14.9 0.6 copy-done.4
  15.6 0.0 copy-start.5
  15.6 0.7 copy-done.5
  16.2 3.1 %shard_map.82 = (bf16[1536,1024]{1,0:T(8,128)(2,1)S(1)}, s32[24,128]{1,0:T(8,128)S(1)}, s32[8,512]{1,0:T(8,128)S(1)}) custom-call(s32[1]{0:T(128)} %bitcast.11.place, s32[256,2]{1,0:T(8,128)S(1)} %copy.23.pairs, s32[1,128]{1,0:T(1,128)S(1)} %bitcast.60, s32[1,128]{1,0:T(1,128)S(1)} %bitcast.61), custom_call_target="tpu_custom_call" | custom-call | flops 1000000000 | bytes 1000000 | tf_op jit(solution)/shard_map/pallas_call | solution.py:152
  19.3 6.0 %all-to-all-done.1.mine = bf16[128,2,640]{2,1,0:T(2,128)(2,1)} async-done(((bf16[128,2,640]{2,1,0:T(2,128)(2,1)}), bf16[128,2,640]{2,1,0:T(2,128)(2,1)}, u32[]{:S(2)}, u32[]{:S(2)}) %all-to-all-start.1) | async-done | bytes 327712 | tf_op jit(solution)/shard_map/all_to_all | solution.py:26
  25.3 4.1 %shard_map.84 = bf16[128,3,4,640]{3,2,1,0:T(4,128)(2,1)} custom-call(bf16[1536,1024]{1,0:T(8,128)(2,1)S(1)} %get-tuple-element.364.selector, bf16[128,2,640]{2,1,0:T(2,128)(2,1)} %all-to-all-done.1.mine), custom_call_target="tpu_custom_call" | custom-call | flops 1000000000 | bytes 10000000 | tf_op jit(solution)/shard_map/pallas_call | solution.py:194
  29.4 0.0 copy-start
  29.4 5.7 %all-to-all-start.2 = ((bf16[128,3,4,640]{3,2,1,0:T(4,128)(2,1)}), bf16[128,3,4,640]{3,2,1,0:T(4,128)(2,1)}, u32[]{:S(2)}, u32[]{:S(2)}) async-start(bf16[128,3,4,640]{3,2,1,0:T(4,128)(2,1)} %shard_map.84), calls=%async_computation.2 | async-start | bytes 3932160 | tf_op jit(solution)/shard_map/all_to_all | solution.py:26
  35.1 1.4 %collective-permute-start.1 = (bf16[128,1280]{1,0:T(8,128)(2,1)}, bf16[128,1280]{1,0:T(8,128)(2,1)}, u32[]{:S(2)}, u32[]{:S(2)}) collective-permute-start(bf16[128,1280]{1,0:T(8,128)(2,1)} %bitcast.57), channel_id=1, source_target_pairs={{0,1},{1,0},{2,3},{3,2},{4,5},{5,4},{6,7},{7,6},{8,9},{9,8},{10,11... | collective-permute-start | bytes 983048 | tf_op jit(solution)/shard_map/ppermute | solution.py:31
  36.5 0.6 slice.53
  37.1 0.6 and_reduce_fusion.1
  37.7 0.3 collective-permute-done.1.other
  38.1 0.0 copy-done
  38.1 0.0 copy-start.2
  38.1 1.0 %copy-done.2 = bf16[1,128,1280]{2,1,0:T(8,128)(2,1)S(1)} copy-done((bf16[1,128,1280]{2,1,0:T(8,128)(2,1)S(1)}, bf16[1,128,1280]{2,1,0:T(8,128)(2,1)}, u32[]{:S(2)}) %copy-start.2) | copy-done | bytes 327704
  39.1 3.2 %shard_map.85.query_at = bf16[2560,256]{1,0:T(8,128)(2,1)} custom-call(bf16[128,1280]{1,0:T(8,128)(2,1)S(1)} %bitcast.59, bf16[128,1280]{1,0:T(8,128)(2,1)} %collective-permute-done.1.other, bf16[1280,1280]{1,0:T(8,128)(2,1)S(1)} %copy-done), custom_call_target="tpu_custom_call" | custom-call | flops 1000000000 | bytes 10000000 | tf_op jit(solution)/shard_map/pallas_call | solution.py:222
  42.3 21.8 %all-to-all-done.2.got_at = bf16[128,3,4,640]{3,2,1,0:T(4,128)(2,1)} async-done(((bf16[128,3,4,640]{3,2,1,0:T(4,128)(2,1)}), bf16[128,3,4,640]{3,2,1,0:T(4,128)(2,1)}, u32[]{:S(2)}, u32[]{:S(2)}) %all-to-all-start.2) | async-done | bytes 1966112 | tf_op jit(solution)/shard_map/all_to_all | solution.py:26
  64.1 16.2 %shard_map.86 = (f32[128,1280]{1,0:T(8,128)}, bf16[128,1280]{1,0:T(8,128)(2,1)S(1)}) custom-call(s32[24,128]{1,0:T(8,128)S(1)} %get-tuple-element.563.meta, bf16[128,3,4,640]{3,2,1,0:T(4,128)(2,1)} %all-to-all-done.2.got_at, bf16[2560,256]{1,0:T(8,128)(2,1)} %shard_map.85.query_at, bf16[1280,1280]{1,0:T(8,128)(2,1)} %k_at.1, bf16[1280,1280]{1,0:T(8,128)(2,1)} %v_at.1, ...), custom_call_target="tpu_custom_call" | custom-call | flops 10000000000 | bytes 10000000 | tf_op jit(solution)/shard_map/pallas_call | solution.py:378
  80.3 1.0 %collective-permute-start.2 = (bf16[128,1280]{1,0:T(8,128)(2,1)S(1)}, bf16[128,1280]{1,0:T(8,128)(2,1)}, u32[]{:S(2)}, u32[]{:S(2)}) collective-permute-start(bf16[128,1280]{1,0:T(8,128)(2,1)S(1)} %get-tuple-element.368), channel_id=1, source_target_pairs={{0,1},{1,0},{2,3},{3,2},{4,5},{5,4},{6,7},{7,6},{8,9},{9,8},{10,11... | collective-permute-start | bytes 983048 | tf_op jit(solution)/shard_map/ppermute | solution.py:31
  81.3 0.0 copy-start.3
  81.3 0.6 while.16
  81.9 0.7 collective-permute-done.2
  82.7 0.0 copy-done.3
  82.7 2.0 %fusion.35 = bf16[1,128,1280]{2,1,0:T(8,128)(2,1)} fusion(f32[128,1280]{1,0:T(8,128)} %get-tuple-element.367, bf16[128,1280]{1,0:T(8,128)(2,1)} %collective-permute-done.2, bf16[1,128,1280]{2,1,0:T(8,128)(2,1)S(1)} %copy-done.3), kind=kLoop, calls=%fused_computation.76 | loop fusion | flops 819200 | bytes 1638400 | tf_op jit(solution)/shard_map/broadcast_in_dim | solution.py:455
  (3 shorter events, 0.0 us)
Async XLA Ops:
  0.0 1.0 %copy-start.1 = (bf16[1,128,1280]{2,1,0:T(8,128)(2,1)S(1)}, bf16[1,128,1280]{2,1,0:T(8,128)(2,1)}, u32[]{:S(2)}) copy-start(bf16[1,128,1280]{2,1,0:T(8,128)(2,1)} %param.14) | copy-start | bytes 983044
  2.2 23.2 %all-to-all-start.1 = ((bf16[128,2,640]{2,1,0:T(2,128)(2,1)}), bf16[128,2,640]{2,1,0:T(2,128)(2,1)}, u32[]{:S(2)}, u32[]{:S(2)}) async-start(bf16[128,2,640]{2,1,0:T(2,128)(2,1)} %shard_map.83), calls=%async_computation.1 | async-start | bytes 655360 | tf_op jit(solution)/shard_map/all_to_all | solution.py:26
  14.9 0.7 copy-start.4
  15.6 0.7 copy-start.5
  29.4 8.7 %copy-start = (bf16[1280,1280]{1,0:T(8,128)(2,1)S(1)}, bf16[1280,1280]{1,0:T(8,128)(2,1)}, u32[]{:S(2)}) copy-start(bf16[1280,1280]{1,0:T(8,128)(2,1)} %weight.1) | copy-start | bytes 9830404
  29.4 34.7 %all-to-all-start.2 = ((bf16[128,3,4,640]{3,2,1,0:T(4,128)(2,1)}), bf16[128,3,4,640]{3,2,1,0:T(4,128)(2,1)}, u32[]{:S(2)}, u32[]{:S(2)}) async-start(bf16[128,3,4,640]{3,2,1,0:T(4,128)(2,1)} %shard_map.84), calls=%async_computation.2 | async-start | bytes 3932160 | tf_op jit(solution)/shard_map/all_to_all | solution.py:26
  35.1 2.9 %collective-permute-start.1 = (bf16[128,1280]{1,0:T(8,128)(2,1)}, bf16[128,1280]{1,0:T(8,128)(2,1)}, u32[]{:S(2)}, u32[]{:S(2)}) collective-permute-start(bf16[128,1280]{1,0:T(8,128)(2,1)} %bitcast.57), channel_id=1, source_target_pairs={{0,1},{1,0},{2,3},{3,2},{4,5},{5,4},{6,7},{7,6},{8,9},{9,8},{10,11... | collective-permute-start | bytes 983048 | tf_op jit(solution)/shard_map/ppermute | solution.py:31
  38.1 1.0 %copy-start.2 = (bf16[1,128,1280]{2,1,0:T(8,128)(2,1)S(1)}, bf16[1,128,1280]{2,1,0:T(8,128)(2,1)}, u32[]{:S(2)}) copy-start(bf16[1,128,1280]{2,1,0:T(8,128)(2,1)} %param.14) | copy-start | bytes 983044
  80.3 2.4 %collective-permute-start.2 = (bf16[128,1280]{1,0:T(8,128)(2,1)S(1)}, bf16[128,1280]{1,0:T(8,128)(2,1)}, u32[]{:S(2)}, u32[]{:S(2)}) collective-permute-start(bf16[128,1280]{1,0:T(8,128)(2,1)S(1)} %get-tuple-element.368), channel_id=1, source_target_pairs={{0,1},{1,0},{2,3},{3,2},{4,5},{5,4},{6,7},{7,6},{8,9},{9,8},{10,11... | collective-permute-start | bytes 983048 | tf_op jit(solution)/shard_map/ppermute | solution.py:31
  81.3 1.4 %copy-start.3 = (bf16[1,128,1280]{2,1,0:T(8,128)(2,1)S(1)}, bf16[1,128,1280]{2,1,0:T(8,128)(2,1)}, u32[]{:S(2)}) copy-start(bf16[1,128,1280]{2,1,0:T(8,128)(2,1)} %param.14) | copy-start | bytes 983044

commit v7 on v6

--- a/solution.py
+++ b/solution.py
@@ -163,44 +163,58 @@
     )(me.reshape(1), pairs, lengths.reshape(1, -1), holder.reshape(1, -1))
 
 
-def pick_kernel(selector, mine, picked, even, odd):
+def pick_kernel(selector_at, mine_at, picked_at, selector, mine, picked, even, odd, sems):
     rows, _, half = mine.shape
-
-    @pl.when(pl.program_id(0) == 0)
-    def _():
-        units = mine[...].reshape(2 * rows, half)
-        ends = units[:, 512:640].astype(F32)
-        turned = half_turn(ends)
-        low = iota(ends.shape, 1) < 64
-        nil = jnp.zeros_like(ends)
-        main = jnp.concatenate([units[:, 0:256], units[:, 256:512]], axis=0)
-        first = jnp.concatenate([jnp.where(low, ends, nil), jnp.where(low, turned, nil)], axis=0)
-        second = jnp.concatenate([jnp.where(low, nil, turned), jnp.where(low, nil, ends)], axis=0)
-        even[...] = jnp.concatenate([main, first.astype(BF)], axis=1)
-        odd[...] = jnp.concatenate([main, second.astype(BF)], axis=1)
-
-    first = mm(selector[:, : 4 * rows], even[...])
-    second = mm(selector[:, 4 * rows :], odd[...])
-    rest = first[:, 256:] + second[:, 256:]
-    message = jnp.concatenate([first[:, :256], second[:, :256], rest], axis=1).astype(BF)
-    picked[...] = message.reshape(picked.shape)
+    pieces = 4
+    tall, deep = selector.shape[0] // pieces, picked.shape[0] // pieces
+    arrive = [pltpu.make_async_copy(mine_at, mine, sems.at[2 * pieces])]
+    leave = []
+    for i in range(pieces):
+        at, to = pl.ds(i * tall, tall), pl.ds(i * deep, deep)
+        arrive.append(pltpu.make_async_copy(selector_at.at[at], selector.at[at], sems.at[i]))
+        leave.append(pltpu.make_async_copy(picked.at[to], picked_at.at[to], sems.at[pieces + i]))
+    for copy in arrive:
+        copy.start()
+    arrive[0].wait()
+    units = mine[...].reshape(2 * rows, half)
+    ends = units[:, 512:640].astype(F32)
+    turned = half_turn(ends)
+    low = iota(ends.shape, 1) < 64
+    nil = jnp.zeros_like(ends)
+    main = jnp.concatenate([units[:, 0:256], units[:, 256:512]], axis=0)
+    first = jnp.concatenate([jnp.where(low, ends, nil), jnp.where(low, turned, nil)], axis=0)
+    second = jnp.concatenate([jnp.where(low, nil, turned), jnp.where(low, nil, ends)], axis=0)
+    even[...] = jnp.concatenate([main, first.astype(BF)], axis=1)
+    odd[...] = jnp.concatenate([main, second.astype(BF)], axis=1)
+    for i in range(pieces):
+        arrive[1 + i].wait()
+        at, to = slice(i * tall, (i + 1) * tall), slice(i * deep, (i + 1) * deep)
+        first = mm(selector[at, : 4 * rows], even[...])
+        second = mm(selector[at, 4 * rows :], odd[...])
+        rest = first[:, 256:] + second[:, 256:]
+        message = jnp.concatenate([first[:, :256], second[:, :256], rest], axis=1).astype(BF)
+        picked[to] = message.reshape((deep,) + picked.shape[1:])
+        leave[i].start()
+    for copy in leave:
+        copy.wait()
 
 
 def pick(selector, mine, outer):
     devices, _, half = mine.shape
-    rows, units = selector.shape
-    steps = 2
-    nought = (0,) * (len(outer) + 1)
+    shape = (devices,) + outer + (half,)
     return pl.pallas_call(
         pick_kernel,
-        out_shape=jax.ShapeDtypeStruct((devices,) + outer + (half,), BF),
-        grid=(steps,),
-        in_specs=[
-            pl.BlockSpec((rows // steps, units), lambda i: (i, 0)),
-            pl.BlockSpec(mine.shape, lambda i: (0, 0, 0)),
+        out_shape=jax.ShapeDtypeStruct(shape, BF),
+        in_specs=[ANY] * 2,
+        out_specs=ANY,
+        scratch_shapes=[
+            pltpu.VMEM(selector.shape, BF),
+            pltpu.VMEM(mine.shape, BF),
+            pltpu.VMEM(shape, BF),
+            pltpu.VMEM((4 * devices, 384), BF),
+            pltpu.VMEM((4 * devices, 384), BF),
+            pltpu.SemaphoreType.DMA((9,)),
         ],
-        out_specs=pl.BlockSpec((devices // steps,) + outer + (half,), lambda i: (i,) + nought),
-        scratch_shapes=[pltpu.VMEM((4 * devices, 384), BF)] * 2,
         compiler_params=pltpu.CompilerParams(vmem_limit_bytes=16 * MIB),
         cost_estimate=pl.CostEstimate(flops=10**9, bytes_accessed=10**7, transcendentals=0),
     )(selector, mine)
@@ -230,18 +244,25 @@
 
 
 def attend_kernel(
-    meta, got_at, query_at, k_at, v_at, o_at, out, sibling,
-    got, query, weight_k, weight_v, weight_o, rows, keys, values,
-    context, scores, weights, scales, sems,
+    meta_at, got_at, query_at, k_at, v_at, o_at, out_at, sibling_at,
+    meta, got, query, weight_k, weight_v, weight_o, rows, keys, values,
+    context, scores, weights, scales, out, sibling, sems,
 ):
+    def copy(index, source, target):
+        return pltpu.make_async_copy(source, target, sems.at[index])
+
+    quarters = []
+    for quarter in range(4):
+        at = pl.ds(quarter * BLOCK, BLOCK)
+        quarters.append(copy(quarter, got_at.at[at], got.at[at]))
     copies = [
-        pltpu.make_async_copy(a, b, sems.at[i])
+        copy(4 + i, a, b)
         for i, (a, b) in enumerate(
-            [(got_at, got), (k_at, weight_k), (v_at, weight_v), (query_at, query), (o_at, weight_o)]
+            [(meta_at, meta), (k_at, weight_k), (v_at, weight_v), (query_at, query), (o_at, weight_o)]
         )
     ]
-    for copy in copies[:3]:
-        copy.start()
+    for one in quarters + copies[:3]:
+        one.start()
     width = weight_k.shape[0]
     each = 1
     for n in got.shape[1:-1]:
@@ -253,15 +274,13 @@
     n = jnp.int32(each)
     turned = (lead == lax.rem(lane, n) * 16 + lax.div(lane, n)).astype(BF)
     low = iota((tall, 128), 1) < 64
-    copies[0].wait()
-    copies[3].start()
-    copies[4].start()
-    for part in range(2):
-        rests = []
-        for quarter in range(4):
+    rests = {}
+    for quarter in range(4):
+        quarters[quarter].wait()
+        for part in range(2):
             at = quarter * BLOCK + part * 16
             piece = mm(turned, got[at : at + 16].reshape(tall, width // 2))
-            rests.append(piece[:, 512:640])
+            rests[quarter, part] = piece[:, 512:640]
             piece = piece.astype(BF)
             for u in range(2 * each):
                 to = u * BLOCK + part * 16
@@ -270,7 +289,7 @@
                     (u // 2) * 16 : (u // 2) * 16 + 16, side : side + 256
                 ]
             if quarter % 2 == 1:
-                left, right = rests[-2:]
+                left, right = rests[quarter - 1, part], rests[quarter, part]
                 even = jnp.where(low, left, half_turn(right)).astype(BF)
                 odd = jnp.where(low, half_turn(left), right).astype(BF)
                 tile = 1024 + 128 * (quarter // 2)
@@ -279,6 +298,9 @@
                     rows[to : to + 16, tile : tile + 128] = (odd if u % 2 else even)[
                         (u // 2) * 16 : (u // 2) * 16 + 16
                     ]
+    copies[3].start()
+    copies[4].start()
+    copies[0].wait()
     chunks = (meta[0, 7] + 7) // 8
 
     def project(weight, to):
@@ -362,11 +384,20 @@
 
     lax.fori_loop(0, (meta[0, 3] + 1) // 2, two_sides, 0)
     copies[4].wait()
-    for who, to in ((1, sibling), (0, out)):
-        part = context[who * width : (who + 1) * width, :].astype(BF)
-        update = lax.dot_general(part, weight_o[...], DOWN, preferred_element_type=F32)
-        update = jnp.where(iota(update.shape, 0) < meta[0, 4 + who], update, 0.0)
-        to[...] = update.astype(to.dtype)
+    part = context[width:, :].astype(BF)
+    update = lax.dot_general(part, weight_o[...], DOWN, preferred_element_type=F32)
+    sibling[...] = jnp.where(iota(update.shape, 0) < meta[0, 5], update, 0.0).astype(BF)
+    leave = [copy(9, sibling, sibling_at)]
+    leave[0].start()
+    part = context[:width, :].astype(BF)
+    for half in range(2):
+        at = pl.ds(half * (width // 2), width // 2)
+        update = lax.dot_general(part, weight_o[:, at], DOWN, preferred_element_type=F32)
+        out[:, at] = jnp.where(iota(update.shape, 0) < meta[0, 4], update, 0.0)
+        leave.append(copy(10 + half, out.at[:, at], out_at.at[:, at]))
+        leave[-1].start()
+    for one in leave:
+        one.wait()
 
 
 def attend(meta, got, query, weight_k, weight_v, weight_o):
@@ -381,9 +412,10 @@
             jax.ShapeDtypeStruct((128, width), F32),
             jax.ShapeDtypeStruct((128, width), BF),
         ),
-        in_specs=[SMEM] + [ANY] * 5,
-        out_specs=(VMEM, VMEM),
+        in_specs=[ANY] * 6,
+        out_specs=(ANY, ANY),
         scratch_shapes=[
+            pltpu.SMEM(meta.shape, jnp.int32),
             pltpu.VMEM(got.shape, BF),
             pltpu.VMEM(query.shape, BF),
             pltpu.VMEM((width, width), BF),
@@ -396,7 +428,9 @@
             pltpu.VMEM((2, 128, 2 * width), F32),
             pltpu.VMEM((2, 128, 2 * width), BF),
             pltpu.VMEM((2, 8, 2 * width), F32),
-            pltpu.SemaphoreType.DMA((5,)),
+            pltpu.VMEM((128, width), F32),
+            pltpu.VMEM((128, width), BF),
+            pltpu.SemaphoreType.DMA((12,)),
         ],
         compiler_params=pltpu.CompilerParams(vmem_limit_bytes=36 * MIB),
         cost_estimate=pl.CostEstimate(flops=10**10, bytes_accessed=10**7, transcendentals=10**6),

time: 83.7 us -> 80.1 us (0.957)
  the two profiles are of different devices: /device:TPU:1 before, /device:TPU:33 now
where the time goes in v7:
time: 80.1 us; the launch traced here: 79.5 us
  waiting for transfers between devices  27.1 us (34%)
  Pallas kernels  24.6 us (31%)
  starting transfers between devices  19.9 us (25%)
  local copies, waits for them, and re-layouts  4.66 us (6%)
  other arithmetic  2.66 us (3%)
    all_to_all x2, waiting for transfers between devices, exchange(): return lax.all_to_all(array, AXES, split_axis=0, concat_axis=0, tiled=True)  25.9 us
    all_to_all x2, starting transfers between devices, exchange(): return lax.all_to_all(array, AXES, split_axis=0, concat_axis=0, tiled=True)  18 us
    pallas_call x1, Pallas kernels, attend(): pl.pallas_call(attend_kernel, out_shape=(jax.ShapeDtypeStruct((128, width...  12.8 us
    pallas_call x1, Pallas kernels, pick(): pl.pallas_call(pick_kernel, out_shape=jax.ShapeDtypeStruct(shape, BF), in...  4.32 us
    unnamed x13, local copies, waits for them, and re-layouts  4.07 us
    pallas_call x1, Pallas kernels, queries(): pl.pallas_call(query_kernel, out_shape=jax.ShapeDtypeStruct((2 * own.shap...  3.22 us
    pallas_call x1, Pallas kernels, plan(): pl.pallas_call(plan_kernel, out_shape=(jax.ShapeDtypeStruct((devices * FI...  3.08 us
    broadcast_in_dim x1, other arithmetic, local(): return (own.astype(F32) + (kept + received.astype(F32))).astype(BF)[None]  2.01 us
  transfers between devices with their start and end apart: 4, of which 4 were waited for; matrix products, arithmetic and copies ran while one was open for 3% of the time, Pallas kernels for 8%

profile of v7, /device:TPU:33, one launch (start us, length us, event | category | flops | bytes accessed | tf_op | source)
XLA Modules:
  0.0 79.5 jit_solution(7185864828517291729)
XLA Ops:
  0.0 0.0 copy-start.1
  0.0 1.0 %copy-done.1 = bf16[1,128,1280]{2,1,0:T(8,128)(2,1)S(1)} copy-done((bf16[1,128,1280]{2,1,0:T(8,128)(2,1)S(1)}, bf16[1,128,1280]{2,1,0:T(8,128)(2,1)}, u32[]{:S(2)}) %copy-start.1) | copy-done | bytes 327704
  1.0 1.2 %shard_map.83 = bf16[128,2,640]{2,1,0:T(2,128)(2,1)} custom-call(bf16[128,1280]{1,0:T(8,128)(2,1)S(1)} %bitcast.58), custom_call_target="tpu_custom_call" | custom-call | tf_op jit(solution)/shard_map/pallas_call | solution.py:66
  2.2 10.9 %all-to-all-start.1 = ((bf16[128,2,640]{2,1,0:T(2,128)(2,1)}), bf16[128,2,640]{2,1,0:T(2,128)(2,1)}, u32[]{:S(2)}, u32[]{:S(2)}) async-start(bf16[128,2,640]{2,1,0:T(2,128)(2,1)} %shard_map.83), calls=%async_computation.1 | async-start | bytes 655360 | tf_op jit(solution)/shard_map/all_to_all | solution.py:26
  13.1 0.8 %copy.23.pairs = s32[256,2]{1,0:T(8,128)S(1)} copy(s32[256,2]{0,1:T(2,128)} %param.19) | data formatting | bytes 4096 | tf_op args[5]
  13.9 0.0 copy-start.4
  13.9 0.6 copy-done.4
  14.6 0.0 copy-start.5
  14.6 0.7 copy-done.5
  15.2 3.1 %shard_map.82 = (bf16[1536,1024]{1,0:T(8,128)(2,1)S(1)}, s32[24,128]{1,0:T(8,128)S(1)}, s32[8,512]{1,0:T(8,128)S(1)}) custom-call(s32[1]{0:T(128)} %bitcast.11.place, s32[256,2]{1,0:T(8,128)S(1)} %copy.23.pairs, s32[1,128]{1,0:T(1,128)S(1)} %bitcast.60, s32[1,128]{1,0:T(1,128)S(1)} %bitcast.61), custom_call_target="tpu_custom_call" | custom-call | flops 1000000000 | bytes 1000000 | tf_op jit(solution)/shard_map/pallas_call | solution.py:152
  18.3 4.8 %all-to-all-done.1.mine_at = bf16[128,2,640]{2,1,0:T(2,128)(2,1)} async-done(((bf16[128,2,640]{2,1,0:T(2,128)(2,1)}), bf16[128,2,640]{2,1,0:T(2,128)(2,1)}, u32[]{:S(2)}, u32[]{:S(2)}) %all-to-all-start.1) | async-done | bytes 327712 | tf_op jit(solution)/shard_map/all_to_all | solution.py:26
  23.1 4.3 %shard_map.84 = bf16[128,3,4,640]{3,2,1,0:T(4,128)(2,1)} custom-call(bf16[1536,1024]{1,0:T(8,128)(2,1)S(1)} %get-tuple-element.364.selector_at, bf16[128,2,640]{2,1,0:T(2,128)(2,1)} %all-to-all-done.1.mine_at), custom_call_target="tpu_custom_call" | custom-call | flops 1000000000 | bytes 10000000 | tf_op jit(solution)/shard_map/pallas_call | solution.py:205
  27.5 0.0 copy-start
  27.5 7.1 %all-to-all-start.2 = ((bf16[128,3,4,640]{3,2,1,0:T(4,128)(2,1)}), bf16[128,3,4,640]{3,2,1,0:T(4,128)(2,1)}, u32[]{:S(2)}, u32[]{:S(2)}) async-start(bf16[128,3,4,640]{3,2,1,0:T(4,128)(2,1)} %shard_map.84), calls=%async_computation.2 | async-start | bytes 3932160 | tf_op jit(solution)/shard_map/all_to_all | solution.py:26
  34.6 0.4 collective-permute-start.1
  35.0 0.6 slice.53
  35.6 0.6 and_reduce_fusion.1
  36.3 0.4 collective-permute-done.1.other
  36.6 0.0 copy-done
  36.6 0.0 copy-start.2
  36.6 1.0 %copy-done.2 = bf16[1,128,1280]{2,1,0:T(8,128)(2,1)S(1)} copy-done((bf16[1,128,1280]{2,1,0:T(8,128)(2,1)S(1)}, bf16[1,128,1280]{2,1,0:T(8,128)(2,1)}, u32[]{:S(2)}) %copy-start.2) | copy-done | bytes 327704
  37.6 3.2 %shard_map.85.query_at = bf16[2560,256]{1,0:T(8,128)(2,1)} custom-call(bf16[128,1280]{1,0:T(8,128)(2,1)S(1)} %bitcast.59, bf16[128,1280]{1,0:T(8,128)(2,1)} %collective-permute-done.1.other, bf16[1280,1280]{1,0:T(8,128)(2,1)S(1)} %copy-done), custom_call_target="tpu_custom_call" | custom-call | flops 1000000000 | bytes 10000000 | tf_op jit(solution)/shard_map/pallas_call | solution.py:236
  40.8 21.1 %all-to-all-done.2.got_at = bf16[128,3,4,640]{3,2,1,0:T(4,128)(2,1)} async-done(((bf16[128,3,4,640]{3,2,1,0:T(4,128)(2,1)}), bf16[128,3,4,640]{3,2,1,0:T(4,128)(2,1)}, u32[]{:S(2)}, u32[]{:S(2)}) %all-to-all-start.2) | async-done | bytes 1966112 | tf_op jit(solution)/shard_map/all_to_all | solution.py:26
  61.9 12.8 %shard_map.86 = (f32[128,1280]{1,0:T(8,128)}, bf16[128,1280]{1,0:T(8,128)(2,1)S(1)}) custom-call(s32[24,128]{1,0:T(8,128)S(1)} %get-tuple-element.563.meta_at, bf16[128,3,4,640]{3,2,1,0:T(4,128)(2,1)} %all-to-all-done.2.got_at, bf16[2560,256]{1,0:T(8,128)(2,1)} %shard_map.85.query_at, bf16[1280,1280]{1,0:T(8,128)(2,1)} %k_at.1, bf16[1280,1280]{1,0:T(8,128)(2,1)} %v_at.1, ...), custom_call_target="tpu_custom_call" | custom-call | flops 10000000000 | bytes 10000000 | tf_op jit(solution)/shard_map/pallas_call | solution.py:409
  74.7 1.4 %collective-permute-start.2 = (bf16[128,1280]{1,0:T(8,128)(2,1)S(1)}, bf16[128,1280]{1,0:T(8,128)(2,1)}, u32[]{:S(2)}, u32[]{:S(2)}) collective-permute-start(bf16[128,1280]{1,0:T(8,128)(2,1)S(1)} %get-tuple-element.368), channel_id=1, source_target_pairs={{0,1},{1,0},{2,3},{3,2},{4,5},{5,4},{6,7},{7,6},{8,9},{9,8},{10,11... | collective-permute-start | bytes 983048 | tf_op jit(solution)/shard_map/ppermute | solution.py:31
  76.1 0.0 copy-start.3
  76.1 0.6 while.16
  76.8 0.7 collective-permute-done.2
  77.5 0.0 copy-done.3
  77.5 2.0 %fusion.35 = bf16[1,128,1280]{2,1,0:T(8,128)(2,1)} fusion(f32[128,1280]{1,0:T(8,128)} %get-tuple-element.367, bf16[128,1280]{1,0:T(8,128)(2,1)} %collective-permute-done.2, bf16[1,128,1280]{2,1,0:T(8,128)(2,1)S(1)} %copy-done.3), kind=kLoop, calls=%fused_computation.76 | loop fusion | flops 819200 | bytes 1638400 | tf_op jit(solution)/shard_map/broadcast_in_dim | solution.py:489
  (3 shorter events, 0.0 us)
Async XLA Ops:
  0.0 1.0 %copy-start.1 = (bf16[1,128,1280]{2,1,0:T(8,128)(2,1)S(1)}, bf16[1,128,1280]{2,1,0:T(8,128)(2,1)}, u32[]{:S(2)}) copy-start(bf16[1,128,1280]{2,1,0:T(8,128)(2,1)} %param.14) | copy-start | bytes 983044
  2.2 21.0 %all-to-all-start.1 = ((bf16[128,2,640]{2,1,0:T(2,128)(2,1)}), bf16[128,2,640]{2,1,0:T(2,128)(2,1)}, u32[]{:S(2)}, u32[]{:S(2)}) async-start(bf16[128,2,640]{2,1,0:T(2,128)(2,1)} %shard_map.83), calls=%async_computation.1 | async-start | bytes 655360 | tf_op jit(solution)/shard_map/all_to_all | solution.py:26
  13.9 0.7 copy-start.4
  14.6 0.7 copy-start.5
  27.5 9.1 %copy-start = (bf16[1280,1280]{1,0:T(8,128)(2,1)S(1)}, bf16[1280,1280]{1,0:T(8,128)(2,1)}, u32[]{:S(2)}) copy-start(bf16[1280,1280]{1,0:T(8,128)(2,1)} %weight.1) | copy-start | bytes 9830404
  27.5 34.5 %all-to-all-start.2 = ((bf16[128,3,4,640]{3,2,1,0:T(4,128)(2,1)}), bf16[128,3,4,640]{3,2,1,0:T(4,128)(2,1)}, u32[]{:S(2)}, u32[]{:S(2)}) async-start(bf16[128,3,4,640]{3,2,1,0:T(4,128)(2,1)} %shard_map.84), calls=%async_computation.2 | async-start | bytes 3932160 | tf_op jit(solution)/shard_map/all_to_all | solution.py:26
  34.6 2.1 %collective-permute-start.1 = (bf16[128,1280]{1,0:T(8,128)(2,1)}, bf16[128,1280]{1,0:T(8,128)(2,1)}, u32[]{:S(2)}, u32[]{:S(2)}) collective-permute-start(bf16[128,1280]{1,0:T(8,128)(2,1)} %bitcast.57), channel_id=1, source_target_pairs={{0,1},{1,0},{2,3},{3,2},{4,5},{5,4},{6,7},{7,6},{8,9},{9,8},{10,11... | collective-permute-start | bytes 983048 | tf_op jit(solution)/shard_map/ppermute | solution.py:31
  36.6 1.0 %copy-start.2 = (bf16[1,128,1280]{2,1,0:T(8,128)(2,1)S(1)}, bf16[1,128,1280]{2,1,0:T(8,128)(2,1)}, u32[]{:S(2)}) copy-start(bf16[1,128,1280]{2,1,0:T(8,128)(2,1)} %param.14) | copy-start | bytes 983044
  74.7 2.8 %collective-permute-start.2 = (bf16[128,1280]{1,0:T(8,128)(2,1)S(1)}, bf16[128,1280]{1,0:T(8,128)(2,1)}, u32[]{:S(2)}, u32[]{:S(2)}) collective-permute-start(bf16[128,1280]{1,0:T(8,128)(2,1)S(1)} %get-tuple-element.368), channel_id=1, source_target_pairs={{0,1},{1,0},{2,3},{3,2},{4,5},{5,4},{6,7},{7,6},{8,9},{9,8},{10,11... | collective-permute-start | bytes 983048 | tf_op jit(solution)/shard_map/ppermute | solution.py:31
  76.1 1.4 %copy-start.3 = (bf16[1,128,1280]{2,1,0:T(8,128)(2,1)S(1)}, bf16[1,128,1280]{2,1,0:T(8,128)(2,1)}, u32[]{:S(2)}) copy-start(bf16[1,128,1280]{2,1,0:T(8,128)(2,1)} %param.14) | copy-start | bytes 983044

commit v8 on v7

--- a/solution.py
+++ b/solution.py
@@ -43,14 +43,23 @@
     return pltpu.roll(array.astype(F32), 64, 1)
 
 
-def front_kernel(own, pieces):
+def front_kernel(own_at, pieces_at, own, pieces, sems):
     low = iota((BLOCK, 128), 1) < 64
-    for quarter in range(4):
-        main = slice(256 * quarter, 256 * quarter + 256)
-        tile = slice(1024 + 128 * (quarter // 2), 1152 + 128 * (quarter // 2))
-        for h in range(2):
-            even = slice(2 * h * BLOCK, (2 * h + 1) * BLOCK)
-            odd = slice((2 * h + 1) * BLOCK, (2 * h + 2) * BLOCK)
+    arrive, leave = [], []
+    for i in range(4):
+        at = pl.ds(i * BLOCK, BLOCK)
+        arrive.append(pltpu.make_async_copy(own_at.at[at], own.at[at], sems.at[i]))
+        leave.append(pltpu.make_async_copy(pieces.at[at], pieces_at.at[at], sems.at[4 + i]))
+    for copy in arrive:
+        copy.start()
+    for h in range(2):
+        arrive[2 * h].wait()
+        arrive[2 * h + 1].wait()
+        even = slice(2 * h * BLOCK, (2 * h + 1) * BLOCK)
+        odd = slice((2 * h + 1) * BLOCK, (2 * h + 2) * BLOCK)
+        for quarter in range(4):
+            main = slice(256 * quarter, 256 * quarter + 256)
+            tile = slice(1024 + 128 * (quarter // 2), 1152 + 128 * (quarter // 2))
             if quarter % 2 == 0:
                 rest = jnp.where(low, own[even, tile].astype(F32), half_turn(own[odd, tile]))
             else:
@@ -59,6 +68,10 @@
             pieces[to, h, 0:256] = own[even, main]
             pieces[to, h, 256:512] = own[odd, main]
             pieces[to, h, 512:640] = rest.astype(BF)
+            if h == 1:
+                leave[quarter].start()
+    for copy in leave:
+        copy.wait()
 
 
 def front(own):
@@ -66,8 +79,13 @@
     return pl.pallas_call(
         front_kernel,
         out_shape=jax.ShapeDtypeStruct((rows, 2, width // 2), BF),
-        in_specs=[VMEM],
-        out_specs=VMEM,
+        in_specs=[ANY],
+        out_specs=ANY,
+        scratch_shapes=[
+            pltpu.VMEM((rows, width), BF),
+            pltpu.VMEM((rows, 2, width // 2), BF),
+            pltpu.SemaphoreType.DMA((8,)),
+        ],
         compiler_params=pltpu.CompilerParams(vmem_limit_bytes=4 * MIB),
     )(own)
 
@@ -117,14 +135,14 @@
     row, lane = iota((rows, devices), 0), iota((rows, devices), 1)
     which, v = lax.div(row, jnp.int32(FIRST // 2)), lax.rem(row, jnp.int32(FIRST // 2))
     spread = mm(jnp.where(which == lane, 1.0, 0.0).astype(BF), table.astype(BF))
-    columns = iota((rows, 4 * devices), 1)
-    unit_at = 2 * (columns % (2 * devices)) + columns // (2 * devices)
+    columns = iota((rows, 2 * devices), 1)
     for side in range(2):
         u = 2 * v + side
         value = jnp.where(lane == u, 4.0 * spread, jnp.where(lane == u + 64, spread, 0.0))
         unit = jnp.sum(value, axis=1, keepdims=True).astype(jnp.int32) - 4
-        at = slice(side * 4 * devices, (side + 1) * 4 * devices)
-        selector[:, at] = jnp.where(unit == unit_at, 1.0, 0.0).astype(BF)
+        sign = (1 - 2 * (unit % 2)).astype(F32)
+        at = slice(side * 2 * devices, (side + 1) * 2 * devices)
+        selector[:, at] = jnp.where(unit // 2 == columns, sign, 0.0).astype(BF)
     held = active & (dest == me)
     chosen = held & (slot == iota((FIRST, total), 0))
 
@@ -152,7 +170,7 @@
     return pl.pallas_call(
         plan_kernel,
         out_shape=(
-            jax.ShapeDtypeStruct((devices * FIRST // 2, 8 * devices), BF),
+            jax.ShapeDtypeStruct((devices * FIRST // 2, 4 * devices), BF),
             jax.ShapeDtypeStruct((FIRST, 128), jnp.int32),
             jax.ShapeDtypeStruct((8, 2 * pairs.shape[0]), jnp.int32),
         ),
@@ -163,9 +181,9 @@
     )(me.reshape(1), pairs, lengths.reshape(1, -1), holder.reshape(1, -1))
 
 
-def pick_kernel(selector_at, mine_at, picked_at, selector, mine, picked, even, odd, sems):
+def pick_kernel(selector_at, mine_at, picked_at, selector, mine, picked, units, sems):
     rows, _, half = mine.shape
-    pieces = 4
+    pieces = 2
     tall, deep = selector.shape[0] // pieces, picked.shape[0] // pieces
     arrive = [pltpu.make_async_copy(mine_at, mine, sems.at[2 * pieces])]
     leave = []
@@ -176,23 +194,24 @@
     for copy in arrive:
         copy.start()
     arrive[0].wait()
-    units = mine[...].reshape(2 * rows, half)
-    ends = units[:, 512:640].astype(F32)
-    turned = half_turn(ends)
-    low = iota(ends.shape, 1) < 64
-    nil = jnp.zeros_like(ends)
-    main = jnp.concatenate([units[:, 0:256], units[:, 256:512]], axis=0)
-    first = jnp.concatenate([jnp.where(low, ends, nil), jnp.where(low, turned, nil)], axis=0)
-    second = jnp.concatenate([jnp.where(low, nil, turned), jnp.where(low, nil, ends)], axis=0)
-    even[...] = jnp.concatenate([main, first.astype(BF)], axis=1)
-    odd[...] = jnp.concatenate([main, second.astype(BF)], axis=1)
+    units[:, :half] = mine[...].reshape(2 * rows, half)
+    units[:, half:] = jnp.ones((2 * rows, 128), BF)
+    low = iota((tall, 128), 1) < 64
     for i in range(pieces):
         arrive[1 + i].wait()
         at, to = slice(i * tall, (i + 1) * tall), slice(i * deep, (i + 1) * deep)
-        first = mm(selector[at, : 4 * rows], even[...])
-        second = mm(selector[at, 4 * rows :], odd[...])
-        rest = first[:, 256:] + second[:, 256:]
-        message = jnp.concatenate([first[:, :256], second[:, :256], rest], axis=1).astype(BF)
+        tiles, rests = [], []
+        for side in range(2):
+            row = mm(selector[at, side * 2 * rows : (side + 1) * 2 * rows], units[...])
+            left = row[:, half:] > 0.0
+            for tile in range(2):
+                one, two = tile * 128, 256 + tile * 128
+                tiles.append(jnp.where(left, row[:, one : one + 128], -row[:, two : two + 128]))
+            ends = row[:, 512:640]
+            turned = half_turn(ends)
+            rests.append(jnp.where(left, turned, -ends) if side else jnp.where(left, ends, -turned))
+        tiles.append(jnp.where(low, rests[0], rests[1]))
+        message = jnp.concatenate(tiles, axis=1).astype(BF)
         picked[to] = message.reshape((deep,) + picked.shape[1:])
         leave[i].start()
     for copy in leave:
@@ -211,8 +230,7 @@
             pltpu.VMEM(selector.shape, BF),
             pltpu.VMEM(mine.shape, BF),
             pltpu.VMEM(shape, BF),
-            pltpu.VMEM((4 * devices, 384), BF),
-            pltpu.VMEM((4 * devices, 384), BF),
+            pltpu.VMEM((2 * devices, half + 128), BF),
             pltpu.SemaphoreType.DMA((9,)),
         ],
         compiler_params=pltpu.CompilerParams(vmem_limit_bytes=16 * MIB),
@@ -244,8 +262,8 @@
 
 
 def attend_kernel(
-    meta_at, got_at, query_at, k_at, v_at, o_at, out_at, sibling_at,
-    meta, got, query, weight_k, weight_v, weight_o, rows, keys, values,
+    meta_at, got_at, query_at, k_at, v_at, o_at, own_at, out_at, sibling_at,
+    meta, own, got, query, weight_k, weight_v, weight_o, rows, keys, values,
     context, scores, weights, scales, out, sibling, sems,
 ):
     def copy(index, source, target):
@@ -258,7 +276,8 @@
     copies = [
         copy(4 + i, a, b)
         for i, (a, b) in enumerate(
-            [(meta_at, meta), (k_at, weight_k), (v_at, weight_v), (query_at, query), (o_at, weight_o)]
+            [(meta_at, meta), (k_at, weight_k), (v_at, weight_v), (query_at, query), (o_at, weight_o),
+             (own_at, own)]
         )
     ]
     for one in quarters + copies[:3]:
@@ -300,16 +319,26 @@
                     ]
     copies[3].start()
     copies[4].start()
+    copies[5].start()
     copies[0].wait()
-    chunks = (meta[0, 7] + 7) // 8
+    full = (meta[0, 7] + 3) // 8
+    partial = (meta[0, 7] > full * 8).astype(jnp.int32)
 
     def project(weight, to):
-        def some(chunk, carry):
-            at = pl.ds(pl.multiple_of(chunk * 256, 256), 256)
+        def some(first, size):
+            at = pl.ds(pl.multiple_of(first, size), size)
             to[at, :] = mm(rows[at, :], weight[...]).astype(BF)
+
+        def whole(chunk, carry):
+            some(chunk * 256, 256)
             return carry
 
-        lax.fori_loop(0, chunks, some, 0)
+        def rest(chunk, carry):
+            some(full * 256, 128)
+            return carry
+
+        lax.fori_loop(0, full, whole, 0)
+        lax.fori_loop(0, partial, rest, 0)
 
     copies[1].wait()
     project(weight_k, keys)
@@ -384,23 +413,25 @@
 
     lax.fori_loop(0, (meta[0, 3] + 1) // 2, two_sides, 0)
     copies[4].wait()
+    copies[5].wait()
     part = context[width:, :].astype(BF)
     update = lax.dot_general(part, weight_o[...], DOWN, preferred_element_type=F32)
     sibling[...] = jnp.where(iota(update.shape, 0) < meta[0, 5], update, 0.0).astype(BF)
-    leave = [copy(9, sibling, sibling_at)]
+    leave = [copy(10, sibling, sibling_at)]
     leave[0].start()
     part = context[:width, :].astype(BF)
     for half in range(2):
         at = pl.ds(half * (width // 2), width // 2)
         update = lax.dot_general(part, weight_o[:, at], DOWN, preferred_element_type=F32)
-        out[:, at] = jnp.where(iota(update.shape, 0) < meta[0, 4], update, 0.0)
-        leave.append(copy(10 + half, out.at[:, at], out_at.at[:, at]))
+        update = jnp.where(iota(update.shape, 0) < meta[0, 4], update, 0.0)
+        out[:, at] = own[:, at].astype(F32) + update
+        leave.append(copy(11 + half, out.at[:, at], out_at.at[:, at]))
         leave[-1].start()
     for one in leave:
         one.wait()
 
 
-def attend(meta, got, query, weight_k, weight_v, weight_o):
+def attend(meta, got, query, weight_k, weight_v, weight_o, own):
     width = weight_k.shape[0]
     each = 1
     for n in got.shape[1:-1]:
@@ -412,10 +443,11 @@
             jax.ShapeDtypeStruct((128, width), F32),
             jax.ShapeDtypeStruct((128, width), BF),
         ),
-        in_specs=[ANY] * 6,
+        in_specs=[ANY] * 7,
         out_specs=(ANY, ANY),
         scratch_shapes=[
             pltpu.SMEM(meta.shape, jnp.int32),
+            pltpu.VMEM(own.shape, BF),
             pltpu.VMEM(got.shape, BF),
             pltpu.VMEM(query.shape, BF),
             pltpu.VMEM((width, width), BF),
@@ -430,11 +462,11 @@
             pltpu.VMEM((2, 8, 2 * width), F32),
             pltpu.VMEM((128, width), F32),
             pltpu.VMEM((128, width), BF),
-            pltpu.SemaphoreType.DMA((12,)),
+            pltpu.SemaphoreType.DMA((13,)),
         ],
         compiler_params=pltpu.CompilerParams(vmem_limit_bytes=36 * MIB),
         cost_estimate=pl.CostEstimate(flops=10**10, bytes_accessed=10**7, transcendentals=10**6),
-    )(meta, got, query, weight_k, weight_v, weight_o)
+    )(meta, got, query, weight_k, weight_v, weight_o, own)
 
 
 def later_round(number, sides, me, count, meta):
@@ -449,9 +481,9 @@
     entries = [jnp.where(there, source[:, None] + 1, 0), jnp.where(there, spots - base[:, None], 0)]
     high, low = (mm(target.astype(BF), entry.astype(BF)).astype(jnp.int32) for entry in entries)
     unit = (4 * (high - 1) + low).reshape(-1, 2)
-    columns = jnp.arange(4 * count, dtype=jnp.int32)
-    unit_at = 2 * (columns % (2 * count)) + columns // (2 * count)
-    selector = (unit[:, :, None] == unit_at).reshape(unit.shape[0], -1).astype(BF)
+    columns = jnp.arange(2 * count, dtype=jnp.int32)
+    selector = jnp.where((unit // 2)[:, :, None] == columns, (1 - 2 * (unit % 2))[:, :, None], 0)
+    selector = selector.reshape(unit.shape[0], -1).astype(BF)
     held = active & (dest == me)
     order = jnp.sum(held[:, None] & (base[:, None] < base[None, :]), axis=0)
     chosen = held[None, :] & (order[None, :] == spots[:, None])
@@ -474,19 +506,20 @@
     rounds = meta[0, 6]
     query = queries(own, swap(own), weight_q)
 
-    def one_round(selector, meta, outer):
+    def one_round(selector, meta, outer, base):
         got = exchange(pick(selector, mine, outer))
-        return attend(meta, got, query, weight_k, weight_v, weight_o)
+        return attend(meta, got, query, weight_k, weight_v, weight_o, base)
 
     def another(carry):
         number, total = carry
-        kept, given = one_round(*later_round(number, sides, me, count, meta), (LATER // 2,))
+        nothing = jnp.zeros_like(own)
+        kept, given = one_round(*later_round(number, sides, me, count, meta), (LATER // 2,), nothing)
         return number + 1, total + kept + swap(given).astype(F32)
 
-    kept, given = one_round(selector, meta, (FIRST // 8, 4))
+    kept, given = one_round(selector, meta, (FIRST // 8, 4), own)
     received = swap(given)
     _, kept = lax.while_loop(lambda c: c[0] <= rounds, another, (jnp.int32(1), kept))
-    return (own.astype(F32) + (kept + received.astype(F32))).astype(BF)[None]
+    return (kept + received.astype(F32)).astype(BF)[None]
 
 
 def solution(mesh):

time: 80.1 us -> 80.6 us (level)
  the two profiles are of different devices: /device:TPU:33 before, /device:TPU:1 now
where the time goes in v8:
time: 80.6 us; the launch traced here: 79.5 us
  waiting for transfers between devices  28.2 us (35%)
  Pallas kernels  22.3 us (28%)
  starting transfers between devices  19.5 us (24%)
  local copies, waits for them, and re-layouts  6.35 us (8%)
  other arithmetic  2.46 us (3%)
    all_to_all x2, waiting for transfers between devices, exchange(): return lax.all_to_all(array, AXES, split_axis=0, concat_axis=0, tiled=True)  27.1 us
    all_to_all x2, starting transfers between devices, exchange(): return lax.all_to_all(array, AXES, split_axis=0, concat_axis=0, tiled=True)  17.2 us
    pallas_call x1, Pallas kernels, attend(): pl.pallas_call(attend_kernel, out_shape=(jax.ShapeDtypeStruct((128, width...  10.3 us
    unnamed x17, local copies, waits for them, and re-layouts  5.77 us
    pallas_call x1, Pallas kernels, plan(): pl.pallas_call(plan_kernel, out_shape=(jax.ShapeDtypeStruct((devices * FI...  4.14 us
    pallas_call x1, Pallas kernels, queries(): pl.pallas_call(query_kernel, out_shape=jax.ShapeDtypeStruct((2 * own.shap...  3.18 us
    pallas_call x1, Pallas kernels, pick(): pl.pallas_call(pick_kernel, out_shape=jax.ShapeDtypeStruct(shape, BF), in...  3.14 us
    ppermute x2, starting transfers between devices, swap(): return lax.ppermute(array, 'dev', [(i, i ^ 1) for i in range(count)])  2.32 us
  transfers between devices with their start and end apart: 4, of which 4 were waited for; matrix products, arithmetic and copies ran while one was open for 3% of the time, Pallas kernels for 9%

profile of v8, /device:TPU:1, one launch (start us, length us, event | category | flops | bytes accessed | tf_op | source)
XLA Modules:
  0.0 79.5 jit_solution(9545814628665822663)
XLA Ops:
  0.0 0.0 copy-start.1
  0.0 1.0 %copy-done.1 = bf16[1,128,1280]{2,1,0:T(8,128)(2,1)S(1)} copy-done((bf16[1,128,1280]{2,1,0:T(8,128)(2,1)S(1)}, bf16[1,128,1280]{2,1,0:T(8,128)(2,1)}, u32[]{:S(2)}) %copy-start.1) | copy-done | bytes 327704
  1.0 1.5 %shard_map.83 = bf16[128,2,640]{2,1,0:T(2,128)(2,1)} custom-call(bf16[128,1280]{1,0:T(8,128)(2,1)S(1)} %bitcast.63), custom_call_target="tpu_custom_call" | custom-call | tf_op jit(solution)/shard_map/pallas_call | solution.py:79
  2.5 11.5 %all-to-all-start.1 = ((bf16[128,2,640]{2,1,0:T(2,128)(2,1)}), bf16[128,2,640]{2,1,0:T(2,128)(2,1)S(1)}, u32[]{:S(2)}, u32[]{:S(2)}) async-start(bf16[128,2,640]{2,1,0:T(2,128)(2,1)} %shard_map.83), calls=%async_computation.1 | async-start | bytes 655360 | tf_op jit(solution)/shard_map/all_to_all | solution.py:26
  14.0 0.8 %copy.23.pairs = s32[256,2]{1,0:T(8,128)S(1)} copy(s32[256,2]{0,1:T(2,128)} %param.19) | data formatting | bytes 4096 | tf_op args[5]
  14.8 0.0 copy-start.4
  14.8 0.6 copy-done.4
  15.5 0.0 copy-start.5
  15.5 0.7 copy-done.5
  16.1 4.1 %shard_map.82 = (bf16[1536,512]{1,0:T(8,128)(2,1)S(1)}, s32[24,128]{1,0:T(8,128)S(1)}, s32[8,512]{1,0:T(8,128)S(1)}) custom-call(s32[1]{0:T(128)} %bitcast.10.place, s32[256,2]{1,0:T(8,128)S(1)} %copy.23.pairs, s32[1,128]{1,0:T(1,128)S(1)} %bitcast.66, s32[1,128]{1,0:T(1,128)S(1)} %bitcast.67), custom_call_target="tpu_custom_call" | custom-call | flops 1000000000 | bytes 1000000 | tf_op jit(solution)/shard_map/pallas_call | solution.py:170
  20.3 5.3 %all-to-all-done.1.mine_at = bf16[128,2,640]{2,1,0:T(2,128)(2,1)S(1)} async-done(((bf16[128,2,640]{2,1,0:T(2,128)(2,1)}), bf16[128,2,640]{2,1,0:T(2,128)(2,1)S(1)}, u32[]{:S(2)}, u32[]{:S(2)}) %all-to-all-start.1) | async-done | bytes 327712 | tf_op jit(solution)/shard_map/all_to_all | solution.py:26
  25.6 0.0 copy-start.6
  25.6 0.7 copy-done.6
  26.3 3.1 %shard_map.84 = bf16[128,3,4,640]{3,2,1,0:T(4,128)(2,1)} custom-call(bf16[1536,512]{1,0:T(8,128)(2,1)S(1)} %get-tuple-element.354.selector_at, bf16[128,2,640]{2,1,0:T(2,128)(2,1)S(1)} %all-to-all-done.1.mine_at), custom_call_target="tpu_custom_call" | custom-call | flops 1000000000 | bytes 10000000 | tf_op jit(solution)/shard_map/pallas_call | solution.py:224
  29.4 0.0 copy-start
  29.4 5.7 %all-to-all-start.2 = ((bf16[128,3,4,640]{3,2,1,0:T(4,128)(2,1)}), bf16[128,3,4,640]{3,2,1,0:T(4,128)(2,1)}, u32[]{:S(2)}, u32[]{:S(2)}) async-start(bf16[128,3,4,640]{3,2,1,0:T(4,128)(2,1)} %shard_map.84), calls=%async_computation.2 | async-start | bytes 3932160 | tf_op jit(solution)/shard_map/all_to_all | solution.py:26
  35.2 1.4 %collective-permute-start.1 = (bf16[128,1280]{1,0:T(8,128)(2,1)}, bf16[128,1280]{1,0:T(8,128)(2,1)}, u32[]{:S(2)}, u32[]{:S(2)}) collective-permute-start(bf16[128,1280]{1,0:T(8,128)(2,1)} %bitcast.62), channel_id=1, source_target_pairs={{0,1},{1,0},{2,3},{3,2},{4,5},{5,4},{6,7},{7,6},{8,9},{9,8},{10,11... | collective-permute-start | bytes 983048 | tf_op jit(solution)/shard_map/ppermute | solution.py:31
  36.5 0.6 slice.53
  37.1 0.7 and_reduce_fusion.1
  37.8 0.3 collective-permute-done.1.other
  38.1 0.0 copy-done
  38.1 0.0 copy-start.2
  38.1 1.0 %copy-done.2 = bf16[1,128,1280]{2,1,0:T(8,128)(2,1)S(1)} copy-done((bf16[1,128,1280]{2,1,0:T(8,128)(2,1)S(1)}, bf16[1,128,1280]{2,1,0:T(8,128)(2,1)}, u32[]{:S(2)}) %copy-start.2) | copy-done | bytes 327704
  39.1 3.2 %shard_map.85.query_at = bf16[2560,256]{1,0:T(8,128)(2,1)} custom-call(bf16[128,1280]{1,0:T(8,128)(2,1)S(1)} %bitcast.64, bf16[128,1280]{1,0:T(8,128)(2,1)} %collective-permute-done.1.other, bf16[1280,1280]{1,0:T(8,128)(2,1)S(1)} %copy-done), custom_call_target="tpu_custom_call" | custom-call | flops 1000000000 | bytes 10000000 | tf_op jit(solution)/shard_map/pallas_call | solution.py:254
  42.3 21.9 %all-to-all-done.2.got_at = bf16[128,3,4,640]{3,2,1,0:T(4,128)(2,1)} async-done(((bf16[128,3,4,640]{3,2,1,0:T(4,128)(2,1)}), bf16[128,3,4,640]{3,2,1,0:T(4,128)(2,1)}, u32[]{:S(2)}, u32[]{:S(2)}) %all-to-all-start.2) | async-done | bytes 1966112 | tf_op jit(solution)/shard_map/all_to_all | solution.py:26
  64.1 0.0 copy-start.3
  64.1 1.0 %copy-done.3 = bf16[1,128,1280]{2,1,0:T(8,128)(2,1)S(1)} copy-done((bf16[1,128,1280]{2,1,0:T(8,128)(2,1)S(1)}, bf16[1,128,1280]{2,1,0:T(8,128)(2,1)}, u32[]{:S(2)}) %copy-start.3) | copy-done | bytes 327704
  65.1 0.0 copy-start.7
  65.1 10.3 %shard_map.86 = (f32[128,1280]{1,0:T(8,128)S(1)}, bf16[128,1280]{1,0:T(8,128)(2,1)S(1)}) custom-call(s32[24,128]{1,0:T(8,128)S(1)} %get-tuple-element.559.meta_at, bf16[128,3,4,640]{3,2,1,0:T(4,128)(2,1)} %all-to-all-done.2.got_at, bf16[2560,256]{1,0:T(8,128)(2,1)} %shard_map.85.query_at, bf16[1280,1280]{1,0:T(8,128)(2,1)} %k_at.1, bf16[1280,1280]{1,0:T(8,128)(2,1)} %v_at.1, ...), custom_call_target="tpu_custom_call" | custom-call | flops 10000000000 | bytes 10000000 | tf_op jit(solution)/shard_map/pallas_call | solution.py:440
  75.4 1.0 %collective-permute-start.2 = (bf16[128,1280]{1,0:T(8,128)(2,1)S(1)}, bf16[128,1280]{1,0:T(8,128)(2,1)}, u32[]{:S(2)}, u32[]{:S(2)}) collective-permute-start(bf16[128,1280]{1,0:T(8,128)(2,1)S(1)} %get-tuple-element.358), channel_id=1, source_target_pairs={{0,1},{1,0},{2,3},{3,2},{4,5},{5,4},{6,7},{7,6},{8,9},{9,8},{10,11... | collective-permute-start | bytes 983048 | tf_op jit(solution)/shard_map/ppermute | solution.py:31
  76.4 0.0 copy-done.7
  76.4 0.6 while.16
  77.0 0.8 %collective-permute-done.2 = bf16[128,1280]{1,0:T(8,128)(2,1)} collective-permute-done((bf16[128,1280]{1,0:T(8,128)(2,1)S(1)}, bf16[128,1280]{1,0:T(8,128)(2,1)}, u32[]{:S(2)}, u32[]{:S(2)}) %collective-permute-start.2) | collective-permute-done | bytes 327712 | tf_op jit(solution)/shard_map/ppermute | solution.py:31
  77.8 1.8 %fusion.30 = bf16[1,128,1280]{2,1,0:T(8,128)(2,1)} fusion(f32[128,1280]{1,0:T(8,128)S(1)} %get-tuple-element.632, bf16[128,1280]{1,0:T(8,128)(2,1)} %collective-permute-done.2), kind=kLoop, calls=%fused_computation.73 | loop fusion | flops 491520 | bytes 1310720 | tf_op jit(solution)/shard_map/broadcast_in_dim | solution.py:522
  (3 shorter events, 0.0 us)
Async XLA Ops:
  0.0 1.0 %copy-start.1 = (bf16[1,128,1280]{2,1,0:T(8,128)(2,1)S(1)}, bf16[1,128,1280]{2,1,0:T(8,128)(2,1)}, u32[]{:S(2)}) copy-start(bf16[1,128,1280]{2,1,0:T(8,128)(2,1)} %param.14) | copy-start | bytes 983044
  2.5 23.1 %all-to-all-start.1 = ((bf16[128,2,640]{2,1,0:T(2,128)(2,1)}), bf16[128,2,640]{2,1,0:T(2,128)(2,1)S(1)}, u32[]{:S(2)}, u32[]{:S(2)}) async-start(bf16[128,2,640]{2,1,0:T(2,128)(2,1)} %shard_map.83), calls=%async_computation.1 | async-start | bytes 655360 | tf_op jit(solution)/shard_map/all_to_all | solution.py:26
  14.8 0.7 copy-start.4
  15.5 0.7 copy-start.5
  25.6 0.7 copy-start.6
  29.4 8.7 %copy-start = (bf16[1280,1280]{1,0:T(8,128)(2,1)S(1)}, bf16[1280,1280]{1,0:T(8,128)(2,1)}, u32[]{:S(2)}) copy-start(bf16[1280,1280]{1,0:T(8,128)(2,1)} %weight.1) | copy-start | bytes 9830404
  29.4 34.7 %all-to-all-start.2 = ((bf16[128,3,4,640]{3,2,1,0:T(4,128)(2,1)}), bf16[128,3,4,640]{3,2,1,0:T(4,128)(2,1)}, u32[]{:S(2)}, u32[]{:S(2)}) async-start(bf16[128,3,4,640]{3,2,1,0:T(4,128)(2,1)} %shard_map.84), calls=%async_computation.2 | async-start | bytes 3932160 | tf_op jit(solution)/shard_map/all_to_all | solution.py:26
  35.2 2.9 %collective-permute-start.1 = (bf16[128,1280]{1,0:T(8,128)(2,1)}, bf16[128,1280]{1,0:T(8,128)(2,1)}, u32[]{:S(2)}, u32[]{:S(2)}) collective-permute-start(bf16[128,1280]{1,0:T(8,128)(2,1)} %bitcast.62), channel_id=1, source_target_pairs={{0,1},{1,0},{2,3},{3,2},{4,5},{5,4},{6,7},{7,6},{8,9},{9,8},{10,11... | collective-permute-start | bytes 983048 | tf_op jit(solution)/shard_map/ppermute | solution.py:31
  38.1 1.0 %copy-start.2 = (bf16[1,128,1280]{2,1,0:T(8,128)(2,1)S(1)}, bf16[1,128,1280]{2,1,0:T(8,128)(2,1)}, u32[]{:S(2)}) copy-start(bf16[1,128,1280]{2,1,0:T(8,128)(2,1)} %param.14) | copy-start | bytes 983044
  64.1 1.0 %copy-start.3 = (bf16[1,128,1280]{2,1,0:T(8,128)(2,1)S(1)}, bf16[1,128,1280]{2,1,0:T(8,128)(2,1)}, u32[]{:S(2)}) copy-start(bf16[1,128,1280]{2,1,0:T(8,128)(2,1)} %param.14) | copy-start | bytes 983044
  65.1 11.3 %copy-start.7 = (bf16[128,2,640]{2,1,0:T(2,128)(2,1)S(1)}, bf16[128,2,640]{2,1,0:T(2,128)(2,1)}, u32[]{:S(2)}) copy-start(bf16[128,2,640]{2,1,0:T(2,128)(2,1)} %copy-done.6) | copy-start | bytes 983044
  75.4 2.4 %collective-permute-start.2 = (bf16[128,1280]{1,0:T(8,128)(2,1)S(1)}, bf16[128,1280]{1,0:T(8,128)(2,1)}, u32[]{:S(2)}, u32[]{:S(2)}) collective-permute-start(bf16[128,1280]{1,0:T(8,128)(2,1)S(1)} %get-tuple-element.358), channel_id=1, source_target_pairs={{0,1},{1,0},{2,3},{3,2},{4,5},{5,4},{6,7},{7,6},{8,9},{9,8},{10,11... | collective-permute-start | bytes 983048 | tf_op jit(solution)/shard_map/ppermute | solution.py:31

commit v9 on v8

--- a/solution.py
+++ b/solution.py
@@ -17,7 +17,7 @@
 F32 = jnp.float32
 VMEM = pl.BlockSpec(memory_space=pltpu.VMEM)
 SMEM = pl.BlockSpec(memory_space=pltpu.SMEM)
-ANY = pl.BlockSpec(memory_space=pl.ANY)
+HBM = pl.BlockSpec(memory_space=pltpu.HBM)
 ACROSS = (((1,), (1,)), ((), ()))
 DOWN = (((0,), (0,)), ((), ()))
 
@@ -79,14 +79,14 @@
     return pl.pallas_call(
         front_kernel,
         out_shape=jax.ShapeDtypeStruct((rows, 2, width // 2), BF),
-        in_specs=[ANY],
-        out_specs=ANY,
+        in_specs=[HBM],
+        out_specs=HBM,
         scratch_shapes=[
             pltpu.VMEM((rows, width), BF),
             pltpu.VMEM((rows, 2, width // 2), BF),
             pltpu.SemaphoreType.DMA((8,)),
         ],
-        compiler_params=pltpu.CompilerParams(vmem_limit_bytes=4 * MIB),
+        compiler_params=pltpu.CompilerParams(vmem_limit_bytes=60 * MIB),
     )(own)
 
 
@@ -224,8 +224,8 @@
     return pl.pallas_call(
         pick_kernel,
         out_shape=jax.ShapeDtypeStruct(shape, BF),
-        in_specs=[ANY] * 2,
-        out_specs=ANY,
+        in_specs=[HBM] * 2,
+        out_specs=HBM,
         scratch_shapes=[
             pltpu.VMEM(selector.shape, BF),
             pltpu.VMEM(mine.shape, BF),
@@ -262,8 +262,8 @@
 
 
 def attend_kernel(
-    meta_at, got_at, query_at, k_at, v_at, o_at, own_at, out_at, sibling_at,
-    meta, own, got, query, weight_k, weight_v, weight_o, rows, keys, values,
+    meta_at, got_at, query_at, k_at, v_at, o_at, out_at, sibling_at,
+    meta, got, query, weight_k, weight_v, weight_o, rows, keys, values,
     context, scores, weights, scales, out, sibling, sems,
 ):
     def copy(index, source, target):
@@ -276,8 +276,7 @@
     copies = [
         copy(4 + i, a, b)
         for i, (a, b) in enumerate(
-            [(meta_at, meta), (k_at, weight_k), (v_at, weight_v), (query_at, query), (o_at, weight_o),
-             (own_at, own)]
+            [(meta_at, meta), (k_at, weight_k), (v_at, weight_v), (query_at, query), (o_at, weight_o)]
         )
     ]
     for one in quarters + copies[:3]:
@@ -319,7 +318,6 @@
                     ]
     copies[3].start()
     copies[4].start()
-    copies[5].start()
     copies[0].wait()
     full = (meta[0, 7] + 3) // 8
     partial = (meta[0, 7] > full * 8).astype(jnp.int32)
@@ -413,25 +411,23 @@
 
     lax.fori_loop(0, (meta[0, 3] + 1) // 2, two_sides, 0)
     copies[4].wait()
-    copies[5].wait()
     part = context[width:, :].astype(BF)
     update = lax.dot_general(part, weight_o[...], DOWN, preferred_element_type=F32)
     sibling[...] = jnp.where(iota(update.shape, 0) < meta[0, 5], update, 0.0).astype(BF)
-    leave = [copy(10, sibling, sibling_at)]
+    leave = [copy(9, sibling, sibling_at)]
     leave[0].start()
     part = context[:width, :].astype(BF)
     for half in range(2):
         at = pl.ds(half * (width // 2), width // 2)
         update = lax.dot_general(part, weight_o[:, at], DOWN, preferred_element_type=F32)
-        update = jnp.where(iota(update.shape, 0) < meta[0, 4], update, 0.0)
-        out[:, at] = own[:, at].astype(F32) + update
-        leave.append(copy(11 + half, out.at[:, at], out_at.at[:, at]))
+        out[:, at] = jnp.where(iota(update.shape, 0) < meta[0, 4], update, 0.0)
+        leave.append(copy(10 + half, out.at[:, at], out_at.at[:, at]))
         leave[-1].start()
     for one in leave:
         one.wait()
 
 
-def attend(meta, got, query, weight_k, weight_v, weight_o, own):
+def attend(meta, got, query, weight_k, weight_v, weight_o):
     width = weight_k.shape[0]
     each = 1
     for n in got.shape[1:-1]:
@@ -443,11 +439,10 @@
             jax.ShapeDtypeStruct((128, width), F32),
             jax.ShapeDtypeStruct((128, width), BF),
         ),
-        in_specs=[ANY] * 7,
-        out_specs=(ANY, ANY),
+        in_specs=[HBM] * 6,
+        out_specs=(HBM, HBM),
         scratch_shapes=[
             pltpu.SMEM(meta.shape, jnp.int32),
-            pltpu.VMEM(own.shape, BF),
             pltpu.VMEM(got.shape, BF),
             pltpu.VMEM(query.shape, BF),
             pltpu.VMEM((width, width), BF),
@@ -462,11 +457,11 @@
             pltpu.VMEM((2, 8, 2 * width), F32),
             pltpu.VMEM((128, width), F32),
             pltpu.VMEM((128, width), BF),
-            pltpu.SemaphoreType.DMA((13,)),
+            pltpu.SemaphoreType.DMA((12,)),
         ],
         compiler_params=pltpu.CompilerParams(vmem_limit_bytes=36 * MIB),
         cost_estimate=pl.CostEstimate(flops=10**10, bytes_accessed=10**7, transcendentals=10**6),
-    )(meta, got, query, weight_k, weight_v, weight_o, own)
+    )(meta, got, query, weight_k, weight_v, weight_o)
 
 
 def later_round(number, sides, me, count, meta):
@@ -506,20 +501,19 @@
     rounds = meta[0, 6]
     query = queries(own, swap(own), weight_q)
 
-    def one_round(selector, meta, outer, base):
+    def one_round(selector, meta, outer):
         got = exchange(pick(selector, mine, outer))
-        return attend(meta, got, query, weight_k, weight_v, weight_o, base)
+        return attend(meta, got, query, weight_k, weight_v, weight_o)
 
     def another(carry):
         number, total = carry
-        nothing = jnp.zeros_like(own)
-        kept, given = one_round(*later_round(number, sides, me, count, meta), (LATER // 2,), nothing)
+        kept, given = one_round(*later_round(number, sides, me, count, meta), (LATER // 2,))
         return number + 1, total + kept + swap(given).astype(F32)
 
-    kept, given = one_round(selector, meta, (FIRST // 8, 4), own)
+    kept, given = one_round(selector, meta, (FIRST // 8, 4))
     received = swap(given)
     _, kept = lax.while_loop(lambda c: c[0] <= rounds, another, (jnp.int32(1), kept))
-    return (kept + received.astype(F32)).astype(BF)[None]
+    return (own.astype(F32) + (kept + received.astype(F32))).astype(BF)[None]
 
 
 def solution(mesh):

time: 80.6 us -> 81.9 us (1.016)
  local copies, waits for them, and re-layouts: 6.35 us -> 4.41 us
  Pallas kernels: 22.3 us -> 24.2 us
  starting transfers between devices: 19.5 us -> 20.6 us
    unnamed x17 -> x15, local copies, waits for them, and re-layouts: 5.77 us -> 3.83 us
    pallas_call x1, Pallas kernels: 10.3 us -> 11.7 us  [attend(): pl.pallas_call(attend_kernel, out_shape=(jax.ShapeDtypeStruct((128, width...]
    ppermute x2, starting transfers between devices: 2.32 us -> 3.4 us  [swap(): return lax.ppermute(array, 'dev', [(i, i ^ 1) for i in range(count)])]
where the time goes in v9:
time: 81.9 us; the launch traced here: 80.8 us
  waiting for transfers between devices  28.2 us (34%)
  Pallas kernels  24.2 us (30%)
  starting transfers between devices  20.6 us (25%)
  local copies, waits for them, and re-layouts  4.41 us (5%)
  other arithmetic  2.7 us (3%)
    all_to_all x2, waiting for transfers between devices, exchange(): return lax.all_to_all(array, AXES, split_axis=0, concat_axis=0, tiled=True)  27.1 us
    all_to_all x2, starting transfers between devices, exchange(): return lax.all_to_all(array, AXES, split_axis=0, concat_axis=0, tiled=True)  17.2 us
    pallas_call x1, Pallas kernels, attend(): pl.pallas_call(attend_kernel, out_shape=(jax.ShapeDtypeStruct((128, width...  11.7 us
    pallas_call x1, Pallas kernels, plan(): pl.pallas_call(plan_kernel, out_shape=(jax.ShapeDtypeStruct((devices * FI...  4.14 us
    unnamed x15, local copies, waits for them, and re-layouts  3.83 us
    ppermute x2, starting transfers between devices, swap(): return lax.ppermute(array, 'dev', [(i, i ^ 1) for i in range(count)])  3.4 us
    pallas_call x1, Pallas kernels, queries(): pl.pallas_call(query_kernel, out_shape=jax.ShapeDtypeStruct((2 * own.shap...  3.18 us
    pallas_call x1, Pallas kernels, pick(): pl.pallas_call(pick_kernel, out_shape=jax.ShapeDtypeStruct(shape, BF), in...  3.13 us
  transfers between devices with their start and end apart: 4, of which 4 were waited for; matrix products, arithmetic and copies ran while one was open for 3% of the time, Pallas kernels for 9%

profile of v9, /device:TPU:1, one launch (start us, length us, event | category | flops | bytes accessed | tf_op | source)
XLA Modules:
  0.0 80.8 jit_solution(8079278530930675927)
XLA Ops:
  0.0 2.0 %shard_map.83 = bf16[128,2,640]{2,1,0:T(2,128)(2,1)} custom-call(bf16[128,1280]{1,0:T(8,128)(2,1)} %bitcast.63), custom_call_target="tpu_custom_call" | custom-call | tf_op jit(solution)/shard_map/pallas_call | solution.py:79
  2.0 11.5 %all-to-all-start.1 = ((bf16[128,2,640]{2,1,0:T(2,128)(2,1)}), bf16[128,2,640]{2,1,0:T(2,128)(2,1)S(1)}, u32[]{:S(2)}, u32[]{:S(2)}) async-start(bf16[128,2,640]{2,1,0:T(2,128)(2,1)} %shard_map.83), calls=%async_computation.1 | async-start | bytes 655360 | tf_op jit(solution)/shard_map/all_to_all | solution.py:26
  13.6 0.8 %copy.23.pairs = s32[256,2]{1,0:T(8,128)S(1)} copy(s32[256,2]{0,1:T(2,128)} %param.19) | data formatting | bytes 4096 | tf_op args[5]
  14.4 0.0 copy-start.3
  14.4 0.6 copy-done.3
  15.0 0.0 copy-start.4
  15.0 0.7 copy-done.4
  15.7 4.1 %shard_map.82 = (bf16[1536,512]{1,0:T(8,128)(2,1)S(1)}, s32[24,128]{1,0:T(8,128)S(1)}, s32[8,512]{1,0:T(8,128)S(1)}) custom-call(s32[1]{0:T(128)} %bitcast.11.place, s32[256,2]{1,0:T(8,128)S(1)} %copy.23.pairs, s32[1,128]{1,0:T(1,128)S(1)} %bitcast.66, s32[1,128]{1,0:T(1,128)S(1)} %bitcast.67), custom_call_target="tpu_custom_call" | custom-call | flops 1000000000 | bytes 1000000 | tf_op jit(solution)/shard_map/pallas_call | solution.py:170
  19.8 5.3 %all-to-all-done.1.mine_at = bf16[128,2,640]{2,1,0:T(2,128)(2,1)S(1)} async-done(((bf16[128,2,640]{2,1,0:T(2,128)(2,1)}), bf16[128,2,640]{2,1,0:T(2,128)(2,1)S(1)}, u32[]{:S(2)}, u32[]{:S(2)}) %all-to-all-start.1) | async-done | bytes 327712 | tf_op jit(solution)/shard_map/all_to_all | solution.py:26
  25.1 0.0 copy-start.5
  25.1 0.7 copy-done.5
  25.8 3.1 %shard_map.84 = bf16[128,3,4,640]{3,2,1,0:T(4,128)(2,1)} custom-call(bf16[1536,512]{1,0:T(8,128)(2,1)S(1)} %get-tuple-element.354.selector_at, bf16[128,2,640]{2,1,0:T(2,128)(2,1)S(1)} %all-to-all-done.1.mine_at), custom_call_target="tpu_custom_call" | custom-call | flops 1000000000 | bytes 10000000 | tf_op jit(solution)/shard_map/pallas_call | solution.py:224
  29.0 0.0 copy-start
  29.0 5.7 %all-to-all-start.2 = ((bf16[128,3,4,640]{3,2,1,0:T(4,128)(2,1)}), bf16[128,3,4,640]{3,2,1,0:T(4,128)(2,1)}, u32[]{:S(2)}, u32[]{:S(2)}) async-start(bf16[128,3,4,640]{3,2,1,0:T(4,128)(2,1)} %shard_map.84), calls=%async_computation.2 | async-start | bytes 3932160 | tf_op jit(solution)/shard_map/all_to_all | solution.py:26
  34.7 1.4 %collective-permute-start.1 = (bf16[128,1280]{1,0:T(8,128)(2,1)}, bf16[128,1280]{1,0:T(8,128)(2,1)}, u32[]{:S(2)}, u32[]{:S(2)}) collective-permute-start(bf16[128,1280]{1,0:T(8,128)(2,1)} %bitcast.64), channel_id=1, source_target_pairs={{0,1},{1,0},{2,3},{3,2},{4,5},{5,4},{6,7},{7,6},{8,9},{9,8},{10,11... | collective-permute-start | bytes 983048 | tf_op jit(solution)/shard_map/ppermute | solution.py:31
  36.1 0.6 slice.53
  36.7 0.7 and_reduce_fusion.1
  37.4 0.3 collective-permute-done.1.other
  37.7 0.0 copy-done
  37.7 0.0 copy-start.1
  37.7 1.0 %copy-done.1 = bf16[1,128,1280]{2,1,0:T(8,128)(2,1)S(1)} copy-done((bf16[1,128,1280]{2,1,0:T(8,128)(2,1)S(1)}, bf16[1,128,1280]{2,1,0:T(8,128)(2,1)}, u32[]{:S(2)}) %copy-start.1) | copy-done | bytes 327704
  38.6 3.2 %shard_map.85.query_at = bf16[2560,256]{1,0:T(8,128)(2,1)} custom-call(bf16[128,1280]{1,0:T(8,128)(2,1)S(1)} %bitcast.65, bf16[128,1280]{1,0:T(8,128)(2,1)} %collective-permute-done.1.other, bf16[1280,1280]{1,0:T(8,128)(2,1)S(1)} %copy-done), custom_call_target="tpu_custom_call" | custom-call | flops 1000000000 | bytes 10000000 | tf_op jit(solution)/shard_map/pallas_call | solution.py:254
  41.8 0.0 copy-start.6
  41.8 21.9 %all-to-all-done.2.got_at = bf16[128,3,4,640]{3,2,1,0:T(4,128)(2,1)} async-done(((bf16[128,3,4,640]{3,2,1,0:T(4,128)(2,1)}), bf16[128,3,4,640]{3,2,1,0:T(4,128)(2,1)}, u32[]{:S(2)}, u32[]{:S(2)}) %all-to-all-start.2) | async-done | bytes 1966112 | tf_op jit(solution)/shard_map/all_to_all | solution.py:26
  63.7 11.7 %shard_map.86 = (f32[128,1280]{1,0:T(8,128)}, bf16[128,1280]{1,0:T(8,128)(2,1)S(1)}) custom-call(s32[24,128]{1,0:T(8,128)S(1)} %get-tuple-element.559.meta_at, bf16[128,3,4,640]{3,2,1,0:T(4,128)(2,1)} %all-to-all-done.2.got_at, bf16[2560,256]{1,0:T(8,128)(2,1)} %shard_map.85.query_at, bf16[1280,1280]{1,0:T(8,128)(2,1)} %k_at.1, bf16[1280,1280]{1,0:T(8,128)(2,1)} %v_at.1, ...), custom_call_target="tpu_custom_call" | custom-call | flops 10000000000 | bytes 10000000 | tf_op jit(solution)/shard_map/pallas_call | solution.py:436
  75.4 2.0 %collective-permute-start.2 = (bf16[128,1280]{1,0:T(8,128)(2,1)S(1)}, bf16[128,1280]{1,0:T(8,128)(2,1)}, u32[]{:S(2)}, u32[]{:S(2)}) collective-permute-start(bf16[128,1280]{1,0:T(8,128)(2,1)S(1)} %get-tuple-element.358), channel_id=1, source_target_pairs={{0,1},{1,0},{2,3},{3,2},{4,5},{5,4},{6,7},{7,6},{8,9},{9,8},{10,11... | collective-permute-start | bytes 983048 | tf_op jit(solution)/shard_map/ppermute | solution.py:31
  77.4 0.0 copy-done.6
  77.4 0.0 copy-start.2
  77.4 0.6 while.16
  78.1 0.8 collective-permute-done.2
  78.8 0.0 copy-done.2
  78.8 2.0 %fusion.30 = bf16[1,128,1280]{2,1,0:T(8,128)(2,1)} fusion(f32[128,1280]{1,0:T(8,128)} %get-tuple-element.357, bf16[128,1280]{1,0:T(8,128)(2,1)} %collective-permute-done.2, bf16[1,128,1280]{2,1,0:T(8,128)(2,1)S(1)} %copy-done.2), kind=kLoop, calls=%fused_computation.73 | loop fusion | flops 819200 | bytes 1638400 | tf_op jit(solution)/shard_map/broadcast_in_dim | solution.py:516
  (3 shorter events, 0.0 us)
Async XLA Ops:
  2.0 23.1 %all-to-all-start.1 = ((bf16[128,2,640]{2,1,0:T(2,128)(2,1)}), bf16[128,2,640]{2,1,0:T(2,128)(2,1)S(1)}, u32[]{:S(2)}, u32[]{:S(2)}) async-start(bf16[128,2,640]{2,1,0:T(2,128)(2,1)} %shard_map.83), calls=%async_computation.1 | async-start | bytes 655360 | tf_op jit(solution)/shard_map/all_to_all | solution.py:26
  14.4 0.7 copy-start.3
  15.0 0.7 copy-start.4
  25.1 0.7 copy-start.5
  29.0 8.7 %copy-start = (bf16[1280,1280]{1,0:T(8,128)(2,1)S(1)}, bf16[1280,1280]{1,0:T(8,128)(2,1)}, u32[]{:S(2)}) copy-start(bf16[1280,1280]{1,0:T(8,128)(2,1)} %weight.1) | copy-start | bytes 9830404
  29.0 34.7 %all-to-all-start.2 = ((bf16[128,3,4,640]{3,2,1,0:T(4,128)(2,1)}), bf16[128,3,4,640]{3,2,1,0:T(4,128)(2,1)}, u32[]{:S(2)}, u32[]{:S(2)}) async-start(bf16[128,3,4,640]{3,2,1,0:T(4,128)(2,1)} %shard_map.84), calls=%async_computation.2 | async-start | bytes 3932160 | tf_op jit(solution)/shard_map/all_to_all | solution.py:26
  34.7 2.9 %collective-permute-start.1 = (bf16[128,1280]{1,0:T(8,128)(2,1)}, bf16[128,1280]{1,0:T(8,128)(2,1)}, u32[]{:S(2)}, u32[]{:S(2)}) collective-permute-start(bf16[128,1280]{1,0:T(8,128)(2,1)} %bitcast.64), channel_id=1, source_target_pairs={{0,1},{1,0},{2,3},{3,2},{4,5},{5,4},{6,7},{7,6},{8,9},{9,8},{10,11... | collective-permute-start | bytes 983048 | tf_op jit(solution)/shard_map/ppermute | solution.py:31
  37.7 1.0 %copy-start.1 = (bf16[1,128,1280]{2,1,0:T(8,128)(2,1)S(1)}, bf16[1,128,1280]{2,1,0:T(8,128)(2,1)}, u32[]{:S(2)}) copy-start(bf16[1,128,1280]{2,1,0:T(8,128)(2,1)} %param.14) | copy-start | bytes 983044
  41.8 35.6 %copy-start.6 = (bf16[128,2,640]{2,1,0:T(2,128)(2,1)S(1)}, bf16[128,2,640]{2,1,0:T(2,128)(2,1)}, u32[]{:S(2)}) copy-start(bf16[128,2,640]{2,1,0:T(2,128)(2,1)} %copy-done.5) | copy-start | bytes 983044
  75.4 3.4 %collective-permute-start.2 = (bf16[128,1280]{1,0:T(8,128)(2,1)S(1)}, bf16[128,1280]{1,0:T(8,128)(2,1)}, u32[]{:S(2)}, u32[]{:S(2)}) collective-permute-start(bf16[128,1280]{1,0:T(8,128)(2,1)S(1)} %get-tuple-element.358), channel_id=1, source_target_pairs={{0,1},{1,0},{2,3},{3,2},{4,5},{5,4},{6,7},{7,6},{8,9},{9,8},{10,11... | collective-permute-start | bytes 983048 | tf_op jit(solution)/shard_map/ppermute | solution.py:31
  77.4 1.4 %copy-start.2 = (bf16[1,128,1280]{2,1,0:T(8,128)(2,1)S(1)}, bf16[1,128,1280]{2,1,0:T(8,128)(2,1)}, u32[]{:S(2)}) copy-start(bf16[1,128,1280]{2,1,0:T(8,128)(2,1)} %param.14) | copy-start | bytes 983044
